TPU v7x, 256 devices: a whole 4x4x8 slice. The times are simulated.
256 devices in a mesh: sec: 4 (over x), gx: 8 (over z_lo, y), gy: 8 (over z_hi, core).
Axes of the slice: x: 4, y: 4, z: 8 (z_hi: 4, z_lo: 2; z = z_hi * 2 + z_lo), core: 2. Of those that a mesh axis runs over, the one named last changes fastest.
Arguments:
- air_surface: float32 [5, 256, 32, 4, 128], P(None, 'gx', 'gy', 'sec'), may hold values from -4 to 4
- remap_weights: bfloat16 [256, 32, 4, 2, 128, 128], P('gx', 'gy', 'sec'), may hold values from -0.25 to 0.25
- sources: int32 [256, 32, 4, 2], P('gx', 'gy', 'sec'), may hold values from 0 to 8
- live_count: int32 [256, 32, 4], P('gx', 'gy', 'sec'), may hold values from 1 to 2, as said below
- land_sea: int32 [256, 32], P('gx', 'gy'), may hold values from 0 to 1, as said below
- tracers: float32 [2, 40, 256, 4096], P(None, 'sec', 'gx', 'gy'), may hold values from -5 to 5
- currents: float32 [2, 40, 256, 4096], P(None, 'sec', 'gx', 'gy'), may hold values from -2 to 2
Outputs:
- tracers_out: float32 [2, 40, 256, 4096], P(None, 'sec', 'gx', 'gy')
- ocean_flux: float32 [4, 256, 4096], P(None, 'gx', 'gy')
Inputs may be any that keep to these rules, and one draw needn't show every extreme that they name: `sources`: code c names the tile at offset (c // 3 - 1, c % 3 - 1) in ocean tiles from the destination, of the same quadrant as the slot. `live_count`: some tile and quadrant uses all 2 slots. `land_sea`: for every even column x >= 2 some tile row has ocean at x and land at x - 1.
All inputs are finite; a program needn't handle non-finite values.
Results may differ from a plain program's by a relative error of at most 0.003.
Values may be sent and summed in bfloat16 or wider, within the bound.
No kernel may reach another device: no remote copies, remote signals or barrier semaphores. Data moves between devices by JAX's collectives and lax.ppermute only.
A program may use at most 128 MiB of HBM per device.

v0:
```python
import jax
import jax.numpy as jnp
from jax import lax
from jax.sharding import PartitionSpec as P

TILE = 128
SLOTS = 2
STEPS = 3


drag_coef = 0.6
wind_gain = 0.5
heat_gain = 0.5
salt_gain = 0.5
diffusion = 0.15
advection = 0.5
vertical_mix = 0.2


def extended(block, sides, width):
    for axis, dim in sides:
        count = lax.axis_size(axis)
        forward = [(i, i + 1) for i in range(count - 1)]
        backward = [(target, source) for source, target in forward]
        low = lax.ppermute(
            lax.slice_in_dim(block, block.shape[dim] - width, None, axis=dim), axis, forward
        )
        high = lax.ppermute(lax.slice_in_dim(block, 0, width, axis=dim), axis, backward)
        block = jnp.concatenate([low, block, high], axis=dim)
    return block


def bulk_fluxes(air_surface):
    wind_u = air_surface[0]
    wind_v = air_surface[1]
    air_temp = air_surface[2]
    humidity = air_surface[3]
    skin_temp = air_surface[4]
    bulk_rate = (1.0 + 0.5 * jnp.tanh(skin_temp - air_temp)) * jnp.sqrt(
        wind_u * wind_u + wind_v * wind_v + 1.0
    )
    stacked = jnp.stack(
        [
            drag_coef * bulk_rate * wind_u,
            drag_coef * bulk_rate * wind_v,
            drag_coef * bulk_rate * (skin_temp - air_temp),
            drag_coef * bulk_rate * (jnp.exp(0.3 * skin_temp) - humidity),
        ]
    )
    return stacked.astype(jnp.bfloat16)


def openings(level_ids, total_levels):
    up_open = (level_ids > 0).astype(jnp.float32)[:, None, None]
    down_open = (level_ids < total_levels - 1).astype(jnp.float32)[:, None, None]
    return (up_open, down_open)


def stencil(padded, mask_pad, east_flow, north_flow, up_open, down_open):
    centre = padded[:, 1:-1, 1:-1, 1:-1]
    mask_mid = mask_pad[1:-1, 1:-1, 1:-1]
    east_cell = padded[:, 1:-1, 2:, 1:-1]
    west_cell = padded[:, 1:-1, :-2, 1:-1]
    north_cell = padded[:, 1:-1, 1:-1, 2:]
    south_cell = padded[:, 1:-1, 1:-1, :-2]
    above_cell = padded[:, :-2, 1:-1, 1:-1]
    below_cell = padded[:, 2:, 1:-1, 1:-1]
    mask_east = mask_pad[1:-1, 2:, 1:-1]
    mask_west = mask_pad[1:-1, :-2, 1:-1]
    mask_north = mask_pad[1:-1, 1:-1, 2:]
    mask_south = mask_pad[1:-1, 1:-1, :-2]
    spread = (
        mask_east * (east_cell - centre)
        + mask_west * (west_cell - centre)
        + mask_north * (north_cell - centre)
        + mask_south * (south_cell - centre)
    )
    carried = east_flow * (mask_east * east_cell - mask_west * west_cell) + north_flow * (
        mask_north * north_cell - mask_south * south_cell
    )
    mixed = up_open * (above_cell - centre) + down_open * (below_cell - centre)
    return centre + mask_mid * (diffusion * spread - advection * carried + vertical_mix * mixed)


def tile_cells(sea_tiles, margin_width, tile_count):
    spread_cells = jnp.repeat(sea_tiles.astype(jnp.float32), TILE, axis=1)
    return spread_cells[:, TILE - margin_width : TILE * (tile_count + 1) + margin_width]


def on_device(air_surface, remap_weights, sources, live_count, land_sea, tracers, currents):
    columns = air_surface.shape[1]
    tile_count = air_surface.shape[2]
    fluxes = bulk_fluxes(air_surface[:, :, :, 0, :])
    rimmed = extended(fluxes, (("gx", 1), ("gy", 2)), 1)
    flat_rim = rimmed.reshape(4, (columns + 2) * (tile_count + 2), TILE)
    source_code = sources[:, :, 0, :]
    row_ids = jnp.arange(columns, dtype=jnp.int32)[:, None, None] + source_code // 3
    col_ids = jnp.arange(tile_count, dtype=jnp.int32)[None, :, None] + source_code % 3
    flat_ids = (row_ids * (tile_count + 2) + col_ids).reshape(-1)
    blocks = jnp.take(flat_rim, flat_ids, axis=1).reshape(4, columns, tile_count, SLOTS, TILE)
    live_mask = jnp.arange(SLOTS, dtype=jnp.int32)[None, None, :] < live_count[:, :, 0][:, :, None]
    blocks = jnp.where(live_mask[None, :, :, :, None], blocks, jnp.zeros((), jnp.bfloat16))
    partial_value = jnp.einsum(
        "fxtsc,xtsdc->fxtd", blocks, remap_weights[:, :, 0], preferred_element_type=jnp.float32
    )
    partial_value = partial_value.reshape(4, columns, tile_count * TILE)
    summed = lax.psum(partial_value, "sec")
    cell_mask = jnp.repeat(land_sea.astype(jnp.float32), TILE, axis=1)
    ocean_flux = summed * cell_mask
    levels = tracers.shape[1]
    total_levels = levels * lax.axis_size("sec")
    level_ids = lax.axis_index("sec") * levels + jnp.arange(levels, dtype=jnp.int32)
    level_zero = (level_ids == 0).astype(jnp.float32)[:, None, None]
    forced_u = currents[0] + wind_gain * level_zero * ocean_flux[0]
    forced_v = currents[1] + wind_gain * level_zero * ocean_flux[1]
    heated = tracers[0] + heat_gain * level_zero * ocean_flux[2]
    freshened = tracers[1] - salt_gain * level_zero * ocean_flux[3]
    fields = jnp.stack([heated, freshened])
    sea_near = extended(land_sea, (("gx", 0), ("gy", 1)), 1)
    near_cells = tile_cells(sea_near, 1, tile_count)
    mask_pad = jnp.broadcast_to(near_cells, (levels + 2,) + near_cells.shape)
    up_open, down_open = openings(level_ids, total_levels)
    for step_index in range(STEPS):
        padded = extended(fields, (("sec", 1), ("gx", 2), ("gy", 3)), 1)
        fields = stencil(padded, mask_pad, forced_u, forced_v, up_open, down_open)
    return (fields, ocean_flux)


def solution(mesh):
    return jax.shard_map(
        on_device,
        mesh=mesh,
        in_specs=(
            P(None, "gx", "gy", "sec", None),
            P("gx", "gy", "sec", None, None, None),
            P("gx", "gy", "sec", None),
            P("gx", "gy", "sec"),
            P("gx", "gy"),
            P(None, "sec", "gx", "gy"),
            P(None, "sec", "gx", "gy"),
        ),
        out_specs=(P(None, "sec", "gx", "gy"), P(None, "gx", "gy")),
        check_vma=False,
    )
```

profile of v0, /device:TPU:160, one launch (start us, length us, event | category | flops | bytes accessed | tf_op | source)
XLA Modules:
  0.0 244.2 jit_solution(1166555297117273181)
XLA Ops:
  8.0 3.5 %collective-permute-start.4 = (s32[1,4]{0,1:T(4,128)S(1)}, s32[1,4]{0,1:T(4,128)S(1)}, u32[]{:S(2)}, u32[]{:S(2)}) collective-permute-start(s32[1,4]{0,1:T(4,128)S(1)} %get-tuple-element.48), channel_id=1, source_target_pairs={{0,8},{8,16},{16,24},{24,32},{32,40},{40,48},{48,56},{1,9},{9,17},... | collective-permute-start | bytes 56 | tf_op jit(solution)/shard_map/ppermute | solution.py:25
  11.5 4.5 %collective-permute-start.5 = (s32[1,4]{0,1:T(4,128)S(1)}, s32[1,4]{0,1:T(4,128)S(1)}, u32[]{:S(2)}, u32[]{:S(2)}) collective-permute-start(s32[1,4]{0,1:T(4,128)S(1)} %get-tuple-element.49), channel_id=1, source_target_pairs={{8,0},{16,8},{24,16},{32,24},{40,32},{48,40},{56,48},{9,1},{17,9},... | collective-permute-start | bytes 56 | tf_op jit(solution)/shard_map/ppermute | solution.py:28
  16.8 1.0 multiply_convert_fusion.2
  17.8 1.0 multiply_convert_fusion.1
  18.9 1.9 collective-permute-start
  20.8 6.0 %collective-permute-start.1 = (bf16[4,1,4,128]{3,2,1,0:T(4,128)(2,1)S(1)}, bf16[4,1,4,128]{3,2,1,0:T(4,128)(2,1)S(1)}, u32[]{:S(2)}, u32[]{:S(2)}) collective-permute-start(bf16[4,1,4,128]{3,2,1,0:T(4,128)(2,1)S(1)} %get-tuple-element.38), channel_id=1, source_target_pairs={{8,0},{16,8},{24,16},{32,24},{40,32},{48,40},{56,48},{9,1},{17,9},... | collective-permute-start | bytes 12296 | tf_op jit(solution)/shard_map/ppermute | solution.py:28
  30.6 1.9 collective-permute-start.2
  32.5 5.8 %collective-permute-start.3 = (bf16[4,34,1,128]{3,2,1,0:T(2,128)(2,1)S(1)}, bf16[4,34,1,128]{3,2,1,0:T(2,128)(2,1)S(1)}, u32[]{:S(2)}, u32[]{:S(2)}) collective-permute-start(bf16[4,34,1,128]{3,2,1,0:T(2,128)(2,1)S(1)} %get-tuple-element.36), channel_id=1, source_target_pairs={{1,0},{2,1},{3,2},{4,3},{5,4},{6,5},{7,6},{9,8},{10,9},{11,10},{12... | collective-permute-start | bytes 104456 | tf_op jit(solution)/shard_map/ppermute | solution.py:28
  38.4 1.8 collective-permute-done.3
  41.5 6.9 %fusion.34 = f32[4,32,4,128]{3,0,2,1:T(4,128)S(1)} fusion(bf16[32,4,1,2,128,128]{5,4,3,2,1,0:T(8,128)(2,1)} %param.8, bf16[4,32,4,2,128]{4,0,3,2,1:T(4,128)(2,1)S(1)} %bitcast.95, pred[32,4,2]{2,1,0:T(4,128)(4,1)S(1)} %copy.39, pred[32,4,2]{2,1,0:T(4,128)(4,1)S(1)} %iota_compare_fusion), kind=kOutput, calls=%fused_computation.100 | convolution fusion | flops 33816576 | bytes 8913408 | tf_op jit(solution)/shard_map/fxtsc,xtsdc->fxtd/dot_general | solution.py:103
  49.7 46.7 %all-reduce.2.cloned.1.call-done = f32[4,32,512]{2,1,0:T(8,128)} async-done(((f32[4,32,512]{2,1,0:T(8,128)}), f32[4,32,512]{2,1,0:T(8,128)}) %all-reduce.2.cloned.1.call-update) | async-done | bytes 262160 | tf_op jit(solution)/shard_map/psum | solution.py:107
  97.3 2.2 add_bitcast_fusion.1
  99.6 2.3 collective-permute-start.8
  101.9 1.3 collective-permute-start.9
  103.2 1.9 collective-permute-start.6
  105.1 5.8 %collective-permute-start.7 = (s32[34,1]{0,1:T(1,128)S(1)}, s32[34,1]{0,1:T(1,128)S(1)}, u32[]{:S(2)}, u32[]{:S(2)}) collective-permute-start(s32[34,1]{0,1:T(1,128)S(1)} %get-tuple-element.47), channel_id=1, source_target_pairs={{1,0},{2,1},{3,2},{4,3},{5,4},{6,5},{7,6},{9,8},{10,9},{11,10},{12... | collective-permute-start | bytes 416 | tf_op jit(solution)/shard_map/ppermute | solution.py:28
  111.0 3.4 %collective-permute-start.11 = (f32[2,12,1,512]{3,2,1,0:T(1,128)S(1)}, f32[2,12,1,512]{3,2,1,0:T(1,128)S(1)}, u32[]{:S(2)}, u32[]{:S(2)}) collective-permute-start(f32[2,12,1,512]{3,2,1,0:T(1,128)S(1)} %get-tuple-element.16), channel_id=1, source_target_pairs={{0,8},{8,16},{16,24},{24,32},{32,40},{40,48},{48,56},{1,9},{9,17},... | collective-permute-start | bytes 147464 | tf_op jit(solution)/shard_map/ppermute | solution.py:25
  114.4 4.6 %collective-permute-start.10 = (f32[2,12,1,512]{3,2,1,0:T(1,128)S(1)}, f32[2,12,1,512]{3,2,1,0:T(1,128)S(1)}, u32[]{:S(2)}, u32[]{:S(2)}) collective-permute-start(f32[2,12,1,512]{3,2,1,0:T(1,128)S(1)} %get-tuple-element.17), channel_id=1, source_target_pairs={{8,0},{16,8},{24,16},{32,24},{40,32},{48,40},{56,48},{9,1},{17,9},... | collective-permute-start | bytes 147464 | tf_op jit(solution)/shard_map/ppermute | solution.py:28
  119.3 1.4 collective-permute-done.10
  120.9 1.9 collective-permute-start.12
  122.9 2.4 collective-permute-start.13
  125.4 8.6 %collective-permute-done.12 = f32[2,12,34,1]{3,2,1,0:T(8,128)S(1)} collective-permute-done((f32[2,12,34,1]{3,2,1,0:T(8,128)S(1)}, f32[2,12,34,1]{3,2,1,0:T(8,128)S(1)}, u32[]{:S(2)}, u32[]{:S(2)}) %collective-permute-start.12) | collective-permute-done | bytes 3296 | tf_op jit(solution)/shard_map/ppermute | solution.py:28
  134.0 4.5 %collective-permute-done.13 = f32[2,12,34,1]{3,2,1,0:T(8,128)S(1)} collective-permute-done((f32[2,12,34,1]{3,2,1,0:T(8,128)S(1)}, f32[2,12,34,1]{3,2,1,0:T(8,128)S(1)}, u32[]{:S(2)}, u32[]{:S(2)}) %collective-permute-start.13) | collective-permute-done | bytes 3296 | tf_op jit(solution)/shard_map/ppermute | solution.py:25
  138.5 6.0 %fusion.26 = f32[2,10,32,512]{3,2,1,0:T(8,128)S(1)} fusion(f32[2,1,32,512]{3,2,1,0:T(8,128)S(1)} %collective-permute-done.9, f32[1,10,32,512]{3,2,1,0:T(8,128)S(1)} %get-tuple-element.51, f32[1,10,32,512]{3,2,1,0:T(8,128)S(1)} %get-tuple-element.50, f32[2,1,32,512]{3,2,1,0:T(8,128)S(1)} %collective-permute-done.8, ...), kind=kLoop, calls=%fused_computation.69 | loop fusion | flops 18677760 | bytes 4626896 | tf_op jit(solution)/shard_map/add | solution.py:82
  144.5 4.6 %collective-permute-start.14 = (f32[2,1,32,512]{3,2,1,0:T(8,128)S(1)}, f32[2,1,32,512]{3,2,1,0:T(8,128)S(1)}, u32[]{:S(2)}, u32[]{:S(2)}) collective-permute-start(f32[2,1,32,512]{3,2,1,0:T(8,128)S(1)} %get-tuple-element.24), channel_id=1, source_target_pairs={{0,64},{64,128},{128,192},{1,65},{65,129},{129,193},{2,66},{66,130... | collective-permute-start | bytes 393224 | tf_op jit(solution)/shard_map/ppermute | solution.py:25
  149.0 1.3 collective-permute-start.15
  150.3 1.2 collective-permute-done.14
  151.5 4.4 %collective-permute-done.15 = f32[2,1,32,512]{3,2,1,0:T(8,128)S(1)} collective-permute-done((f32[2,1,32,512]{3,2,1,0:T(8,128)S(1)}, f32[2,1,32,512]{3,2,1,0:T(8,128)S(1)}, u32[]{:S(2)}, u32[]{:S(2)}) %collective-permute-start.15) | collective-permute-done | bytes 131104 | tf_op jit(solution)/shard_map/ppermute | solution.py:28
  156.0 3.1 %collective-permute-start.17 = (f32[2,12,1,512]{3,2,1,0:T(1,128)S(1)}, f32[2,12,1,512]{3,2,1,0:T(1,128)S(1)}, u32[]{:S(2)}, u32[]{:S(2)}) collective-permute-start(f32[2,12,1,512]{3,2,1,0:T(1,128)S(1)} %get-tuple-element.14), channel_id=1, source_target_pairs={{0,8},{8,16},{16,24},{24,32},{32,40},{40,48},{48,56},{1,9},{9,17},... | collective-permute-start | bytes 147464 | tf_op jit(solution)/shard_map/ppermute | solution.py:25
  159.1 4.9 %collective-permute-start.16 = (f32[2,12,1,512]{3,2,1,0:T(1,128)S(1)}, f32[2,12,1,512]{3,2,1,0:T(1,128)S(1)}, u32[]{:S(2)}, u32[]{:S(2)}) collective-permute-start(f32[2,12,1,512]{3,2,1,0:T(1,128)S(1)} %get-tuple-element.15), channel_id=1, source_target_pairs={{8,0},{16,8},{24,16},{32,24},{40,32},{48,40},{56,48},{9,1},{17,9},... | collective-permute-start | bytes 147464 | tf_op jit(solution)/shard_map/ppermute | solution.py:28
  164.1 6.0 %collective-permute-done.16 = f32[2,12,1,512]{3,2,1,0:T(1,128)S(1)} collective-permute-done((f32[2,12,1,512]{3,2,1,0:T(1,128)S(1)}, f32[2,12,1,512]{3,2,1,0:T(1,128)S(1)}, u32[]{:S(2)}, u32[]{:S(2)}) %collective-permute-start.16) | collective-permute-done | bytes 49184 | tf_op jit(solution)/shard_map/ppermute | solution.py:28
  170.4 1.9 collective-permute-start.18
  172.3 2.4 collective-permute-start.19
  174.7 4.2 %collective-permute-done.18 = f32[2,12,34,1]{3,2,1,0:T(8,128)S(1)} collective-permute-done((f32[2,12,34,1]{3,2,1,0:T(8,128)S(1)}, f32[2,12,34,1]{3,2,1,0:T(8,128)S(1)}, u32[]{:S(2)}, u32[]{:S(2)}) %collective-permute-start.18) | collective-permute-done | bytes 3296 | tf_op jit(solution)/shard_map/ppermute | solution.py:28
  178.9 10.8 %collective-permute-done.19 = f32[2,12,34,1]{3,2,1,0:T(8,128)S(1)} collective-permute-done((f32[2,12,34,1]{3,2,1,0:T(8,128)S(1)}, f32[2,12,34,1]{3,2,1,0:T(8,128)S(1)}, u32[]{:S(2)}, u32[]{:S(2)}) %collective-permute-start.19) | collective-permute-done | bytes 3296 | tf_op jit(solution)/shard_map/ppermute | solution.py:25
  189.7 4.6 %fusion.17 = f32[2,10,32,512]{3,2,1,0:T(8,128)S(1)} fusion(f32[2,10,32,512]{3,2,1,0:T(8,128)S(1)} %fusion.26, f32[2,1,32,512]{3,2,1,0:T(8,128)S(1)} %collective-permute-done.15, f32[2,1,32,512]{3,2,1,0:T(8,128)S(1)} %collective-permute-done.14, f32[2,12,1,512]{3,2,1,0:T(1,128)S(1)} %collective-permute-done.16, ...), kind=kLoop, calls=%fused_computation.42 | loop fusion | flops 16384000 | bytes 4626896 | tf_op jit(solution)/shard_map/add | solution.py:82
  194.4 3.7 %collective-permute-start.20 = (f32[2,1,32,512]{3,2,1,0:T(8,128)S(1)}, f32[2,1,32,512]{3,2,1,0:T(8,128)S(1)}, u32[]{:S(2)}, u32[]{:S(2)}) collective-permute-start(f32[2,1,32,512]{3,2,1,0:T(8,128)S(1)} %get-tuple-element.22), channel_id=1, source_target_pairs={{0,64},{64,128},{128,192},{1,65},{65,129},{129,193},{2,66},{66,130... | collective-permute-start | bytes 393224 | tf_op jit(solution)/shard_map/ppermute | solution.py:25
  198.1 1.3 collective-permute-start.21
  199.4 1.2 collective-permute-done.20
  200.6 4.4 %collective-permute-done.21 = f32[2,1,32,512]{3,2,1,0:T(8,128)S(1)} collective-permute-done((f32[2,1,32,512]{3,2,1,0:T(8,128)S(1)}, f32[2,1,32,512]{3,2,1,0:T(8,128)S(1)}, u32[]{:S(2)}, u32[]{:S(2)}) %collective-permute-start.21) | collective-permute-done | bytes 131104 | tf_op jit(solution)/shard_map/ppermute | solution.py:28
  205.0 1.9 collective-permute-start.23
  206.9 6.0 %collective-permute-start.22 = (f32[2,12,1,512]{3,2,1,0:T(1,128)S(1)}, f32[2,12,1,512]{3,2,1,0:T(1,128)S(1)}, u32[]{:S(2)}, u32[]{:S(2)}) collective-permute-start(f32[2,12,1,512]{3,2,1,0:T(1,128)S(1)} %get-tuple-element.13), channel_id=1, source_target_pairs={{8,0},{16,8},{24,16},{32,24},{40,32},{48,40},{56,48},{9,1},{17,9},... | collective-permute-start | bytes 147464 | tf_op jit(solution)/shard_map/ppermute | solution.py:28
  213.1 1.6 collective-permute-done.22
  215.0 2.1 collective-permute-start.24
  217.1 2.4 collective-permute-start.25
  219.5 7.4 %collective-permute-done.24 = f32[2,12,34,1]{3,2,1,0:T(8,128)S(1)} collective-permute-done((f32[2,12,34,1]{3,2,1,0:T(8,128)S(1)}, f32[2,12,34,1]{3,2,1,0:T(8,128)S(1)}, u32[]{:S(2)}, u32[]{:S(2)}) %collective-permute-start.24) | collective-permute-done | bytes 3296 | tf_op jit(solution)/shard_map/ppermute | solution.py:28
  226.9 5.0 %collective-permute-done.25 = f32[2,12,34,1]{3,2,1,0:T(8,128)S(1)} collective-permute-done((f32[2,12,34,1]{3,2,1,0:T(8,128)S(1)}, f32[2,12,34,1]{3,2,1,0:T(8,128)S(1)}, u32[]{:S(2)}, u32[]{:S(2)}) %collective-permute-start.25) | collective-permute-done | bytes 3296 | tf_op jit(solution)/shard_map/ppermute | solution.py:25
  231.9 5.5 %fusion.8 = f32[2,10,32,512]{3,2,1,0:T(8,128)} fusion(f32[2,10,32,512]{3,2,1,0:T(8,128)S(1)} %fusion.17, f32[2,1,32,512]{3,2,1,0:T(8,128)S(1)} %collective-permute-done.21, f32[2,1,32,512]{3,2,1,0:T(8,128)S(1)} %collective-permute-done.20, f32[2,12,1,512]{3,2,1,0:T(1,128)S(1)} %collective-permute-done.22, f32[2,12,1,512]{3,2,1,0:T(1,128)S(1)} %collective-permute-done.23, ...), kind=kLoop, calls=%fused_computation.15 | loop fusion | flops 16384000 | bytes 4626896 | tf_op jit(solution)/shard_map/add | solution.py:82
  (70 shorter events, 10.7 us)
Async XLA Ops:
  7.2 89.2 %all-reduce.2.cloned.1.call-start = ((), (), s32[]{:S(2)}) async-start(), calls=%async_computation | async-start | bytes 524288 | tf_op jit(solution)/shard_map/psum | solution.py:107
  8.0 41.5 %collective-permute-start.4 = (s32[1,4]{0,1:T(4,128)S(1)}, s32[1,4]{0,1:T(4,128)S(1)}, u32[]{:S(2)}, u32[]{:S(2)}) collective-permute-start(s32[1,4]{0,1:T(4,128)S(1)} %get-tuple-element.48), channel_id=1, source_target_pairs={{0,8},{8,16},{16,24},{24,32},{32,40},{40,48},{48,56},{1,9},{9,17},... | collective-permute-start | bytes 56 | tf_op jit(solution)/shard_map/ppermute | solution.py:25
  11.5 38.0 %collective-permute-start.5 = (s32[1,4]{0,1:T(4,128)S(1)}, s32[1,4]{0,1:T(4,128)S(1)}, u32[]{:S(2)}, u32[]{:S(2)}) collective-permute-start(s32[1,4]{0,1:T(4,128)S(1)} %get-tuple-element.49), channel_id=1, source_target_pairs={{8,0},{16,8},{24,16},{32,24},{40,32},{48,40},{56,48},{9,1},{17,9},... | collective-permute-start | bytes 56 | tf_op jit(solution)/shard_map/ppermute | solution.py:28
  18.9 11.4 %collective-permute-start = (bf16[4,1,4,128]{3,2,1,0:T(4,128)(2,1)S(1)}, bf16[4,1,4,128]{3,2,1,0:T(4,128)(2,1)S(1)}, u32[]{:S(2)}, u32[]{:S(2)}) collective-permute-start(bf16[4,1,4,128]{3,2,1,0:T(4,128)(2,1)S(1)} %get-tuple-element.37), channel_id=1, source_target_pairs={{0,8},{8,16},{16,24},{24,32},{32,40},{40,48},{48,56},{1,9},{9,17},... | collective-permute-start | bytes 12296 | tf_op jit(solution)/shard_map/ppermute | solution.py:25
  20.8 9.5 %collective-permute-start.1 = (bf16[4,1,4,128]{3,2,1,0:T(4,128)(2,1)S(1)}, bf16[4,1,4,128]{3,2,1,0:T(4,128)(2,1)S(1)}, u32[]{:S(2)}, u32[]{:S(2)}) collective-permute-start(bf16[4,1,4,128]{3,2,1,0:T(4,128)(2,1)S(1)} %get-tuple-element.38), channel_id=1, source_target_pairs={{8,0},{16,8},{24,16},{32,24},{40,32},{48,40},{56,48},{9,1},{17,9},... | collective-permute-start | bytes 12296 | tf_op jit(solution)/shard_map/ppermute | solution.py:28
  30.6 7.8 %collective-permute-start.2 = (bf16[4,34,1,128]{3,2,1,0:T(2,128)(2,1)S(1)}, bf16[4,34,1,128]{3,2,1,0:T(2,128)(2,1)S(1)}, u32[]{:S(2)}, u32[]{:S(2)}) collective-permute-start(bf16[4,34,1,128]{3,2,1,0:T(2,128)(2,1)S(1)} %get-tuple-element.35), channel_id=1, source_target_pairs={{0,1},{1,2},{2,3},{3,4},{4,5},{5,6},{6,7},{8,9},{9,10},{10,11},{11... | collective-permute-start | bytes 104456 | tf_op jit(solution)/shard_map/ppermute | solution.py:25
  32.5 7.7 %collective-permute-start.3 = (bf16[4,34,1,128]{3,2,1,0:T(2,128)(2,1)S(1)}, bf16[4,34,1,128]{3,2,1,0:T(2,128)(2,1)S(1)}, u32[]{:S(2)}, u32[]{:S(2)}) collective-permute-start(bf16[4,34,1,128]{3,2,1,0:T(2,128)(2,1)S(1)} %get-tuple-element.36), channel_id=1, source_target_pairs={{1,0},{2,1},{3,2},{4,3},{5,4},{6,5},{7,6},{9,8},{10,9},{11,10},{12... | collective-permute-start | bytes 104456 | tf_op jit(solution)/shard_map/ppermute | solution.py:28
  48.4 0.9 copy-start.1
  97.3 2.2 copy-start
  99.6 11.3 %collective-permute-start.8 = (f32[2,1,32,512]{3,2,1,0:T(8,128)S(1)}, f32[2,1,32,512]{3,2,1,0:T(8,128)S(1)}, u32[]{:S(2)}, u32[]{:S(2)}) collective-permute-start(f32[2,1,32,512]{3,2,1,0:T(8,128)S(1)} %get-tuple-element.26), channel_id=1, source_target_pairs={{0,64},{64,128},{128,192},{1,65},{65,129},{129,193},{2,66},{66,130... | collective-permute-start | bytes 393224 | tf_op jit(solution)/shard_map/ppermute | solution.py:25
  101.9 9.0 %collective-permute-start.9 = (f32[2,1,32,512]{3,2,1,0:T(8,128)S(1)}, f32[2,1,32,512]{3,2,1,0:T(8,128)S(1)}, u32[]{:S(2)}, u32[]{:S(2)}) collective-permute-start(f32[2,1,32,512]{3,2,1,0:T(8,128)S(1)} %get-tuple-element.27), channel_id=1, source_target_pairs={{64,0},{128,64},{192,128},{65,1},{129,65},{193,129},{66,2},{130,66... | collective-permute-start | bytes 393224 | tf_op jit(solution)/shard_map/ppermute | solution.py:28
  103.2 15.8 %collective-permute-start.6 = (s32[34,1]{0,1:T(1,128)S(1)}, s32[34,1]{0,1:T(1,128)S(1)}, u32[]{:S(2)}, u32[]{:S(2)}) collective-permute-start(s32[34,1]{0,1:T(1,128)S(1)} %get-tuple-element.46), channel_id=1, source_target_pairs={{0,1},{1,2},{2,3},{3,4},{4,5},{5,6},{6,7},{8,9},{9,10},{10,11},{11... | collective-permute-start | bytes 416 | tf_op jit(solution)/shard_map/ppermute | solution.py:25
  105.1 13.8 %collective-permute-start.7 = (s32[34,1]{0,1:T(1,128)S(1)}, s32[34,1]{0,1:T(1,128)S(1)}, u32[]{:S(2)}, u32[]{:S(2)}) collective-permute-start(s32[34,1]{0,1:T(1,128)S(1)} %get-tuple-element.47), channel_id=1, source_target_pairs={{1,0},{2,1},{3,2},{4,3},{5,4},{6,5},{7,6},{9,8},{10,9},{11,10},{12... | collective-permute-start | bytes 416 | tf_op jit(solution)/shard_map/ppermute | solution.py:28
  111.0 8.3 %collective-permute-start.11 = (f32[2,12,1,512]{3,2,1,0:T(1,128)S(1)}, f32[2,12,1,512]{3,2,1,0:T(1,128)S(1)}, u32[]{:S(2)}, u32[]{:S(2)}) collective-permute-start(f32[2,12,1,512]{3,2,1,0:T(1,128)S(1)} %get-tuple-element.16), channel_id=1, source_target_pairs={{0,8},{8,16},{16,24},{24,32},{32,40},{40,48},{48,56},{1,9},{9,17},... | collective-permute-start | bytes 147464 | tf_op jit(solution)/shard_map/ppermute | solution.py:25
  114.4 6.3 %collective-permute-start.10 = (f32[2,12,1,512]{3,2,1,0:T(1,128)S(1)}, f32[2,12,1,512]{3,2,1,0:T(1,128)S(1)}, u32[]{:S(2)}, u32[]{:S(2)}) collective-permute-start(f32[2,12,1,512]{3,2,1,0:T(1,128)S(1)} %get-tuple-element.17), channel_id=1, source_target_pairs={{8,0},{16,8},{24,16},{32,24},{40,32},{48,40},{56,48},{9,1},{17,9},... | collective-permute-start | bytes 147464 | tf_op jit(solution)/shard_map/ppermute | solution.py:28
  120.9 13.1 %collective-permute-start.12 = (f32[2,12,34,1]{3,2,1,0:T(8,128)S(1)}, f32[2,12,34,1]{3,2,1,0:T(8,128)S(1)}, u32[]{:S(2)}, u32[]{:S(2)}) collective-permute-start(f32[2,12,34,1]{3,2,1,0:T(8,128)S(1)} %get-tuple-element.10), channel_id=1, source_target_pairs={{1,0},{2,1},{3,2},{4,3},{5,4},{6,5},{7,6},{9,8},{10,9},{11,10},{12... | collective-permute-start | bytes 9800 | tf_op jit(solution)/shard_map/ppermute | solution.py:28
  122.9 15.6 %collective-permute-start.13 = (f32[2,12,34,1]{3,2,1,0:T(8,128)S(1)}, f32[2,12,34,1]{3,2,1,0:T(8,128)S(1)}, u32[]{:S(2)}, u32[]{:S(2)}) collective-permute-start(f32[2,12,34,1]{3,2,1,0:T(8,128)S(1)} %get-tuple-element.11), channel_id=1, source_target_pairs={{0,1},{1,2},{2,3},{3,4},{4,5},{5,6},{6,7},{8,9},{9,10},{10,11},{11... | collective-permute-start | bytes 9800 | tf_op jit(solution)/shard_map/ppermute | solution.py:25
  144.5 7.1 %collective-permute-start.14 = (f32[2,1,32,512]{3,2,1,0:T(8,128)S(1)}, f32[2,1,32,512]{3,2,1,0:T(8,128)S(1)}, u32[]{:S(2)}, u32[]{:S(2)}) collective-permute-start(f32[2,1,32,512]{3,2,1,0:T(8,128)S(1)} %get-tuple-element.24), channel_id=1, source_target_pairs={{0,64},{64,128},{128,192},{1,65},{65,129},{129,193},{2,66},{66,130... | collective-permute-start | bytes 393224 | tf_op jit(solution)/shard_map/ppermute | solution.py:25
  149.0 6.9 %collective-permute-start.15 = (f32[2,1,32,512]{3,2,1,0:T(8,128)S(1)}, f32[2,1,32,512]{3,2,1,0:T(8,128)S(1)}, u32[]{:S(2)}, u32[]{:S(2)}) collective-permute-start(f32[2,1,32,512]{3,2,1,0:T(8,128)S(1)} %get-tuple-element.25), channel_id=1, source_target_pairs={{64,0},{128,64},{192,128},{65,1},{129,65},{193,129},{66,2},{130,66... | collective-permute-start | bytes 393224 | tf_op jit(solution)/shard_map/ppermute | solution.py:28
  156.0 8.1 %collective-permute-start.17 = (f32[2,12,1,512]{3,2,1,0:T(1,128)S(1)}, f32[2,12,1,512]{3,2,1,0:T(1,128)S(1)}, u32[]{:S(2)}, u32[]{:S(2)}) collective-permute-start(f32[2,12,1,512]{3,2,1,0:T(1,128)S(1)} %get-tuple-element.14), channel_id=1, source_target_pairs={{0,8},{8,16},{16,24},{24,32},{32,40},{40,48},{48,56},{1,9},{9,17},... | collective-permute-start | bytes 147464 | tf_op jit(solution)/shard_map/ppermute | solution.py:25
  159.1 11.0 %collective-permute-start.16 = (f32[2,12,1,512]{3,2,1,0:T(1,128)S(1)}, f32[2,12,1,512]{3,2,1,0:T(1,128)S(1)}, u32[]{:S(2)}, u32[]{:S(2)}) collective-permute-start(f32[2,12,1,512]{3,2,1,0:T(1,128)S(1)} %get-tuple-element.15), channel_id=1, source_target_pairs={{8,0},{16,8},{24,16},{32,24},{40,32},{48,40},{56,48},{9,1},{17,9},... | collective-permute-start | bytes 147464 | tf_op jit(solution)/shard_map/ppermute | solution.py:28
  170.4 8.6 %collective-permute-start.18 = (f32[2,12,34,1]{3,2,1,0:T(8,128)S(1)}, f32[2,12,34,1]{3,2,1,0:T(8,128)S(1)}, u32[]{:S(2)}, u32[]{:S(2)}) collective-permute-start(f32[2,12,34,1]{3,2,1,0:T(8,128)S(1)} %get-tuple-element.8), channel_id=1, source_target_pairs={{1,0},{2,1},{3,2},{4,3},{5,4},{6,5},{7,6},{9,8},{10,9},{11,10},{12... | collective-permute-start | bytes 9800 | tf_op jit(solution)/shard_map/ppermute | solution.py:28
  172.3 17.4 %collective-permute-start.19 = (f32[2,12,34,1]{3,2,1,0:T(8,128)S(1)}, f32[2,12,34,1]{3,2,1,0:T(8,128)S(1)}, u32[]{:S(2)}, u32[]{:S(2)}) collective-permute-start(f32[2,12,34,1]{3,2,1,0:T(8,128)S(1)} %get-tuple-element.9), channel_id=1, source_target_pairs={{0,1},{1,2},{2,3},{3,4},{4,5},{5,6},{6,7},{8,9},{9,10},{10,11},{11... | collective-permute-start | bytes 9800 | tf_op jit(solution)/shard_map/ppermute | solution.py:25
  194.4 6.2 %collective-permute-start.20 = (f32[2,1,32,512]{3,2,1,0:T(8,128)S(1)}, f32[2,1,32,512]{3,2,1,0:T(8,128)S(1)}, u32[]{:S(2)}, u32[]{:S(2)}) collective-permute-start(f32[2,1,32,512]{3,2,1,0:T(8,128)S(1)} %get-tuple-element.22), channel_id=1, source_target_pairs={{0,64},{64,128},{128,192},{1,65},{65,129},{129,193},{2,66},{66,130... | collective-permute-start | bytes 393224 | tf_op jit(solution)/shard_map/ppermute | solution.py:25
  198.1 6.9 %collective-permute-start.21 = (f32[2,1,32,512]{3,2,1,0:T(8,128)S(1)}, f32[2,1,32,512]{3,2,1,0:T(8,128)S(1)}, u32[]{:S(2)}, u32[]{:S(2)}) collective-permute-start(f32[2,1,32,512]{3,2,1,0:T(8,128)S(1)} %get-tuple-element.23), channel_id=1, source_target_pairs={{64,0},{128,64},{192,128},{65,1},{129,65},{193,129},{66,2},{130,66... | collective-permute-start | bytes 393224 | tf_op jit(solution)/shard_map/ppermute | solution.py:28
  205.0 8.1 %collective-permute-start.23 = (f32[2,12,1,512]{3,2,1,0:T(1,128)S(1)}, f32[2,12,1,512]{3,2,1,0:T(1,128)S(1)}, u32[]{:S(2)}, u32[]{:S(2)}) collective-permute-start(f32[2,12,1,512]{3,2,1,0:T(1,128)S(1)} %get-tuple-element.12), channel_id=1, source_target_pairs={{0,8},{8,16},{16,24},{24,32},{32,40},{40,48},{48,56},{1,9},{9,17},... | collective-permute-start | bytes 147464 | tf_op jit(solution)/shard_map/ppermute | solution.py:25
  206.9 7.8 %collective-permute-start.22 = (f32[2,12,1,512]{3,2,1,0:T(1,128)S(1)}, f32[2,12,1,512]{3,2,1,0:T(1,128)S(1)}, u32[]{:S(2)}, u32[]{:S(2)}) collective-permute-start(f32[2,12,1,512]{3,2,1,0:T(1,128)S(1)} %get-tuple-element.13), channel_id=1, source_target_pairs={{8,0},{16,8},{24,16},{32,24},{40,32},{48,40},{56,48},{9,1},{17,9},... | collective-permute-start | bytes 147464 | tf_op jit(solution)/shard_map/ppermute | solution.py:28
  215.0 11.9 %collective-permute-start.24 = (f32[2,12,34,1]{3,2,1,0:T(8,128)S(1)}, f32[2,12,34,1]{3,2,1,0:T(8,128)S(1)}, u32[]{:S(2)}, u32[]{:S(2)}) collective-permute-start(f32[2,12,34,1]{3,2,1,0:T(8,128)S(1)} %get-tuple-element.6), channel_id=1, source_target_pairs={{1,0},{2,1},{3,2},{4,3},{5,4},{6,5},{7,6},{9,8},{10,9},{11,10},{12... | collective-permute-start | bytes 9800 | tf_op jit(solution)/shard_map/ppermute | solution.py:28
  217.1 14.8 %collective-permute-start.25 = (f32[2,12,34,1]{3,2,1,0:T(8,128)S(1)}, f32[2,12,34,1]{3,2,1,0:T(8,128)S(1)}, u32[]{:S(2)}, u32[]{:S(2)}) collective-permute-start(f32[2,12,34,1]{3,2,1,0:T(8,128)S(1)} %get-tuple-element.7), channel_id=1, source_target_pairs={{0,1},{1,2},{2,3},{3,4},{4,5},{5,6},{6,7},{8,9},{9,10},{10,11},{11... | collective-permute-start | bytes 9800 | tf_op jit(solution)/shard_map/ppermute | solution.py:25
Sparse Core Ops, SparseCore 0:
  49.4 46.8 all-reduce.1
where the time goes:
time: 245 us; the launch traced here: 244 us
  waiting for transfers between devices  109 us (44%)
  starting transfers between devices  82.7 us (34%)
  other arithmetic  24.4 us (10%)
  between operations  14.6 us (6%)
  matrix products  6.88 us (3%)
  local copies, waits for them, and re-layouts  6.32 us (3%)
    ppermute x13, starting transfers between devices, extended(): lax.ppermute(lax.slice_in_dim(block, 0, width, axis=dim), axis, backward)  47.3 us
    psum x1, waiting for transfers between devices, on_device(): summed = lax.psum(partial_value, 'sec')  46.7 us
    ppermute x13, waiting for transfers between devices, extended(): lax.ppermute(lax.slice_in_dim(block, 0, width, axis=dim), axis, backward)  39.7 us
    ppermute x13, starting transfers between devices, extended(): lax.ppermute(lax.slice_in_dim(block, block.shape[dim] - width, None, axis...  35.4 us
    ppermute x13, waiting for transfers between devices, extended(): lax.ppermute(lax.slice_in_dim(block, block.shape[dim] - width, None, axis...  22.9 us
    add x3, other arithmetic, stencil(): centre + mask_mid * (diffusion * spread - advection * carried + vertical_...  16.1 us
    dot_general x1, matrix products, on_device(): jnp.einsum('fxtsc,xtsdc->fxtd', blocks, remap_weights[:, :, 0], preferred...  6.88 us
  transfers between devices with their start and end apart: 27, of which 17 were waited for; matrix products, arithmetic and copies ran while one was open for 7% of the time, Pallas kernels for 0%

commit v1 on v0

v1 whole, which is shorter than its diff:
```python
import jax
import jax.numpy as jnp
from jax import lax
from jax.experimental import pallas as pl
from jax.experimental.pallas import tpu as pltpu
from jax.sharding import PartitionSpec as P

f32 = jnp.float32
bf16 = jnp.bfloat16

DRAG = 0.6
WIND_GAIN = 0.5
HEAT_GAIN = 0.5
SALT_GAIN = 0.5
DIFFUSION = 0.15
ADVECTION = 0.5
VERTICAL = 0.2

NX = 32
NT = 4
NL = 10
LANES = 128

YF, YW, YC, YT, YROWS = 0, 256, 448, 464, 528
XPLANE, XF, XROWS = 176, 880, 912
CZ, CROWS = 640, 1024

VMEM_BYTES = 48 * 1024 * 1024

PLANES = (
    [("t", 0, level) for level in range(NL)]
    + [("t", 1, level) for level in range(NL)]
    + [("c", 0, 0), ("c", 0, 9), ("c", 1, 0), ("c", 1, 9)]
    + [("c", 0, level) for level in range(1, 9)]
    + [("c", 1, level) for level in range(1, 9)]
)
MASK_PLANE = len(PLANES)
PLANE_AT = {plane: index for index, plane in enumerate(PLANES)}


def column(row):
    rows = lax.broadcasted_iota(jnp.int32, (NX, NX), 0)
    cols = lax.broadcasted_iota(jnp.int32, (NX, NX), 1)
    return jnp.sum(jnp.where(rows == cols, jnp.broadcast_to(row, (NX, NX)), 0.0), axis=1, keepdims=True)


def lane_ids(shape):
    return lax.broadcasted_iota(jnp.int32, shape, len(shape) - 1)


def slot_codes(src, live):
    slot = lax.broadcasted_iota(jnp.int32, (NT, 2, NX), 1)
    return jnp.where(slot < live[...], src[...], 9).astype(f32)


def roll(value, shift, axis):
    shift %= value.shape[axis]
    return value if shift == 0 else pltpu.roll(value, shift, axis)


def unpack_north(pack, plane, rows=slice(None)):
    return roll(pack[plane // 32][rows], -4 * (plane % 32), 1)


def unpack_south(pack, plane, rows=slice(None)):
    return roll(pack[plane // 32][rows], 4 * (plane % 32), 1)


def pack_y_kernel(air, src, live, land, w, tr, cu, yn, ys, flux, air_s, wn, ws, rows_s, code_s, edge, sems):
    copies = [pltpu.make_async_copy(air.at[:, :, t, 0, :], air_s.at[t], sems.at[t]) for t in range(NT)]
    copies.append(pltpu.make_async_copy(w.at[:, NT - 1, 0, :, pl.ds(112, 16), :], wn, sems.at[4]))
    copies.append(pltpu.make_async_copy(w.at[:, 0, 0, :, pl.ds(0, 16), :], ws, sems.at[5]))
    for k, source in enumerate((tr, cu)):
        copies.append(pltpu.make_async_copy(source.at[:, :, :, pl.ds(384, 128)], edge.at[0, k], sems.at[6 + k]))
        copies.append(pltpu.make_async_copy(source.at[:, :, :, pl.ds(0, 128)], edge.at[1, k], sems.at[8 + k]))
    for copy in copies:
        copy.start()
    codes = slot_codes(src, live)
    code_s[...] = jnp.zeros((16, LANES), f32)
    for t in range(NT):
        code_s[2 * t : 2 * t + 2, 0:NX] = codes[t]
    table = code_s[...].astype(bf16)
    yn[YC : YC + 16, :] = table
    ys[YC : YC + 16, :] = table
    for t in range(NT):
        copies[t].wait()
        u, v, ta, qa, ts = (air_s[t, k] for k in range(5))
        rate = DRAG * (1.0 + 0.5 * jnp.tanh(ts - ta)) * jnp.sqrt(u * u + v * v + 1.0)
        values = (rate * u, rate * v, rate * (ts - ta), rate * (jnp.exp(0.3 * ts) - qa))
        for f, value in enumerate(values):
            value = value.astype(bf16)
            flux[t, f] = value
            at = YF + ((t % 2) * 4 + f) * NX
            (ys if t < 2 else yn)[at : at + NX, :] = value
    for copy in copies[4:]:
        copy.wait()
    for send, tile, first in ((yn, wn, 13), (ys, ws, 0)):
        for x in range(NX):
            for s in range(2):
                block = tile[x, s].astype(f32)
                for d in range(3):
                    rows_s[pl.ds(d * 64 + s * 32 + x, 1), :] = block[first + d : first + d + 1]
        send[YW : YW + 192, :] = rows_s[...].astype(bf16)
    group = lane_ids((NX, LANES)) // 4
    for side, send in enumerate((yn, ys)):
        mask_tile = land[NT - 1 if side == 0 else 0 : NT if side == 0 else 1, :].astype(f32)
        for part in range(2):
            pack = jnp.zeros((NX, LANES), f32)
            for at in range(32):
                plane = part * 32 + at
                if plane > MASK_PLANE:
                    break
                if plane == MASK_PLANE:
                    value = jnp.broadcast_to(column(mask_tile), (NX, LANES))
                else:
                    kind, c, level = PLANES[plane]
                    value = edge[side, 0 if kind == "t" else 1, c, level]
                if side == 0:
                    pack = jnp.where(group == 31 - at, roll(value, -4 * at, 1), pack)
                else:
                    pack = jnp.where(group == at, roll(value, 4 * at, 1), pack)
            send[YT + part * NX : YT + (part + 1) * NX, :] = pack.astype(bf16)


def pack_z_kernel(tr, cu, zu, zd, t_s, c_s, sems):
    copies = [
        pltpu.make_async_copy(tr.at[:, pl.ds(0, 3)], t_s.at[0], sems.at[0]),
        pltpu.make_async_copy(cu.at[:, pl.ds(0, 2)], c_s.at[0], sems.at[1]),
        pltpu.make_async_copy(tr.at[:, pl.ds(NL - 3, 3)], t_s.at[1], sems.at[2]),
        pltpu.make_async_copy(cu.at[:, pl.ds(NL - 2, 2)], c_s.at[1], sems.at[3]),
    ]
    for copy in copies:
        copy.start()
    for copy in copies:
        copy.wait()
    for side, send in enumerate((zu, zd)):
        for c in range(2):
            for level in range(3):
                send[c * 3 + level] = t_s[side, c, level].astype(bf16)
            for level in range(2):
                send[6 + c * 2 + level] = c_s[side, c, level].astype(bf16)


def field_packs(y):
    return (y[YT : YT + NX, :].astype(f32), y[YT + NX : YT + 2 * NX, :].astype(f32))


def pack_x_kernel(flux, yn_r, ys_r, land, tr, cu, xe, xw, rows_s, edge, sems):
    copies = []
    for k, source in enumerate((tr, cu)):
        copies.append(pltpu.make_async_copy(source.at[:, :, pl.ds(0, 8), :], edge.at[0, k], sems.at[2 * k]))
        copies.append(pltpu.make_async_copy(source.at[:, :, pl.ds(24, 8), :], edge.at[1, k], sems.at[2 * k + 1]))
    for copy in copies:
        copy.start()
    south, north = field_packs(yn_r), field_packs(ys_r)
    low = lane_ids((8, LANES)) < 64
    masks = [column(land[t : t + 1, :].astype(f32)) for t in range(NT)]
    for copy in copies:
        copy.wait()
    for side, send in enumerate((xw, xe)):
        rows = slice(0, 8) if side == 0 else slice(24, 32)
        keep = slice(0, 4) if side == 0 else slice(4, 8)
        x = 0 if side == 0 else NX - 1
        rows_s[...] = jnp.zeros((XROWS, LANES), f32)
        for plane in range(MASK_PLANE + 1):
            edge_col = jnp.where(low, unpack_north(north, plane, rows), unpack_south(south, plane, rows))
            rows_s[4 * XPLANE + plane * 4 : 4 * XPLANE + plane * 4 + 4, :] = edge_col[keep]
            for c in range(4):
                if plane == MASK_PLANE:
                    value = jnp.broadcast_to(masks[c][rows], (8, LANES))
                else:
                    kind, component, level = PLANES[plane]
                    value = edge[side, 0 if kind == "t" else 1, component, level, :, c * LANES : (c + 1) * LANES]
                rows_s[c * XPLANE + plane * 4 : c * XPLANE + plane * 4 + 4, :] = value[keep]
        for t in range(8):
            for f in range(4):
                if 2 <= t < 6:
                    block = flux[t - 2, f].astype(f32)
                else:
                    got, half = (yn_r, t) if t < 2 else (ys_r, t - 6)
                    at = YF + (half * 4 + f) * NX
                    block = got[at : at + NX, :].astype(f32)
                rows_s[XF + t * 4 + f : XF + t * 4 + f + 1, :] = block[x : x + 1]
        send[...] = rows_s[...].astype(bf16)


def remap_kernel(flux, yn_r, ys_r, xe_r, xw_r, src, live, w, part, up, down, across, rim, rhs, wbuf, sems):
    copies = []
    for t in range(NT):
        for half in range(2):
            rows = pl.ds(half * 16, 16)
            copies.append(pltpu.make_async_copy(w.at[rows, t, 0], wbuf.at[t, rows], sems.at[2 * t + half]))
    for copy in copies:
        copy.start()

    west = xe_r[XF : XF + 32, :].astype(f32)
    east = xw_r[XF : XF + 32, :].astype(f32)
    for t in range(8):
        for f in range(4):
            if 2 <= t < 6:
                block = flux[t - 2, f]
            else:
                got, half = (yn_r, t) if t < 2 else (ys_r, t - 6)
                at = YF + (half * 4 + f) * NX
                block = got[at : at + NX, :]
            rim[t, f, 8 : 8 + NX, :] = block.astype(f32)
            rim[t, f, 7:8, :] = west[t * 4 + f : t * 4 + f + 1]
            rim[t, f, 8 + NX : 9 + NX, :] = east[t * 4 + f : t * 4 + f + 1]

    def blocks(tile, row):
        code = jnp.broadcast_to(column(row), (NX, LANES))
        picked = [code == float(k) for k in range(9)]
        result = []
        for f in range(4):
            block = jnp.zeros((NX, LANES), f32)
            for k in range(9):
                x0 = 7 + k // 3
                block = jnp.where(picked[k], rim[tile + 2 + k % 3 - 1, f, x0 : x0 + NX, :], block)
            result.append(block)
        return result

    codes = slot_codes(src, live)
    for t in range(NT):
        for s in range(2):
            stacked = jnp.concatenate(blocks(t, codes[t, s : s + 1, :]), axis=0)
            rhs[t, s * LANES : (s + 1) * LANES, :] = stacked.T.astype(bf16)

    lane = lane_ids((NX, LANES))
    edges = [jnp.zeros((NX, LANES), f32) for f in range(4)]
    for got, tile, row, at in ((yn_r, -1, 6, 125), (ys_r, NT, 0, 0)):
        table = got[YC : YC + 16, :].astype(f32)
        picked = [blocks(tile, table[row + s : row + s + 1, 0:NX]) for s in range(2)]
        for d in range(3):
            weight = [
                got[YW + (d * 2 + s) * NX : YW + (d * 2 + s + 1) * NX, :].astype(f32) for s in range(2)
            ]
            for f in range(4):
                total = jnp.sum(weight[0] * picked[0][f] + weight[1] * picked[1][f], axis=1, keepdims=True)
                edges[f] = jnp.where(lane == at + d, total, edges[f])
    for f in range(4):
        part[4 * LANES + f * NX : 4 * LANES + (f + 1) * NX, :] = edges[f]

    own = lane_ids((LANES, LANES)) % NX
    for t in range(NT):
        acc = jnp.zeros((LANES, LANES), f32)
        for half in range(2):
            copies[2 * t + half].wait()

            def one(x, acc, t=t):
                weights = jnp.concatenate([wbuf[t, x, 0], wbuf[t, x, 1]], axis=1)
                product = jnp.dot(weights, rhs[t], preferred_element_type=f32)
                return jnp.where(own == x, product, acc)

            acc = lax.fori_loop(half * 16, half * 16 + 16, one, acc, unroll=4)
        part[t * LANES : (t + 1) * LANES, :] = acc.T

    whole = part[...].astype(bf16)
    for send in (up, down, across):
        send[0:CZ, :] = whole
    for send, first in ((up, 0), (down, 32)):
        for side, got in enumerate((xw_r, xe_r)):
            for c in range(5):
                base = c * XPLANE
                if first == 0:
                    heat = got[base : base + 16, :].astype(f32)[0:8]
                    salt = got[base + 32 : base + 48, :].astype(f32)[8:16]
                else:
                    heat = got[base + 32 : base + 48, :].astype(f32)[0:8]
                    salt = got[base + 64 : base + 80, :].astype(f32)[8:16]
                at = CZ + (side * 5 + c) * 32
                send[at : at + 16, :] = jnp.concatenate([heat, salt], axis=0).astype(bf16)
                send[at + 16 : at + 32, :] = got[base + 80 : base + 96, :]
        send[CZ + 320 : CZ + 352, :] = yn_r[YT : YT + NX, :]
        send[CZ + 352 : CZ + 384, :] = ys_r[YT : YT + NX, :]


def flux_kernel(part, up_r, down_r, across_r, land, yn_r, ys_r, out, ext, de, dw, rows_s):
    south, north = field_packs(yn_r), field_packs(ys_r)
    low = lane_ids((NX, LANES)) < 64
    for c in range(5):
        if c < 4:
            mask = jnp.broadcast_to(column(land[c : c + 1, :].astype(f32)), (NX, LANES))
        else:
            mask = jnp.where(low, unpack_north(north, MASK_PLANE), unpack_south(south, MASK_PLANE))
        for f in range(4):
            at = c * LANES + f * NX
            total = part[at : at + NX, :] + up_r[at : at + NX, :].astype(f32)
            total = total + down_r[at : at + NX, :].astype(f32) + across_r[at : at + NX, :].astype(f32)
            total = total * mask
            if c < 4:
                out[f, :, c * LANES : (c + 1) * LANES] = total
            ext[f, c] = total
            rows_s[0, c * 16 + f * 4 : c * 16 + f * 4 + 4, :] = total[0:4]
            rows_s[1, c * 16 + f * 4 : c * 16 + f * 4 + 4, :] = total[NX - 4 : NX]
    dw[...] = rows_s[0].astype(bf16)
    de[...] = rows_s[1].astype(bf16)


def lane_next(value, lane):
    rolled = pltpu.roll(value, LANES - 1, 2)
    return jnp.where(lane == LANES - 1, jnp.concatenate([rolled[1:], rolled[:1]], axis=0), rolled)


def lane_prev(value, lane):
    rolled = pltpu.roll(value, 1, 2)
    return jnp.where(lane == 0, jnp.concatenate([rolled[-1:], rolled[:-1]], axis=0), rolled)


def ocean_kernel(
    tr, cu, zu_r, zd_r, yn_r, ys_r, xe_r, xw_r, up_r, down_r, ext, de_r, dw_r, land, out,
    g0, g1, vel, mask, coef, force, xs,
):
    sec = lax.axis_index("sec")
    own, west, east = slice(12, 44), slice(8, 12), slice(44, 48)
    south, north = field_packs(yn_r), field_packs(ys_r)
    low = lane_ids((NX, LANES)) < 64

    xs[0] = xw_r[0:XF, :].astype(f32)
    xs[1] = xe_r[0:XF, :].astype(f32)

    def edge_col(plane):
        return jnp.where(low, unpack_north(north, plane), unpack_south(south, plane))

    for c in range(4):
        mask[c, own, :] = jnp.broadcast_to(column(land[c : c + 1, :].astype(f32)), (NX, LANES))
    mask[4, own, :] = edge_col(MASK_PLANE)
    for c in range(5):
        at = c * XPLANE + MASK_PLANE * 4
        mask[c, east, :] = xs[0, at : at + 4, :]
        mask[c, west, :] = xs[1, at : at + 4, :]

    lane = lane_ids((5, 8, LANES))
    for r in range(8, 48, 8):
        rows, m = slice(r, r + 8), mask[:, r : r + 8, :]
        around = mask[:, r + 1 : r + 9, :] + mask[:, r - 1 : r + 7, :] + lane_next(m, lane) + lane_prev(m, lane)
        coef[:, rows, :] = m * (1.0 - DIFFUSION * around)

    def put(ref, where, plane_rows, scale=None):
        for c in range(5):
            for rows, value in plane_rows(c):
                ref[where + (c, rows)] = value * mask[c, rows, :]

    for plane, (kind, c, level) in enumerate(PLANES):
        source = tr if kind == "t" else cu

        def pieces(col, plane=plane, source=source, c=c, level=level):
            if col < 4:
                body = source[c, level, :, col * LANES : (col + 1) * LANES]
            else:
                body = edge_col(plane)
            at = col * XPLANE + plane * 4
            return ((own, body), (east, xs[0, at : at + 4, :]), (west, xs[1, at : at + 4, :]))

        if kind == "t":
            put(g0, (c, level + 3), pieces)
        else:
            put(vel, (c, level + 2), pieces)

    for got, z, below in ((up_r, zu_r, True), (down_r, zd_r, False)):
        z_south = (got[CZ + 320 : CZ + 352, :].astype(f32),)
        z_north = (got[CZ + 352 : CZ + 384, :].astype(f32),)
        halo = [[got[CZ + (s * 5 + c) * 32 : CZ + (s * 5 + c + 1) * 32, :].astype(f32) for c in range(5)] for s in (0, 1)]
        for c in range(2):
            for k in range(3):
                at = (13 + k) if below else k
                for col in range(4):
                    body = z[c * 3 + k, :, col * LANES : (col + 1) * LANES].astype(f32)
                    g0[c, at, col, own, :] = body * mask[col, own, :]
                step = k if below else k - 1
                if not 0 <= step < 2:
                    continue
                plane = PLANE_AT[("t", c, k if below else 7 + k)]
                col4 = jnp.where(low, unpack_north(z_north, plane), unpack_south(z_south, plane))
                g0[c, at, 4, own, :] = col4 * mask[4, own, :]
                for col in range(5):
                    r = c * 8 + step * 4
                    g0[c, at, col, east, :] = halo[0][col][r : r + 4] * mask[col, east, :]
                    g0[c, at, col, west, :] = halo[1][col][r : r + 4] * mask[col, west, :]
            for k in range(2):
                at = (12 + k) if below else k
                for col in range(4):
                    body = z[6 + c * 2 + k, :, col * LANES : (col + 1) * LANES].astype(f32)
                    vel[c, at, col, own, :] = body * mask[col, own, :]
                if k != (0 if below else 1):
                    continue
                plane = PLANE_AT[("c", c, 0 if below else 9)]
                col4 = jnp.where(low, unpack_north(z_north, plane), unpack_south(z_south, plane))
                vel[c, at, 4, own, :] = col4 * mask[4, own, :]
                for col in range(5):
                    r = 16 + c * 8 + (0 if below else 4)
                    vel[c, at, col, east, :] = halo[0][col][r : r + 4] * mask[col, east, :]
                    vel[c, at, col, west, :] = halo[1][col][r : r + 4] * mask[col, west, :]

    @pl.when(sec == 0)
    def _():
        dw_f, de_f = dw_r[...].astype(f32), de_r[...].astype(f32)
        for f, (ref, at, gain) in enumerate(
            ((vel, (0, 2), WIND_GAIN), (vel, (1, 2), WIND_GAIN), (g0, (0, 3), HEAT_GAIN), (g0, (1, 3), -SALT_GAIN))
        ):
            for c in range(5):
                r = c * 16 + f * 4
                for rows, value in ((own, ext[f, c]), (east, dw_f[r : r + 4]), (west, de_f[r : r + 4])):
                    ref[at + (c, rows)] += gain * value * mask[c, rows, :]

    first = sec * NL - 3
    total_levels = NL * lax.axis_size("sec")

    def level_step(src, l, rows):
        level = first + l
        up = jnp.where(level > 0, VERTICAL, 0.0).astype(f32)
        down = jnp.where(level < total_levels - 1, VERTICAL, 0.0).astype(f32)
        r = rows.start
        m = mask[:, rows, :]
        a = (ADVECTION) * vel[0, l - 1, :, rows, :]
        b = (ADVECTION) * vel[1, l - 1, :, rows, :]
        base = DIFFUSION * m
        centre = coef[:, rows, :] - (up + down) * m
        mu, md = up * m, down * m
        results = []
        for c in range(2):
            g = src[c, l, :, rows, :]
            new = centre * g
            new += (base - a) * src[c, l, :, r + 1 : r + 9, :] + (base + a) * src[c, l, :, r - 1 : r + 7, :]
            new += (base - b) * lane_next(g, lane) + (base + b) * lane_prev(g, lane)
            new += mu * src[c, l - 1, :, rows, :] + md * src[c, l + 1, :, rows, :]
            results.append(new)
        return results

    for step, (src, dst) in enumerate(((g0, g1), (g1, g0))):

        def one_level(l, _, src=src, dst=dst):
            for r in range(8, 48, 8):
                rows = slice(r, r + 8)
                for c, value in enumerate(level_step(src, l, rows)):
                    dst[c, l, :, rows, :] = value
            return 0

        lax.fori_loop(1 + step, 15 - step, one_level, 0)

    def last_level(l, _):
        for r in range(12, 44, 8):
            rows = slice(r, r + 8)
            for c, value in enumerate(level_step(g0, l, rows)):
                for col in range(4):
                    at = (c, l - 3, slice(r - 12, r - 4), slice(col * LANES, (col + 1) * LANES))
                    out[at] = jnp.where(mask[col, rows, :] > 0.0, value[col], tr[at])
        return 0

    lax.fori_loop(3, 13, last_level, 0)


ANY = pl.BlockSpec(memory_space=pl.ANY)
VMEM = pl.BlockSpec(memory_space=pltpu.VMEM)


def call(kernel, in_specs, outs, scratch, name, flops=0, bytes_accessed=0):
    return pl.pallas_call(
        kernel,
        out_shape=[jax.ShapeDtypeStruct(shape, dtype) for shape, dtype in outs],
        in_specs=in_specs,
        out_specs=[VMEM] * len(outs),
        scratch_shapes=scratch,
        compiler_params=pltpu.CompilerParams(vmem_limit_bytes=VMEM_BYTES),
        cost_estimate=pl.CostEstimate(flops=flops, bytes_accessed=bytes_accessed, transcendentals=0),
        name=name,
    )


def shifted(value, axis, step, wrap=False):
    count = lax.axis_size(axis)
    pairs = [(i, (i + step) % count) for i in range(count) if wrap or 0 <= i + step < count]
    return lax.ppermute(value, axis, pairs)


def on_device(air_surface, remap_weights, sources, live_count, land_sea, tracers, currents):
    src = jnp.transpose(sources[:, :, 0, :], (1, 2, 0))
    live = jnp.transpose(live_count, (1, 2, 0))
    land = jnp.transpose(land_sea, (1, 0))
    dma = pltpu.SemaphoreType.DMA

    yn, ys, flux = call(
        pack_y_kernel,
        [ANY, VMEM, VMEM, VMEM, ANY, ANY, ANY],
        [((YROWS, LANES), bf16), ((YROWS, LANES), bf16), ((NT, 4, NX, LANES), bf16)],
        [
            pltpu.VMEM((NT, 5, NX, LANES), f32),
            pltpu.VMEM((NX, 2, 16, LANES), bf16),
            pltpu.VMEM((NX, 2, 16, LANES), bf16),
            pltpu.VMEM((192, LANES), f32),
            pltpu.VMEM((16, LANES), f32),
            pltpu.VMEM((2, 2, 2, NL, NX, LANES), f32),
            dma((10,)),
        ],
        "pack_y",
        bytes_accessed=4_000_000,
    )(air_surface, src, live, land, remap_weights, tracers, currents)
    yn_r = shifted(yn, "gy", 1)
    ys_r = shifted(ys, "gy", -1)

    zu, zd = call(
        pack_z_kernel,
        [ANY, ANY],
        [((10, NX, 512), bf16)] * 2,
        [pltpu.VMEM((2, 2, 3, NX, 512), f32), pltpu.VMEM((2, 2, 2, NX, 512), f32), dma((4,))],
        "pack_z",
        bytes_accessed=4_000_000,
    )(tracers, currents)
    zu_r = shifted(zu, "sec", -1)
    zd_r = shifted(zd, "sec", 1)

    xe, xw = call(
        pack_x_kernel,
        [VMEM, VMEM, VMEM, VMEM, ANY, ANY],
        [((XROWS, LANES), bf16)] * 2,
        [pltpu.VMEM((XROWS, LANES), f32), pltpu.VMEM((2, 2, 2, NL, 8, 512), f32), dma((4,))],
        "pack_x",
        bytes_accessed=4_000_000,
    )(flux, yn_r, ys_r, land, tracers, currents)
    xe_r = shifted(xe, "gx", 1)
    xw_r = shifted(xw, "gx", -1)

    part, up, down, across = call(
        remap_kernel,
        [VMEM] * 7 + [ANY],
        [((CZ, LANES), f32), ((CROWS, LANES), bf16), ((CROWS, LANES), bf16), ((CZ, LANES), bf16)],
        [
            pltpu.VMEM((8, 4, 48, LANES), f32),
            pltpu.VMEM((NT, 2 * LANES, LANES), bf16),
            pltpu.VMEM((NT, NX, 2, LANES, LANES), bf16),
            dma((8,)),
        ],
        "remap",
        bytes_accessed=16_000_000,
    )(flux, yn_r, ys_r, xe_r, xw_r, src, live, remap_weights)
    up_r = shifted(up, "sec", -1, True)
    down_r = shifted(down, "sec", 1, True)
    across_r = shifted(across, "sec", 2, True)

    ocean_flux, ext, de, dw = call(
        flux_kernel,
        [VMEM] * 7,
        [((4, NX, 512), f32), ((4, 5, NX, LANES), f32), ((80, LANES), bf16), ((80, LANES), bf16)],
        [pltpu.VMEM((2, 80, LANES), f32)],
        "flux_sum",
        bytes_accessed=4_000_000,
    )(part, up_r, down_r, across_r, land, yn_r, ys_r)
    de_r = shifted(de, "gx", 1)
    dw_r = shifted(dw, "gx", -1)

    (tracers_out,) = call(
        ocean_kernel,
        [VMEM] * 14,
        [((2, NL, NX, 512), f32)],
        [
            pltpu.VMEM((2, 16, 5, 56, LANES), f32),
            pltpu.VMEM((2, 16, 5, 56, LANES), f32),
            pltpu.VMEM((2, 14, 5, 56, LANES), f32),
            pltpu.VMEM((5, 56, LANES), f32),
            pltpu.VMEM((5, 56, LANES), f32),
            pltpu.VMEM((4, 5, 56, LANES), f32),
            pltpu.VMEM((2, XF, LANES), f32),
        ],
        "ocean",
        bytes_accessed=16_000_000,
    )(tracers, currents, zu_r, zd_r, yn_r, ys_r, xe_r, xw_r, up_r, down_r, ext, de_r, dw_r, land)
    return (tracers_out, ocean_flux)


def solution(mesh):
    return jax.shard_map(
        on_device,
        mesh=mesh,
        in_specs=(
            P(None, "gx", "gy", "sec", None),
            P("gx", "gy", "sec", None, None, None),
            P("gx", "gy", "sec", None),
            P("gx", "gy", "sec"),
            P("gx", "gy"),
            P(None, "sec", "gx", "gy"),
            P(None, "sec", "gx", "gy"),
        ),
        out_specs=(P(None, "sec", "gx", "gy"), P(None, "gx", "gy")),
        check_vma=False,
    )
```

time: 245 us -> 79 us (0.32)
  the two profiles are of different devices: /device:TPU:160 before, /device:TPU:152 now
where the time goes in v1:
time: 79 us; the launch traced here: 78.5 us
  starting transfers between devices  30.3 us (38%)
  Pallas kernels  21.5 us (27%)
  waiting for transfers between devices  20.1 us (25%)
  local copies, waits for them, and re-layouts  5.67 us (7%)
  between operations  0.81 us (1%)
    ppermute x11, starting transfers between devices, shifted(): return lax.ppermute(value, axis, pairs)  30.3 us
    ppermute x11, waiting for transfers between devices, shifted(): return lax.ppermute(value, axis, pairs)  20.1 us
    pallas_call x1, Pallas kernels, on_device(): call(ocean_kernel, [VMEM] * 14, [((2, NL, NX, 512), f32)], [pltpu.VMEM((2...  9.31 us
    pallas_call x1, Pallas kernels, on_device(): call(remap_kernel, [VMEM] * 7 + [ANY], [((CZ, LANES), f32), ((CROWS, LANE...  8.67 us
    unnamed x22, local copies, waits for them, and re-layouts  5.67 us
    pallas_call x1, Pallas kernels, on_device(): call(pack_y_kernel, [ANY, VMEM, VMEM, VMEM, ANY, ANY, ANY], [((YROWS, LAN...  1.87 us
  transfers between devices with their start and end apart: 11, of which 6 were waited for; matrix products, arithmetic and copies ran while one was open for 0% of the time, Pallas kernels for 13%

profile of v1, /device:TPU:152, one launch (start us, length us, event | category | flops | bytes accessed | tf_op | source)
XLA Modules:
  0.0 78.5 jit_solution(17181964192460137986)
XLA Ops:
  0.6 0.0 copy-start
  0.6 1.3 %copy-done = f32[2,10,32,512]{3,2,1,0:T(8,128)S(1)} copy-done((f32[2,10,32,512]{3,2,1,0:T(8,128)S(1)}, f32[2,10,32,512]{3,2,1,0:T(8,128)}, u32[]{:S(2)}) %copy-start) | copy-done | bytes 1310744
  1.9 0.0 copy-start.2
  2.0 1.3 %copy-done.2 = f32[2,10,32,512]{3,2,1,0:T(8,128)S(1)} copy-done((f32[2,10,32,512]{3,2,1,0:T(8,128)S(1)}, f32[2,10,32,512]{3,2,1,0:T(8,128)}, u32[]{:S(2)}) %copy-start.2) | copy-done | bytes 1310744
  3.3 0.0 copy-start.4
  3.3 1.0 %copy-done.4 = f32[5,32,4,1,128]{4,3,2,1,0:T(1,128)S(1)} copy-done((f32[5,32,4,1,128]{4,3,2,1,0:T(1,128)S(1)}, f32[5,32,4,1,128]{4,3,2,1,0:T(1,128)}, u32[]{:S(2)}) %copy-start.4) | copy-done | bytes 327704
  4.2 0.0 copy-start.5
  4.2 0.7 copy-done.5
  4.9 0.7 copy-done.7
  5.6 0.0 copy-start.9
  5.6 0.7 copy-done.9
  6.3 1.9 %pack_y.1 = (bf16[528,128]{1,0:T(8,128)(2,1)S(1)}, bf16[528,128]{1,0:T(8,128)(2,1)S(1)}, bf16[4,4,32,128]{3,2,1,0:T(8,128)(2,1)S(1)}) custom-call(f32[5,32,4,1,128]{4,3,2,1,0:T(1,128)S(1)} %copy-done.4, s32[4,2,32]{2,1,0:T(2,128)S(1)} %bitcast.9, s32[4,1,32]{2,1,0:T(1,128)S(1)} %bitcast.11, s32[4,32]{1,0:T(4,128)S(1)} %bitcast.5, ...), custom_call_target="tpu_custom_call" | custom-call | bytes 4000000 | tf_op jit(solution)/shard_map/pack_y/pallas_call | solution.py:481
  8.2 1.9 %collective-permute-start.2 = (bf16[528,128]{1,0:T(8,128)(2,1)S(1)}, bf16[528,128]{1,0:T(8,128)(2,1)S(1)}, u32[]{:S(2)}, u32[]{:S(2)}) collective-permute-start(bf16[528,128]{1,0:T(8,128)(2,1)S(1)} %get-tuple-element.19), channel_id=1, source_target_pairs={{0,1},{1,2},{2,3},{3,4},{4,5},{5,6},{6,7},{8,9},{9,10},{10,11},{11... | collective-permute-start | bytes 405512 | tf_op jit(solution)/shard_map/ppermute | solution.py:472
  10.1 5.8 %collective-permute-start.3 = (bf16[528,128]{1,0:T(8,128)(2,1)S(1)}, bf16[528,128]{1,0:T(8,128)(2,1)S(1)}, u32[]{:S(2)}, u32[]{:S(2)}) collective-permute-start(bf16[528,128]{1,0:T(8,128)(2,1)S(1)} %get-tuple-element.20), channel_id=1, source_target_pairs={{1,0},{2,1},{3,2},{4,3},{5,4},{6,5},{7,6},{9,8},{10,9},{11,10},{12... | collective-permute-start | bytes 405512 | tf_op jit(solution)/shard_map/ppermute | solution.py:472
  15.9 1.6 %collective-permute-done.2.yn_r = bf16[528,128]{1,0:T(8,128)(2,1)S(1)} collective-permute-done((bf16[528,128]{1,0:T(8,128)(2,1)S(1)}, bf16[528,128]{1,0:T(8,128)(2,1)S(1)}, u32[]{:S(2)}, u32[]{:S(2)}) %collective-permute-start.2) | collective-permute-done | bytes 135200 | tf_op jit(solution)/shard_map/ppermute | solution.py:472
  17.5 2.2 %collective-permute-done.3.ys_r = bf16[528,128]{1,0:T(8,128)(2,1)S(1)} collective-permute-done((bf16[528,128]{1,0:T(8,128)(2,1)S(1)}, bf16[528,128]{1,0:T(8,128)(2,1)S(1)}, u32[]{:S(2)}, u32[]{:S(2)}) %collective-permute-start.3) | collective-permute-done | bytes 135200 | tf_op jit(solution)/shard_map/ppermute | solution.py:472
  19.7 0.5 pack_x.1
  20.2 1.9 %collective-permute-start.4 = (bf16[912,128]{1,0:T(8,128)(2,1)S(1)}, bf16[912,128]{1,0:T(8,128)(2,1)S(1)}, u32[]{:S(2)}, u32[]{:S(2)}) collective-permute-start(bf16[912,128]{1,0:T(8,128)(2,1)S(1)} %get-tuple-element.22), channel_id=1, source_target_pairs={{0,8},{8,16},{16,24},{24,32},{32,40},{40,48},{48,56},{1,9},{9,17},... | collective-permute-start | bytes 700424 | tf_op jit(solution)/shard_map/ppermute | solution.py:472
  22.1 0.0 copy-start.8
  22.1 0.0 copy-start.10
  22.1 3.9 %collective-permute-start.5 = (bf16[912,128]{1,0:T(8,128)(2,1)S(1)}, bf16[912,128]{1,0:T(8,128)(2,1)S(1)}, u32[]{:S(2)}, u32[]{:S(2)}) collective-permute-start(bf16[912,128]{1,0:T(8,128)(2,1)S(1)} %get-tuple-element.23), channel_id=1, source_target_pairs={{8,0},{16,8},{24,16},{32,24},{40,32},{48,40},{56,48},{9,1},{17,9},... | collective-permute-start | bytes 700424 | tf_op jit(solution)/shard_map/ppermute | solution.py:472
  26.1 0.3 pack_z.1
  26.4 1.3 %collective-permute-start = (bf16[10,32,512]{2,1,0:T(8,128)(2,1)S(1)}, bf16[10,32,512]{2,1,0:T(8,128)(2,1)S(1)}, u32[]{:S(2)}, u32[]{:S(2)}) collective-permute-start(bf16[10,32,512]{2,1,0:T(8,128)(2,1)S(1)} %get-tuple-element.17), channel_id=1, source_target_pairs={{64,0},{128,64},{192,128},{65,1},{129,65},{193,129},{66,2},{130,66... | collective-permute-start | bytes 983048 | tf_op jit(solution)/shard_map/ppermute | solution.py:472
  27.7 0.0 copy-start.6
  27.7 4.6 %collective-permute-start.1 = (bf16[10,32,512]{2,1,0:T(8,128)(2,1)S(1)}, bf16[10,32,512]{2,1,0:T(8,128)(2,1)S(1)}, u32[]{:S(2)}, u32[]{:S(2)}) collective-permute-start(bf16[10,32,512]{2,1,0:T(8,128)(2,1)S(1)} %get-tuple-element.18), channel_id=1, source_target_pairs={{0,64},{64,128},{128,192},{1,65},{65,129},{129,193},{2,66},{66,130... | collective-permute-start | bytes 983048 | tf_op jit(solution)/shard_map/ppermute | solution.py:472
  32.3 0.0 collective-permute-done.4.xe_r
  32.3 2.2 %collective-permute-done.5.xw_r = bf16[912,128]{1,0:T(8,128)(2,1)S(1)} collective-permute-done((bf16[912,128]{1,0:T(8,128)(2,1)S(1)}, bf16[912,128]{1,0:T(8,128)(2,1)S(1)}, u32[]{:S(2)}, u32[]{:S(2)}) %collective-permute-start.5) | collective-permute-done | bytes 233504 | tf_op jit(solution)/shard_map/ppermute | solution.py:472
  34.5 0.0 copy-done.8
  34.5 0.0 copy-done.10
  34.5 0.0 copy-start.1
  34.5 8.7 %remap.1 = (f32[640,128]{1,0:T(8,128)S(1)}, bf16[1024,128]{1,0:T(8,128)(2,1)S(1)}, bf16[1024,128]{1,0:T(8,128)(2,1)S(1)}, bf16[640,128]{1,0:T(8,128)(2,1)S(1)}) custom-call(bf16[4,4,32,128]{3,2,1,0:T(8,128)(2,1)S(1)} %get-tuple-element.21.flux, bf16[528,128]{1,0:T(8,128)(2,1)S(1)} %collective-permute-done.2.yn_r, ...), custom_call_target="tpu_custom_call" | custom-call | bytes 16000000 | tf_op jit(solution)/shard_map/remap/pallas_call | solution.py:522
  43.2 2.8 %collective-permute-start.6 = (bf16[1024,128]{1,0:T(8,128)(2,1)S(1)}, bf16[1024,128]{1,0:T(8,128)(2,1)S(1)}, u32[]{:S(2)}, u32[]{:S(2)}) collective-permute-start(bf16[1024,128]{1,0:T(8,128)(2,1)S(1)} %get-tuple-element.24), channel_id=1, source_target_pairs={{0,192},{64,0},{128,64},{192,128},{1,193},{65,1},{129,65},{193,129... | collective-permute-start | bytes 786440 | tf_op jit(solution)/shard_map/ppermute | solution.py:472
  46.0 0.0 collective-permute-start.7
  46.0 2.3 %collective-permute-start.8 = (bf16[640,128]{1,0:T(8,128)(2,1)S(1)}, bf16[640,128]{1,0:T(8,128)(2,1)S(1)}, u32[]{:S(2)}, u32[]{:S(2)}) collective-permute-start(bf16[640,128]{1,0:T(8,128)(2,1)S(1)} %get-tuple-element.27), channel_id=1, source_target_pairs={{0,128},{64,192},{128,0},{192,64},{1,129},{65,193},{129,1},{193,65... | collective-permute-start | bytes 491528 | tf_op jit(solution)/shard_map/ppermute | solution.py:472
  48.3 9.4 %collective-permute-done.8.across_r = bf16[640,128]{1,0:T(8,128)(2,1)S(1)} collective-permute-done((bf16[640,128]{1,0:T(8,128)(2,1)S(1)}, bf16[640,128]{1,0:T(8,128)(2,1)S(1)}, u32[]{:S(2)}, u32[]{:S(2)}) %collective-permute-start.8) | collective-permute-done | bytes 163872 | tf_op jit(solution)/shard_map/ppermute | solution.py:472
  57.7 0.0 collective-permute-done.6.up_r
  57.7 0.8 %collective-permute-done.7.down_r = bf16[1024,128]{1,0:T(8,128)(2,1)S(1)} collective-permute-done((bf16[1024,128]{1,0:T(8,128)(2,1)S(1)}, bf16[1024,128]{1,0:T(8,128)(2,1)S(1)}, u32[]{:S(2)}, u32[]{:S(2)}) %collective-permute-start.7) | collective-permute-done | bytes 262176 | tf_op jit(solution)/shard_map/ppermute | solution.py:472
  58.6 0.0 copy-done.6
  58.6 0.9 %flux_sum.1 = (f32[4,32,512]{2,1,0:T(8,128)}, f32[4,5,32,128]{3,2,1,0:T(8,128)S(1)}, bf16[80,128]{1,0:T(8,128)(2,1)S(1)}, bf16[80,128]{1,0:T(8,128)(2,1)S(1)}) custom-call(f32[640,128]{1,0:T(8,128)S(1)} %get-tuple-element.26.part, bf16[1024,128]{1,0:T(8,128)(2,1)S(1)} %collective-permute-done.6.up_r, bf16[1024,128]{1,0:T(8,128)(2,1)S(1)} %collective-permute-done.7.down_r, ...), custom_call_target="tpu_custom_call" | custom-call | bytes 4000000 | tf_op jit(solution)/shard_map/flux_sum/pallas_call | solution.py:539
  59.4 1.9 %collective-permute-start.9 = (bf16[80,128]{1,0:T(8,128)(2,1)S(1)}, bf16[80,128]{1,0:T(8,128)(2,1)S(1)}, u32[]{:S(2)}, u32[]{:S(2)}) collective-permute-start(bf16[80,128]{1,0:T(8,128)(2,1)S(1)} %get-tuple-element.29), channel_id=1, source_target_pairs={{0,8},{8,16},{16,24},{24,32},{32,40},{40,48},{48,56},{1,9},{9,17},... | collective-permute-start | bytes 61448 | tf_op jit(solution)/shard_map/ppermute | solution.py:472
  61.4 3.9 %collective-permute-start.10 = (bf16[80,128]{1,0:T(8,128)(2,1)S(1)}, bf16[80,128]{1,0:T(8,128)(2,1)S(1)}, u32[]{:S(2)}, u32[]{:S(2)}) collective-permute-start(bf16[80,128]{1,0:T(8,128)(2,1)S(1)} %get-tuple-element.30), channel_id=1, source_target_pairs={{8,0},{16,8},{24,16},{32,24},{40,32},{48,40},{56,48},{9,1},{17,9},... | collective-permute-start | bytes 61448 | tf_op jit(solution)/shard_map/ppermute | solution.py:472
  65.3 0.0 collective-permute-done.zu_r
  65.3 0.0 collective-permute-done.1.zd_r
  65.3 0.0 collective-permute-done.9.de_r
  65.3 3.8 %collective-permute-done.10.dw_r = bf16[80,128]{1,0:T(8,128)(2,1)S(1)} collective-permute-done((bf16[80,128]{1,0:T(8,128)(2,1)S(1)}, bf16[80,128]{1,0:T(8,128)(2,1)S(1)}, u32[]{:S(2)}, u32[]{:S(2)}) %collective-permute-start.10) | collective-permute-done | bytes 20512 | tf_op jit(solution)/shard_map/ppermute | solution.py:472
  69.1 0.0 copy-done.1
  69.1 0.0 copy-done.3
  69.2 9.3 %ocean.1 = f32[2,10,32,512]{3,2,1,0:T(8,128)} custom-call(f32[2,10,32,512]{3,2,1,0:T(8,128)S(1)} %copy-done.1, f32[2,10,32,512]{3,2,1,0:T(8,128)S(1)} %copy-done.3, bf16[10,32,512]{2,1,0:T(8,128)(2,1)S(1)} %collective-permute-done.zu_r, bf16[10,32,512]{2,1,0:T(8,128)(2,1)S(1)} %collective-permute-done.1.zd_r, ...), custom_call_target="tpu_custom_call" | custom-call | bytes 16000000 | tf_op jit(solution)/shard_map/ocean/pallas_call | solution.py:550
  (2 shorter events, 0.0 us)
Async XLA Ops:
  0.6 1.3 %copy-start = (f32[2,10,32,512]{3,2,1,0:T(8,128)S(1)}, f32[2,10,32,512]{3,2,1,0:T(8,128)}, u32[]{:S(2)}) copy-start(f32[2,10,32,512]{3,2,1,0:T(8,128)} %tr.7) | copy-start | bytes 3932164
  1.9 1.3 %copy-start.2 = (f32[2,10,32,512]{3,2,1,0:T(8,128)S(1)}, f32[2,10,32,512]{3,2,1,0:T(8,128)}, u32[]{:S(2)}) copy-start(f32[2,10,32,512]{3,2,1,0:T(8,128)} %cu.7) | copy-start | bytes 3932164
  3.3 1.0 %copy-start.4 = (f32[5,32,4,1,128]{4,3,2,1,0:T(1,128)S(1)}, f32[5,32,4,1,128]{4,3,2,1,0:T(1,128)}, u32[]{:S(2)}) copy-start(f32[5,32,4,1,128]{4,3,2,1,0:T(1,128)} %air.1) | copy-start | bytes 983044
  4.2 0.7 copy-start.5
  4.9 0.7 copy-start.7
  5.6 0.7 copy-start.9
  8.2 9.3 %collective-permute-start.2 = (bf16[528,128]{1,0:T(8,128)(2,1)S(1)}, bf16[528,128]{1,0:T(8,128)(2,1)S(1)}, u32[]{:S(2)}, u32[]{:S(2)}) collective-permute-start(bf16[528,128]{1,0:T(8,128)(2,1)S(1)} %get-tuple-element.19), channel_id=1, source_target_pairs={{0,1},{1,2},{2,3},{3,4},{4,5},{5,6},{6,7},{8,9},{9,10},{10,11},{11... | collective-permute-start | bytes 405512 | tf_op jit(solution)/shard_map/ppermute | solution.py:472
  10.1 9.6 %collective-permute-start.3 = (bf16[528,128]{1,0:T(8,128)(2,1)S(1)}, bf16[528,128]{1,0:T(8,128)(2,1)S(1)}, u32[]{:S(2)}, u32[]{:S(2)}) collective-permute-start(bf16[528,128]{1,0:T(8,128)(2,1)S(1)} %get-tuple-element.20), channel_id=1, source_target_pairs={{1,0},{2,1},{3,2},{4,3},{5,4},{6,5},{7,6},{9,8},{10,9},{11,10},{12... | collective-permute-start | bytes 405512 | tf_op jit(solution)/shard_map/ppermute | solution.py:472
  20.2 12.1 %collective-permute-start.4 = (bf16[912,128]{1,0:T(8,128)(2,1)S(1)}, bf16[912,128]{1,0:T(8,128)(2,1)S(1)}, u32[]{:S(2)}, u32[]{:S(2)}) collective-permute-start(bf16[912,128]{1,0:T(8,128)(2,1)S(1)} %get-tuple-element.22), channel_id=1, source_target_pairs={{0,8},{8,16},{16,24},{24,32},{32,40},{40,48},{48,56},{1,9},{9,17},... | collective-permute-start | bytes 700424 | tf_op jit(solution)/shard_map/ppermute | solution.py:472
  22.1 12.4 %copy-start.8 = (s32[32,4,1,2]{0,3,2,1:T(2,128)S(1)}, s32[32,4,1,2]{0,3,2,1:T(2,128)}, u32[]{:S(2)}) copy-start(s32[32,4,1,2]{0,3,2,1:T(2,128)} %param.9) | copy-start | bytes 3076
  22.1 12.4 %copy-start.10 = (s32[32,4,1]{0,2,1:T(1,128)S(1)}, s32[32,4,1]{0,2,1:T(1,128)}, u32[]{:S(2)}) copy-start(s32[32,4,1]{0,2,1:T(1,128)} %param.10) | copy-start | bytes 1540
  22.1 12.4 %collective-permute-start.5 = (bf16[912,128]{1,0:T(8,128)(2,1)S(1)}, bf16[912,128]{1,0:T(8,128)(2,1)S(1)}, u32[]{:S(2)}, u32[]{:S(2)}) collective-permute-start(bf16[912,128]{1,0:T(8,128)(2,1)S(1)} %get-tuple-element.23), channel_id=1, source_target_pairs={{8,0},{16,8},{24,16},{32,24},{40,32},{48,40},{56,48},{9,1},{17,9},... | collective-permute-start | bytes 700424 | tf_op jit(solution)/shard_map/ppermute | solution.py:472
  26.4 38.9 %collective-permute-start = (bf16[10,32,512]{2,1,0:T(8,128)(2,1)S(1)}, bf16[10,32,512]{2,1,0:T(8,128)(2,1)S(1)}, u32[]{:S(2)}, u32[]{:S(2)}) collective-permute-start(bf16[10,32,512]{2,1,0:T(8,128)(2,1)S(1)} %get-tuple-element.17), channel_id=1, source_target_pairs={{64,0},{128,64},{192,128},{65,1},{129,65},{193,129},{66,2},{130,66... | collective-permute-start | bytes 983048 | tf_op jit(solution)/shard_map/ppermute | solution.py:472
  27.7 30.8 %copy-start.6 = (s32[32,4]{0,1:T(4,128)S(1)}, s32[32,4]{0,1:T(4,128)}, u32[]{:S(2)}) copy-start(s32[32,4]{0,1:T(4,128)} %param.11) | copy-start | bytes 1540
  27.7 37.6 %collective-permute-start.1 = (bf16[10,32,512]{2,1,0:T(8,128)(2,1)S(1)}, bf16[10,32,512]{2,1,0:T(8,128)(2,1)S(1)}, u32[]{:S(2)}, u32[]{:S(2)}) collective-permute-start(bf16[10,32,512]{2,1,0:T(8,128)(2,1)S(1)} %get-tuple-element.18), channel_id=1, source_target_pairs={{0,64},{64,128},{128,192},{1,65},{65,129},{129,193},{2,66},{66,130... | collective-permute-start | bytes 983048 | tf_op jit(solution)/shard_map/ppermute | solution.py:472
  34.5 34.7 %copy-start.1 = (f32[2,10,32,512]{3,2,1,0:T(8,128)S(1)}, f32[2,10,32,512]{3,2,1,0:T(8,128)}, u32[]{:S(2)}) copy-start(f32[2,10,32,512]{3,2,1,0:T(8,128)} %tr.7) | copy-start | bytes 3932164
  34.5 34.7 %copy-start.3 = (f32[2,10,32,512]{3,2,1,0:T(8,128)S(1)}, f32[2,10,32,512]{3,2,1,0:T(8,128)}, u32[]{:S(2)}) copy-start(f32[2,10,32,512]{3,2,1,0:T(8,128)} %cu.7) | copy-start | bytes 3932164
  43.2 14.6 %collective-permute-start.6 = (bf16[1024,128]{1,0:T(8,128)(2,1)S(1)}, bf16[1024,128]{1,0:T(8,128)(2,1)S(1)}, u32[]{:S(2)}, u32[]{:S(2)}) collective-permute-start(bf16[1024,128]{1,0:T(8,128)(2,1)S(1)} %get-tuple-element.24), channel_id=1, source_target_pairs={{0,192},{64,0},{128,64},{192,128},{1,193},{65,1},{129,65},{193,129... | collective-permute-start | bytes 786440 | tf_op jit(solution)/shard_map/ppermute | solution.py:472
  46.0 12.5 %collective-permute-start.7 = (bf16[1024,128]{1,0:T(8,128)(2,1)S(1)}, bf16[1024,128]{1,0:T(8,128)(2,1)S(1)}, u32[]{:S(2)}, u32[]{:S(2)}) collective-permute-start(bf16[1024,128]{1,0:T(8,128)(2,1)S(1)} %get-tuple-element.25), channel_id=1, source_target_pairs={{0,64},{64,128},{128,192},{192,0},{1,65},{65,129},{129,193},{193,1... | collective-permute-start | bytes 786440 | tf_op jit(solution)/shard_map/ppermute | solution.py:472
  46.0 11.7 %collective-permute-start.8 = (bf16[640,128]{1,0:T(8,128)(2,1)S(1)}, bf16[640,128]{1,0:T(8,128)(2,1)S(1)}, u32[]{:S(2)}, u32[]{:S(2)}) collective-permute-start(bf16[640,128]{1,0:T(8,128)(2,1)S(1)} %get-tuple-element.27), channel_id=1, source_target_pairs={{0,128},{64,192},{128,0},{192,64},{1,129},{65,193},{129,1},{193,65... | collective-permute-start | bytes 491528 | tf_op jit(solution)/shard_map/ppermute | solution.py:472
  59.4 5.9 %collective-permute-start.9 = (bf16[80,128]{1,0:T(8,128)(2,1)S(1)}, bf16[80,128]{1,0:T(8,128)(2,1)S(1)}, u32[]{:S(2)}, u32[]{:S(2)}) collective-permute-start(bf16[80,128]{1,0:T(8,128)(2,1)S(1)} %get-tuple-element.29), channel_id=1, source_target_pairs={{0,8},{8,16},{16,24},{24,32},{32,40},{40,48},{48,56},{1,9},{9,17},... | collective-permute-start | bytes 61448 | tf_op jit(solution)/shard_map/ppermute | solution.py:472
  61.4 7.8 %collective-permute-start.10 = (bf16[80,128]{1,0:T(8,128)(2,1)S(1)}, bf16[80,128]{1,0:T(8,128)(2,1)S(1)}, u32[]{:S(2)}, u32[]{:S(2)}) collective-permute-start(bf16[80,128]{1,0:T(8,128)(2,1)S(1)} %get-tuple-element.30), channel_id=1, source_target_pairs={{8,0},{16,8},{24,16},{32,24},{40,32},{48,40},{56,48},{9,1},{17,9},... | collective-permute-start | bytes 61448 | tf_op jit(solution)/shard_map/ppermute | solution.py:472

commit v2 on v1

v2 whole, which is shorter than its diff:
```python
import jax
import jax.numpy as jnp
from jax import lax
from jax.experimental import pallas as pl
from jax.experimental.pallas import tpu as pltpu
from jax.sharding import PartitionSpec as P

f32 = jnp.float32
bf16 = jnp.bfloat16

DRAG = 0.6
WIND_GAIN = 0.5
HEAT_GAIN = 0.5
SALT_GAIN = 0.5
DIFFUSION = 0.15
ADVECTION = 0.5
VERTICAL = 0.2

NX = 32
NT = 4
NL = 10
LANES = 128

YF, YW, YC, YT, YROWS = 0, 256, 448, 464, 528
XPLANE, XF, XROWS = 176, 880, 912
CROWS = 528
ZROWS = 384
LAND = 8

VMEM_BYTES = 24 * 1024 * 1024

PLANES = (
    [("t", 0, level) for level in range(NL)]
    + [("t", 1, level) for level in range(NL)]
    + [("c", 0, 0), ("c", 0, 9), ("c", 1, 0), ("c", 1, 9)]
    + [("c", 0, level) for level in range(1, 9)]
    + [("c", 1, level) for level in range(1, 9)]
)
MASK_PLANE = len(PLANES)
PLANE_AT = {plane: index for index, plane in enumerate(PLANES)}


def column(row):
    rows = lax.broadcasted_iota(jnp.int32, (NX, NX), 0)
    cols = lax.broadcasted_iota(jnp.int32, (NX, NX), 1)
    return jnp.sum(jnp.where(rows == cols, jnp.broadcast_to(row, (NX, NX)), 0.0), axis=1, keepdims=True)


def lane_ids(shape):
    return lax.broadcasted_iota(jnp.int32, shape, len(shape) - 1)


def start(*copies):
    for copy in copies:
        copy.start()


def wait(*copies):
    for copy in copies:
        copy.wait()


def roll(value, shift, axis):
    shift %= value.shape[axis]
    return value if shift == 0 else pltpu.roll(value, shift, axis)


def unpack_north(pack, plane, rows=slice(None)):
    return roll(pack[plane // 32][rows], -4 * (plane % 32), 1)


def unpack_south(pack, plane, rows=slice(None)):
    return roll(pack[plane // 32][rows], 4 * (plane % 32), 1)


def pack_y_kernel(
    air, src_h, live_h, land_h, w, tr, cu, yn, ys, flux, table, src, live, land, air_s, wn, ws, rows_s, edge, sems
):
    copies = [pltpu.make_async_copy(air.at[:, :, t, 0, :], air_s.at[t], sems.at[t]) for t in range(NT)]
    copies.append(pltpu.make_async_copy(w.at[:, NT - 1, 0, :, pl.ds(112, 16), :], wn, sems.at[4]))
    copies.append(pltpu.make_async_copy(w.at[:, 0, 0, :, pl.ds(0, 16), :], ws, sems.at[5]))
    for k, source in enumerate((tr, cu)):
        copies.append(pltpu.make_async_copy(source.at[:, :, :, pl.ds(384, 128)], edge.at[0, k], sems.at[6 + k]))
        copies.append(pltpu.make_async_copy(source.at[:, :, :, pl.ds(0, 128)], edge.at[1, k], sems.at[8 + k]))
    small = [
        pltpu.make_async_copy(source, target, sems.at[10 + k])
        for k, (source, target) in enumerate(((src_h, src), (live_h, live), (land_h, land)))
    ]
    start(*copies[:4], *small, *copies[4:])
    for t in range(NT):
        copies[t].wait()
        u, v, ta, qa, ts = (air_s[t, k] for k in range(5))
        rate = DRAG * (1.0 + 0.5 * jnp.tanh(ts - ta)) * jnp.sqrt(u * u + v * v + 1.0)
        values = (rate * u, rate * v, rate * (ts - ta), rate * (jnp.exp(0.3 * ts) - qa))
        for f, value in enumerate(values):
            value = value.astype(bf16)
            flux[t, f] = value
            at = YF + ((t % 2) * 4 + f) * NX
            (ys if t < 2 else yn)[at : at + NX, :] = value
    wait(*small)
    slot = lax.broadcasted_iota(jnp.int32, (NT, 2, NX), 1)
    codes = jnp.where(slot < live[...], src[...], 9).astype(f32)
    table[...] = jnp.zeros((16, LANES), f32)
    for t in range(NT):
        table[2 * t : 2 * t + 2, 0:NX] = codes[t]
    table[LAND : LAND + NT, 0:NX] = land[...].astype(f32)
    sent = table[...].astype(bf16)
    yn[YC : YC + 16, :] = sent
    ys[YC : YC + 16, :] = sent
    wait(*copies[4:])
    for send, tile, first in ((yn, wn, 13), (ys, ws, 0)):
        for x in range(NX):
            for s in range(2):
                block = tile[x, s].astype(f32)
                for d in range(3):
                    rows_s[pl.ds(d * 64 + s * 32 + x, 1), :] = block[first + d : first + d + 1]
        send[YW : YW + 192, :] = rows_s[...].astype(bf16)
    group = lane_ids((NX, LANES)) // 4
    for side, send in enumerate((yn, ys)):
        mask_tile = land[NT - 1 if side == 0 else 0 : NT if side == 0 else 1, :].astype(f32)
        for part in range(2):
            pack = jnp.zeros((NX, LANES), f32)
            for at in range(32):
                plane = part * 32 + at
                if plane > MASK_PLANE:
                    break
                if plane == MASK_PLANE:
                    value = jnp.broadcast_to(column(mask_tile), (NX, LANES))
                else:
                    kind, c, level = PLANES[plane]
                    value = edge[side, 0 if kind == "t" else 1, c, level]
                if side == 0:
                    pack = jnp.where(group == 31 - at, roll(value, -4 * at, 1), pack)
                else:
                    pack = jnp.where(group == at, roll(value, 4 * at, 1), pack)
            send[YT + part * NX : YT + (part + 1) * NX, :] = pack.astype(bf16)


def pack_z_kernel(tr, cu, after, zu, zd, t_s, c_s, sems):
    copies = [
        pltpu.make_async_copy(tr.at[:, pl.ds(0, 3)], t_s.at[0], sems.at[0]),
        pltpu.make_async_copy(cu.at[:, pl.ds(0, 2)], c_s.at[0], sems.at[1]),
        pltpu.make_async_copy(tr.at[:, pl.ds(NL - 3, 3)], t_s.at[1], sems.at[2]),
        pltpu.make_async_copy(cu.at[:, pl.ds(NL - 2, 2)], c_s.at[1], sems.at[3]),
    ]
    for copy in copies:
        copy.start()
    for copy in copies:
        copy.wait()
    for side, send in enumerate((zu, zd)):
        for c in range(2):
            for level in range(3):
                send[c * 3 + level] = t_s[side, c, level].astype(bf16)
            for level in range(2):
                send[6 + c * 2 + level] = c_s[side, c, level].astype(bf16)


def inside(axis, low):
    at = lax.axis_index(axis)
    return jnp.where(at > 0 if low else at < lax.axis_size(axis) - 1, 1.0, 0.0).astype(f32)


def field_packs(y):
    return (y[YT : YT + NX, :].astype(f32), y[YT + NX : YT + 2 * NX, :].astype(f32))


def pack_x_kernel(flux, yn_r, ys_r, table, tr, cu, xe, xw, rows_s, edge, sems):
    copies = []
    for k, source in enumerate((tr, cu)):
        copies.append(pltpu.make_async_copy(source.at[:, :, pl.ds(0, 8), :], edge.at[0, k], sems.at[2 * k]))
        copies.append(pltpu.make_async_copy(source.at[:, :, pl.ds(24, 8), :], edge.at[1, k], sems.at[2 * k + 1]))
    for copy in copies:
        copy.start()
    south, north = field_packs(yn_r), field_packs(ys_r)
    low = lane_ids((8, LANES)) < 64
    masks = [column(table[LAND + t : LAND + t + 1, 0:NX]) for t in range(NT)]
    in_south, in_north = inside("gy", True), inside("gy", False)
    for copy in copies:
        copy.wait()
    for side, send in enumerate((xw, xe)):
        rows = slice(0, 8) if side == 0 else slice(24, 32)
        keep = slice(0, 4) if side == 0 else slice(4, 8)
        x = 0 if side == 0 else NX - 1
        rows_s[...] = jnp.zeros((XROWS, LANES), f32)
        for plane in range(MASK_PLANE + 1):
            edge_col = jnp.where(low, unpack_north(north, plane, rows), unpack_south(south, plane, rows))
            if plane == MASK_PLANE:
                edge_col = edge_col * jnp.where(low, in_north, in_south)
            rows_s[4 * XPLANE + plane * 4 : 4 * XPLANE + plane * 4 + 4, :] = edge_col[keep]
            for c in range(4):
                if plane == MASK_PLANE:
                    value = jnp.broadcast_to(masks[c][rows], (8, LANES))
                else:
                    kind, component, level = PLANES[plane]
                    value = edge[side, 0 if kind == "t" else 1, component, level, :, c * LANES : (c + 1) * LANES]
                rows_s[c * XPLANE + plane * 4 : c * XPLANE + plane * 4 + 4, :] = value[keep]
        for t in range(8):
            for f in range(4):
                if 2 <= t < 6:
                    block = flux[t - 2, f].astype(f32)
                else:
                    got, half = (yn_r, t) if t < 2 else (ys_r, t - 6)
                    at = YF + (half * 4 + f) * NX
                    block = got[at : at + NX, :].astype(f32) * (in_south if t < 2 else in_north)
                rows_s[XF + t * 4 + f : XF + t * 4 + f + 1, :] = block[x : x + 1]
        send[...] = rows_s[...].astype(bf16)


def remap_kernel(flux, yn_r, ys_r, table, w, after_x, part, wedge, rim, blk, wbuf, sems):
    copies = []
    for t in range(NT):
        for half in range(2):
            rows = pl.ds(half * 16, 16)
            copies.append(pltpu.make_async_copy(w.at[rows, t, 0], wbuf.at[t, rows], sems.at[2 * t + half]))
    start(*copies)

    zero = jnp.zeros((8, LANES), f32)
    in_south, in_north = inside("gy", True), inside("gy", False)
    for t in range(8):
        for f in range(4):
            if 2 <= t < 6:
                block = flux[t - 2, f].astype(f32)
            else:
                got, half = (yn_r, t) if t < 2 else (ys_r, t - 6)
                at = YF + (half * 4 + f) * NX
                block = got[at : at + NX, :].astype(f32) * (in_south if t < 2 else in_north)
            rim[t, f, 0:8, :] = zero
            rim[t, f, 8 : 8 + NX, :] = block
            rim[t, f, 8 + NX : 16 + NX, :] = zero

    def blocks(tile, row):
        code = jnp.broadcast_to(column(row), (NX, LANES))
        picked = [code == float(k) for k in range(9)]
        result = []
        for f in range(4):
            block = jnp.zeros((NX, LANES), f32)
            for k in range(9):
                x0 = 7 + k // 3
                block = jnp.where(picked[k], rim[tile + 2 + k % 3 - 1, f, x0 : x0 + NX, :], block)
            result.append(block)
        return result

    for t in range(NT):
        for s in range(2):
            row = 2 * t + s
            for f, block in enumerate(blocks(t, table[row : row + 1, 0:NX])):
                blk[row, f * NX : (f + 1) * NX, :] = block

    lane = lane_ids((NX, LANES))
    edges = [jnp.zeros((NX, LANES), f32) for f in range(4)]
    for got, tile, row, at in ((yn_r, -1, 6, 125), (ys_r, NT, 0, 0)):
        codes = got[YC : YC + 16, :].astype(f32)
        picked = [blocks(tile, codes[row + s : row + s + 1, 0:NX]) for s in range(2)]
        for d in range(3):
            weight = [
                got[YW + (d * 2 + s) * NX : YW + (d * 2 + s + 1) * NX, :].astype(f32) for s in range(2)
            ]
            for f in range(4):
                total = jnp.sum(weight[0] * picked[0][f] + weight[1] * picked[1][f], axis=1, keepdims=True)
                edges[f] = jnp.where(lane == at + d, total, edges[f])
    for f in range(4):
        part[4 * LANES + f * NX : 4 * LANES + (f + 1) * NX, :] = edges[f]

    for t in range(NT):
        for half in range(2):
            copies[2 * t + half].wait()

            def pair(i, _, t=t):
                x = 2 * i
                rows = [
                    jnp.concatenate([blk[2 * t + s, pl.ds(x + j, 8, stride=NX), :] for j in range(2)], axis=0)
                    for s in range(2)
                ]
                weights = jnp.concatenate(
                    [jnp.concatenate([wbuf[t, x + j, s] for s in range(2)], axis=1) for j in range(2)], axis=0
                )
                product = lax.dot_general(
                    jnp.concatenate(rows, axis=1).astype(bf16),
                    weights,
                    (((1,), (1,)), ((), ())),
                    preferred_element_type=f32,
                )
                for j in range(2):
                    block = product[8 * j : 8 * j + 4, j * LANES : (j + 1) * LANES]
                    part[pl.ds(t * LANES + x + j, 4, stride=NX), :] = block
                return 0

            lax.fori_loop(half * 8, half * 8 + 8, pair, 0, unroll=8)
        for side, x in enumerate((0, NX - 1)):
            for s in range(2):
                wedge[side, t, s] = wbuf[t, x, s]


def rim_kernel(first_part, wedge, yn_r, ys_r, xe_r, xw_r, table, part, send, z2u, z2d):
    part[...] = first_part[...]
    near = [got[XF : XF + 32, :].astype(f32) * inside("gx", side == 0) for side, got in enumerate((xe_r, xw_r))]

    def blocks(side, tile, codes, row):
        x = 0 if side == 0 else NX - 1
        code = jnp.broadcast_to(codes[row : row + 1, x : x + 1], (4, LANES))
        block = jnp.zeros((4, LANES), f32)
        for k in range(3):
            at = (tile + 1 + k) * 4
            block = jnp.where(code == float(6 * side + k), near[side][at : at + 4], block)
        return block

    own_codes = table[...]
    gap = jnp.zeros((4, LANES), f32)
    for t in range(NT):
        rows = [
            jnp.concatenate([blocks(0, t, own_codes, 2 * t + s), gap, blocks(1, t, own_codes, 2 * t + s), gap], axis=0)
            for s in range(2)
        ]
        weights = jnp.concatenate(
            [jnp.concatenate([wedge[side, t, s] for s in range(2)], axis=1) for side in range(2)], axis=0
        )
        product = lax.dot_general(
            jnp.concatenate(rows, axis=1).astype(bf16), weights, (((1,), (1,)), ((), ())), preferred_element_type=f32
        )
        for side, x in enumerate((0, NX - 1)):
            part[pl.ds(t * LANES + x, 4, stride=NX), :] += product[8 * side : 8 * side + 4, side * LANES : (side + 1) * LANES]
    lane = lane_ids((4, LANES))
    for side, x in enumerate((0, NX - 1)):
        added = jnp.zeros((4, LANES), f32)
        for got, tile, row, at in ((yn_r, -1, 6, 125), (ys_r, NT, 0, 0)):
            codes = got[YC : YC + 16, :].astype(f32)
            picked = [blocks(side, tile, codes, row + s) for s in range(2)]
            for d in range(3):
                total = jnp.zeros((4, LANES), f32)
                for s in range(2):
                    first = YW + (d * 2 + s) * NX
                    weight = got[first : first + NX, :].astype(f32)[x : x + 1]
                    total += weight * picked[s]
                added = jnp.where(lane == at + d, jnp.sum(total, axis=1, keepdims=True), added)
        part[pl.ds(4 * LANES + x, 4, stride=NX), :] += added

    send[0 : 4 * LANES, :] = part[0 : 4 * LANES, :].astype(bf16)
    turned = part[4 * LANES : 5 * LANES, :].T
    send[4 * LANES : CROWS, :] = jnp.concatenate([turned[0:8], turned[LANES - 8 :]], axis=0).astype(bf16)
    for target, first in ((z2u, 0), (z2d, 32)):
        for side, got in enumerate((xw_r, xe_r)):
            for c in range(5):
                base = c * XPLANE
                if first == 0:
                    heat = got[base : base + 16, :].astype(f32)[0:8]
                    salt = got[base + 32 : base + 48, :].astype(f32)[8:16]
                else:
                    heat = got[base + 32 : base + 48, :].astype(f32)[0:8]
                    salt = got[base + 64 : base + 80, :].astype(f32)[8:16]
                at = (side * 5 + c) * 32
                target[at : at + 16, :] = jnp.concatenate([heat, salt], axis=0).astype(bf16)
                target[at + 16 : at + 32, :] = got[base + 80 : base + 96, :]
        target[320:352, :] = yn_r[YT : YT + NX, :]
        target[352:384, :] = ys_r[YT : YT + NX, :]


def flux_kernel(part, up_r, down_r, across_r, mask, ext, de, dw, rows_s):
    got = [ref[4 * LANES : CROWS, :].astype(f32) for ref in (up_r, down_r, across_r)]
    turned = got[0] + got[1] + got[2]
    halo = jnp.concatenate([turned[0:8], jnp.zeros((LANES - 16, LANES), f32), turned[8:16]], axis=0).T
    for c in range(5):
        for f in range(4):
            at = c * LANES + f * NX
            total = part[at : at + NX, :]
            if c < 4:
                for ref in (up_r, down_r, across_r):
                    total = total + ref[at : at + NX, :].astype(f32)
            else:
                total = total + halo[f * NX : (f + 1) * NX]
            total = total * mask[c, OWN, :]
            ext[f, :, c * LANES : (c + 1) * LANES] = total
            rows_s[0, c * 16 + f * 4 : c * 16 + f * 4 + 4, :] = total[0:4]
            rows_s[1, c * 16 + f * 4 : c * 16 + f * 4 + 4, :] = total[NX - 4 : NX]
    dw[...] = rows_s[0].astype(bf16)
    de[...] = rows_s[1].astype(bf16)


def lane_next(value, lane):
    rolled = pltpu.roll(value, LANES - 1, 2)
    return jnp.where(lane == LANES - 1, jnp.concatenate([rolled[1:], rolled[:1]], axis=0), rolled)


def lane_prev(value, lane):
    rolled = pltpu.roll(value, 1, 2)
    return jnp.where(lane == 0, jnp.concatenate([rolled[-1:], rolled[:-1]], axis=0), rolled)


OWN, WEST, EAST = slice(12, 44), slice(8, 12), slice(44, 48)
PLANE = (5, 56, LANES)


def advance(src, at, vel, v, mask, coef, l, rows):
    level = lax.axis_index("sec") * NL + l - 3
    up = jnp.where(level > 0, VERTICAL, 0.0).astype(f32)
    down = jnp.where(level < NL * lax.axis_size("sec") - 1, VERTICAL, 0.0).astype(f32)
    r = rows.start
    lane = lane_ids((5, 8, LANES))
    m = mask[:, rows, :]
    a = ADVECTION * vel[0, v, :, rows, :]
    b = ADVECTION * vel[1, v, :, rows, :]
    base = DIFFUSION * m
    centre = coef[:, rows, :] - (up + down) * m
    mu, md = up * m, down * m
    results = []
    for c in range(2):
        g = src[c, at, :, rows, :]
        new = centre * g
        new += (base - a) * src[c, at, :, r + 1 : r + 9, :] + (base + a) * src[c, at, :, r - 1 : r + 7, :]
        new += (base - b) * lane_next(g, lane) + (base + b) * lane_prev(g, lane)
        new += mu * src[c, at - 1, :, rows, :] + md * src[c, at + 1, :, rows, :]
        results.append(new)
    return results


def sweep(src, dst, vel, mask, coef, levels, src_at, dst_at, vel_at):
    def one_level(l, _):
        for r in range(8, 48, 8):
            rows = slice(r, r + 8)
            for c, value in enumerate(advance(src, l - src_at, vel, l - vel_at, mask, coef, l, rows)):
                dst[c, l - dst_at, :, rows, :] = value
        return 0

    lax.fori_loop(levels[0], levels[1], one_level, 0)


def finish(src, out, vel, mask, coef, levels, src_at, out_at, vel_at, before, before_at):
    def one_level(l, _):
        for r in range(12, 44, 8):
            rows = slice(r, r + 8)
            for c, value in enumerate(advance(src, l - src_at, vel, l - vel_at, mask, coef, l, rows)):
                for col in range(4):
                    at = (slice(r - 12, r - 4), slice(col * LANES, (col + 1) * LANES))
                    kept = before[(c, l - before_at) + at]
                    out[(c, l - out_at) + at] = jnp.where(mask[col, rows, :] > 0.0, value[col], kept)
        return 0

    lax.fori_loop(levels[0], levels[1], one_level, 0)


def middle_kernel(
    tr_h, cu_h, yn_r, ys_r, xe_r, xw_r, table, after, after_zu, after_zd, g0, vel, g1, g2, mask, coef, done, tr, cu, xs, sems
):
    copies = [pltpu.make_async_copy(tr_h, tr, sems.at[0]), pltpu.make_async_copy(cu_h, cu, sems.at[1])]
    start(*copies)
    south, north = field_packs(yn_r), field_packs(ys_r)
    low = lane_ids((NX, LANES)) < 64
    xs[0] = xw_r[0:XF, :].astype(f32)
    xs[1] = xe_r[0:XF, :].astype(f32)

    def edge_col(plane):
        return jnp.where(low, unpack_north(north, plane), unpack_south(south, plane))

    for c in range(4):
        mask[c, OWN, :] = jnp.broadcast_to(column(table[LAND + c : LAND + c + 1, 0:NX]), (NX, LANES))
    mask[4, OWN, :] = edge_col(MASK_PLANE) * jnp.where(low, inside("gy", False), inside("gy", True))
    in_west, in_east = inside("gx", True), inside("gx", False)
    for c in range(5):
        at = c * XPLANE + MASK_PLANE * 4
        mask[c, EAST, :] = xs[0, at : at + 4, :] * in_east
        mask[c, WEST, :] = xs[1, at : at + 4, :] * in_west
    lane = lane_ids((5, 8, LANES))
    for r in range(8, 48, 8):
        rows, m = slice(r, r + 8), mask[:, r : r + 8, :]
        around = mask[:, r + 1 : r + 9, :] + mask[:, r - 1 : r + 7, :] + lane_next(m, lane) + lane_prev(m, lane)
        coef[:, rows, :] = m * (1.0 - DIFFUSION * around)

    wait(*copies)
    for plane, (kind, c, level) in enumerate(PLANES):
        source, target = (tr, g0) if kind == "t" else (cu, vel)
        for col in range(5):
            if col < 4:
                body = source[c, level, :, col * LANES : (col + 1) * LANES]
            else:
                body = edge_col(plane)
            target[c, level, col, OWN, :] = body * mask[col, OWN, :]
            at = col * XPLANE + plane * 4
            target[c, level, col, EAST, :] = xs[0, at : at + 4, :] * mask[col, EAST, :]
            target[c, level, col, WEST, :] = xs[1, at : at + 4, :] * mask[col, WEST, :]

    sweep(g0, g1, vel, mask, coef, (4, 12), 3, 4, 3)
    sweep(g1, g2, vel, mask, coef, (5, 11), 4, 5, 3)
    finish(g2, done, vel, mask, coef, (6, 10), 5, 6, 3, tr, 3)


def outer_kernel(
    tr, g0, vel, g1, g2, mask, coef, zu_r, zd_r, z2u_r, z2d_r, ext, after, done, ocean_flux,
    s0, s1, s2, sv, before, sems,
):
    copies = [
        pltpu.make_async_copy(tr.at[:, pl.ds(0, 3)], before.at[0], sems.at[0]),
        pltpu.make_async_copy(tr.at[:, pl.ds(NL - 3, 3)], before.at[1], sems.at[1]),
        pltpu.make_async_copy(ext.at[:, :, pl.ds(0, 512)], ocean_flux, sems.at[2]),
    ]
    start(*copies)
    low = lane_ids((NX, LANES)) < 64
    for c in range(2):
        for k in range(2):
            s0[0, c, 3 + k] = g0[c, k]
            s0[1, c, k] = g0[c, 8 + k]
            s1[0, c, 3 + k] = g1[c, k]
            s1[1, c, k] = g1[c, 6 + k]
            s2[0, c, 3 + k] = g2[c, k]
            s2[1, c, k] = g2[c, 4 + k]
        for k in range(3):
            sv[0, c, 2 + k] = vel[c, k]
            sv[1, c, k] = vel[c, 7 + k]
    for got, z, face in ((z2d_r, zd_r, 0), (z2u_r, zu_r, 1)):
        z_south = (got[320:352, :].astype(f32),)
        z_north = (got[352:384, :].astype(f32),)
        halo = [[got[(s * 5 + c) * 32 : (s * 5 + c + 1) * 32, :].astype(f32) for c in range(5)] for s in (0, 1)]

        def put(target, body, near, plane, first):
            for col in range(4):
                target[col, OWN, :] = body[:, col * LANES : (col + 1) * LANES].astype(f32) * mask[col, OWN, :]
            if not near:
                return
            col4 = jnp.where(low, unpack_north(z_north, plane), unpack_south(z_south, plane))
            target[4, OWN, :] = col4 * mask[4, OWN, :]
            for col in range(5):
                target[col, EAST, :] = halo[0][col][first : first + 4] * mask[col, EAST, :]
                target[col, WEST, :] = halo[1][col][first : first + 4] * mask[col, WEST, :]

        for c in range(2):
            for k in range(3):
                near = k > 0 if face == 0 else k < 2
                level = 7 + k if face == 0 else k
                first = c * 8 + (k - 1 if face == 0 else k) * 4
                target = s0.at[face, c, k if face == 0 else 2 + k]
                put(target, z[c * 3 + k], near, PLANE_AT[("t", c, level)] if near else 0, first)
            for k in range(2):
                near = k == (1 if face == 0 else 0)
                level = 9 if face == 0 else 0
                first = 16 + c * 8 + (4 if face == 0 else 0)
                target = sv.at[face, c, k if face == 0 else 3 + k]
                put(target, z[6 + c * 2 + k], near, PLANE_AT[("c", c, level)], first)

    wait(copies[0], copies[1])
    for face in range(2):
        a, b, c, v = s0.at[face], s1.at[face], s2.at[face], sv.at[face]
        at0, at1, at2, atv = (0, 1, 2, 1) if face == 0 else (11, 10, 9, 10)
        last = (3, 6) if face == 0 else (10, 13)
        sweep(a, b, v, mask, coef, (1, 4) if face == 0 else (12, 15), at0, at1, atv)
        sweep(b, c, v, mask, coef, (2, 5) if face == 0 else (11, 14), at1, at2, atv)
        finish(c, done.at[face], v, mask, coef, last, at2, last[0], atv, before.at[face], last[0])
    wait(copies[2])


def surface_kernel(
    tr, g0, vel, g1, g2, mask, coef, ext, de_r, dw_r, middle, outer, out, s0, s1, s2, sv, before, top, sems
):
    sec = lax.axis_index("sec")
    writes = [
        pltpu.make_async_copy(outer.at[1], out.at[:, pl.ds(7, 3)], sems.at[0]),
        pltpu.make_async_copy(middle.at[:, pl.ds(1, 3)], out.at[:, pl.ds(4, 3)], sems.at[1]),
    ]
    start(*writes)

    @pl.when(sec != 0)
    def _():
        rest = [
            pltpu.make_async_copy(outer.at[0], out.at[:, pl.ds(0, 3)], sems.at[2]),
            pltpu.make_async_copy(middle.at[:, pl.ds(0, 1)], out.at[:, pl.ds(3, 1)], sems.at[3]),
        ]
        start(*rest)
        wait(*rest)

    @pl.when(sec == 0)
    def _():
        read = pltpu.make_async_copy(tr.at[:, pl.ds(0, 4)], before, sems.at[2])
        read.start()
        zero = jnp.zeros(PLANE, f32)
        for c in range(2):
            for target in (s0, s1, s2):
                target[c, 0] = zero
            for k in range(3):
                s0[c, 1 + k] = g0[c, k]
            for k in range(2):
                s1[c, 3 + k] = g1[c, 1 + k]
                s2[c, 4 + k] = g2[c, 1 + k]
            for k in range(4):
                sv[c, k] = vel[c, k]
        dw_f, de_f = dw_r[...].astype(f32), de_r[...].astype(f32)
        for f, (ref, at, gain) in enumerate(
            ((sv, (0, 0), WIND_GAIN), (sv, (1, 0), WIND_GAIN), (s0, (0, 1), HEAT_GAIN), (s0, (1, 1), -SALT_GAIN))
        ):
            for c in range(5):
                r = c * 16 + f * 4
                body = ext[f, :, c * LANES : (c + 1) * LANES]
                for rows, value in ((OWN, body), (EAST, dw_f[r : r + 4]), (WEST, de_f[r : r + 4])):
                    ref[at + (c, rows)] += gain * value * mask[c, rows, :]
        read.wait()
        sweep(s0, s1, sv, mask, coef, (3, 5), 2, 2, 3)
        sweep(s1, s2, sv, mask, coef, (3, 6), 2, 2, 3)
        finish(s2, top, sv, mask, coef, (3, 7), 2, 3, 3, before, 3)
        write = pltpu.make_async_copy(top, out.at[:, pl.ds(0, 4)], sems.at[3])
        write.start()
        write.wait()

    wait(*writes)


ANY = pl.BlockSpec(memory_space=pl.ANY)
HBM = pl.BlockSpec(memory_space=pltpu.HBM)
VMEM = pl.BlockSpec(memory_space=pltpu.VMEM)


def hbm(value):
    return pltpu.with_memory_space_constraint(value, pltpu.HBM)


def call(kernel, in_specs, outs, scratch, name, bytes_accessed, out_specs=None):
    return pl.pallas_call(
        kernel,
        out_shape=[jax.ShapeDtypeStruct(shape, dtype) for shape, dtype in outs],
        in_specs=in_specs,
        out_specs=out_specs or [VMEM] * len(outs),
        scratch_shapes=scratch,
        compiler_params=pltpu.CompilerParams(vmem_limit_bytes=VMEM_BYTES),
        cost_estimate=pl.CostEstimate(flops=0, bytes_accessed=bytes_accessed, transcendentals=0),
        name=name,
    )


def shifted(value, axis, step):
    count = lax.axis_size(axis)
    return lax.ppermute(value, axis, [(i, (i + step) % count) for i in range(count)])


def on_device(air_surface, remap_weights, sources, live_count, land_sea, tracers, currents):
    src = hbm(jnp.transpose(sources[:, :, 0, :], (1, 2, 0)))
    live = hbm(jnp.transpose(live_count, (1, 2, 0)))
    land = hbm(jnp.transpose(land_sea, (1, 0)))
    dma = pltpu.SemaphoreType.DMA

    yn, ys, flux, table = call(
        pack_y_kernel,
        [HBM] * 7,
        [((YROWS, LANES), bf16), ((YROWS, LANES), bf16), ((NT, 4, NX, LANES), bf16), ((16, LANES), f32)],
        [
            pltpu.VMEM((NT, 2, NX), jnp.int32),
            pltpu.VMEM((NT, 1, NX), jnp.int32),
            pltpu.VMEM((NT, NX), jnp.int32),
            pltpu.VMEM((NT, 5, NX, LANES), f32),
            pltpu.VMEM((NX, 2, 16, LANES), bf16),
            pltpu.VMEM((NX, 2, 16, LANES), bf16),
            pltpu.VMEM((192, LANES), f32),
            pltpu.VMEM((2, 2, 2, NL, NX, LANES), f32),
            dma((13,)),
        ],
        "pack_y",
        6_000_000,
    )(hbm(air_surface), src, live, land, hbm(remap_weights), hbm(tracers), hbm(currents))
    yn_r = shifted(yn, "gy", 1)
    ys_r = shifted(ys, "gy", -1)

    zu, zd = call(
        pack_z_kernel,
        [ANY, ANY, ANY],
        [((10, NX, 512), bf16)] * 2,
        [pltpu.VMEM((2, 2, 3, NX, 512), f32), pltpu.VMEM((2, 2, 2, NX, 512), f32), dma((4,))],
        "pack_z",
        3_000_000,
    )(tracers, currents, table)
    zu_r = shifted(zu, "sec", -1)
    zd_r = shifted(zd, "sec", 1)

    xe, xw = call(
        pack_x_kernel,
        [VMEM, VMEM, VMEM, VMEM, ANY, ANY],
        [((XROWS, LANES), bf16)] * 2,
        [pltpu.VMEM((XROWS, LANES), f32), pltpu.VMEM((2, 2, 2, NL, 8, 512), f32), dma((4,))],
        "pack_x",
        3_000_000,
    )(flux, yn_r, ys_r, table, tracers, currents)
    xe_r = shifted(xe, "gx", 1)
    xw_r = shifted(xw, "gx", -1)

    first_part, wedge = call(
        remap_kernel,
        [VMEM] * 4 + [ANY] * 2,
        [((5 * LANES, LANES), f32), ((2, NT, 2, LANES, LANES), bf16)],
        [
            pltpu.VMEM((8, 4, 48, LANES), f32),
            pltpu.VMEM((2 * NT, 2 * LANES, LANES), f32),
            pltpu.VMEM((NT, NX, 2, LANES, LANES), bf16),
            dma((8,)),
        ],
        "remap",
        18_000_000,
    )(flux, yn_r, ys_r, table, remap_weights, xe)
    part, send, z2u, z2d = call(
        rim_kernel,
        [VMEM] * 7,
        [((5 * LANES, LANES), f32), ((CROWS, LANES), bf16), ((ZROWS, LANES), bf16), ((ZROWS, LANES), bf16)],
        [],
        "rim",
        4_000_000,
    )(first_part, wedge, yn_r, ys_r, xe_r, xw_r, table)
    up_r = shifted(send, "sec", -1)
    down_r = shifted(send, "sec", 1)
    across_r = shifted(send, "sec", 2)
    z2u_r = shifted(z2u, "sec", -1)
    z2d_r = shifted(z2d, "sec", 1)

    plane = (5, 56, LANES)
    g0, vel, g1, g2, mask, coef, middle = call(
        middle_kernel,
        [ANY, ANY] + [VMEM] * 5 + [ANY] * 3,
        [
            ((2, NL) + plane, f32),
            ((2, NL) + plane, f32),
            ((2, NL - 2) + plane, f32),
            ((2, NL - 4) + plane, f32),
            (plane, f32),
            (plane, f32),
            ((2, NL - 6, NX, 512), f32),
        ],
        [
            pltpu.VMEM((2, NL, NX, 512), f32),
            pltpu.VMEM((2, NL, NX, 512), f32),
            pltpu.VMEM((2, XF, LANES), f32),
            dma((2,)),
        ],
        "middle",
        20_000_000,
    )(tracers, currents, yn_r, ys_r, xe_r, xw_r, table, send, zu_r, zd_r)

    ext, de, dw = call(
        flux_kernel,
        [VMEM] * 5,
        [((4, NX, 5 * LANES), f32), ((80, LANES), bf16), ((80, LANES), bf16)],
        [pltpu.VMEM((2, 80, LANES), f32)],
        "flux_sum",
        3_000_000,
    )(part, up_r, down_r, across_r, mask)
    de_r = shifted(de, "gx", 1)
    dw_r = shifted(dw, "gx", -1)

    outer, ocean_flux = call(
        outer_kernel,
        [ANY] + [VMEM] * 11 + [ANY],
        [((2, 2, 3, NX, 512), f32), ((4, NX, 512), f32)],
        [
            pltpu.VMEM((2, 2, 5) + plane, f32),
            pltpu.VMEM((2, 2, 5) + plane, f32),
            pltpu.VMEM((2, 2, 5) + plane, f32),
            pltpu.VMEM((2, 2, 5) + plane, f32),
            pltpu.VMEM((2, 2, 3, NX, 512), f32),
            dma((3,)),
        ],
        "outer",
        18_000_000,
        [VMEM, HBM],
    )(tracers, g0, vel, g1, g2, mask, coef, zu_r, zd_r, z2u_r, z2d_r, ext, de)

    (tracers_out,) = call(
        surface_kernel,
        [ANY] + [VMEM] * 11,
        [((2, NL, NX, 512), f32)],
        [
            pltpu.VMEM((2, 4) + plane, f32),
            pltpu.VMEM((2, 5) + plane, f32),
            pltpu.VMEM((2, 6) + plane, f32),
            pltpu.VMEM((2, 4) + plane, f32),
            pltpu.VMEM((2, 4, NX, 512), f32),
            pltpu.VMEM((2, 4, NX, 512), f32),
            dma((4,)),
        ],
        "surface",
        8_000_000,
        [HBM],
    )(tracers, g0, vel, g1, g2, mask, coef, ext, de_r, dw_r, middle, outer)
    return (tracers_out, ocean_flux)


def solution(mesh):
    return jax.shard_map(
        on_device,
        mesh=mesh,
        in_specs=(
            P(None, "gx", "gy", "sec", None),
            P("gx", "gy", "sec", None, None, None),
            P("gx", "gy", "sec", None),
            P("gx", "gy", "sec"),
            P("gx", "gy"),
            P(None, "sec", "gx", "gy"),
            P(None, "sec", "gx", "gy"),
        ),
        out_specs=(P(None, "sec", "gx", "gy"), P(None, "gx", "gy")),
        check_vma=False,
    )
```

time: 79 us -> 48.1 us (0.61)
  the two profiles are of different devices: /device:TPU:152 before, /device:TPU:8 now
where the time goes in v2:
time: 48.1 us
  starting transfers between devices  23.1 us (48%)
  Pallas kernels  20 us (42%)
  waiting for transfers between devices  4 us (8%)
  between operations  0.94 us (2%)
    ppermute x13, starting transfers between devices, shifted(): lax.ppermute(value, axis, [(i, (i + step) % count) for i in range(count)])  23.1 us
    pallas_call x1, Pallas kernels, on_device(): call(middle_kernel, [ANY, ANY] + [VMEM] * 5 + [ANY] * 3, [((2, NL) + plan...  4.5 us
    pallas_call x1, Pallas kernels, on_device(): call(remap_kernel, [VMEM] * 4 + [ANY] * 2, [((5 * LANES, LANES), f32), ((...  4.4 us
    pallas_call x1, Pallas kernels, on_device(): call(outer_kernel, [ANY] + [VMEM] * 11 + [ANY], [((2, 2, 3, NX, 512), f32...  4.37 us
    ppermute x13, waiting for transfers between devices, shifted(): lax.ppermute(value, axis, [(i, (i + step) % count) for i in range(count)])  4 us
    pallas_call x1, Pallas kernels, on_device(): call(surface_kernel, [ANY] + [VMEM] * 11, [((2, NL, NX, 512), f32)], [plt...  3 us
    pallas_call x1, Pallas kernels, on_device(): call(pack_y_kernel, [HBM] * 7, [((YROWS, LANES), bf16), ((YROWS, LANES),...  2.39 us
  transfers between devices with their start and end apart: 13, of which 3 were waited for; matrix products, arithmetic and copies ran while one was open for 0% of the time, Pallas kernels for 30%

profile of v2, /device:TPU:8, one launch (start us, length us, event | category | flops | bytes accessed | tf_op | source)
XLA Modules:
  0.0 48.1 jit_solution(10104552243977763078)
XLA Ops:
  0.6 0.0 slice-start
  0.6 0.0 copy-start
  0.7 0.0 copy-start.1
  0.7 0.0 slice-start.1
  0.7 2.4 %pack_y.1 = (bf16[528,128]{1,0:T(8,128)(2,1)S(1)}, bf16[528,128]{1,0:T(8,128)(2,1)S(1)}, bf16[4,4,32,128]{3,2,1,0:T(8,128)(2,1)S(1)}, f32[16,128]{1,0:T(8,128)S(1)}) custom-call(f32[5,32,4,1,128]{4,3,2,1,0:T(1,128)} %air.1, s32[4,2,32]{2,1,0:T(2,128)} %bitcast.7, s32[4,1,32]{2,1,0:T(1,128)} %bitcast.8, s32[4,32]{1,0:T(4,128)} %bitcast.9, ...), custom_call_target="tpu_custom_call" | custom-call | bytes 6000000 | tf_op jit(solution)/shard_map/pack_y/pallas_call | solution.py:635
  3.1 0.1 collective-permute-start
  3.2 5.8 %collective-permute-start.1 = (bf16[528,128]{1,0:T(8,128)(2,1)S(1)}, bf16[528,128]{1,0:T(8,128)(2,1)S(1)}, u32[]{:S(2)}, u32[]{:S(2)}) collective-permute-start(bf16[528,128]{1,0:T(8,128)(2,1)S(1)} %get-tuple-element.29), channel_id=1, source_target_pairs={{0,7},{1,0},{2,1},{3,2},{4,3},{5,4},{6,5},{7,6},{8,15},{9,8},{10,9... | collective-permute-start | bytes 405512 | tf_op jit(solution)/shard_map/ppermute | solution.py:626
  9.0 0.0 copy-done
  9.0 0.0 copy-done.1
  9.0 0.3 pack_z.1
  9.3 2.8 %collective-permute-start.4 = (bf16[10,32,512]{2,1,0:T(8,128)(2,1)S(1)}, bf16[10,32,512]{2,1,0:T(8,128)(2,1)S(1)}, u32[]{:S(2)}, u32[]{:S(2)}) collective-permute-start(bf16[10,32,512]{2,1,0:T(8,128)(2,1)S(1)} %get-tuple-element.37), channel_id=1, source_target_pairs={{0,192},{64,0},{128,64},{192,128},{1,193},{65,1},{129,65},{193,129... | collective-permute-start | bytes 983048 | tf_op jit(solution)/shard_map/ppermute | solution.py:626
  12.2 0.0 collective-permute-start.5
  12.2 0.0 collective-permute-done.yn_r
  12.2 0.8 %collective-permute-done.1.ys_r = bf16[528,128]{1,0:T(8,128)(2,1)S(1)} collective-permute-done((bf16[528,128]{1,0:T(8,128)(2,1)S(1)}, bf16[528,128]{1,0:T(8,128)(2,1)S(1)}, u32[]{:S(2)}, u32[]{:S(2)}) %collective-permute-start.1) | collective-permute-done | bytes 135200 | tf_op jit(solution)/shard_map/ppermute | solution.py:626
  13.0 0.5 %pack_x.1 = (bf16[912,128]{1,0:T(8,128)(2,1)S(1)}, bf16[912,128]{1,0:T(8,128)(2,1)S(1)}) custom-call(bf16[4,4,32,128]{3,2,1,0:T(8,128)(2,1)S(1)} %get-tuple-element.30.flux, bf16[528,128]{1,0:T(8,128)(2,1)S(1)} %collective-permute-done.yn_r, bf16[528,128]{1,0:T(8,128)(2,1)S(1)} %collective-permute-done.1.ys_r, f32[16,128]{1,0:T(8,128)S(1)} %get-tuple-element.31.table.after, ...), custom_call_target="tpu_custom_call" | custom-call | bytes 3000000 | tf_op jit(solution)/shard_map/pack_x/pallas_call | solution.py:667
  13.5 0.5 %collective-permute-start.3 = (bf16[912,128]{1,0:T(8,128)(2,1)S(1)}, bf16[912,128]{1,0:T(8,128)(2,1)S(1)}, u32[]{:S(2)}, u32[]{:S(2)}) collective-permute-start(bf16[912,128]{1,0:T(8,128)(2,1)S(1)} %get-tuple-element.33), channel_id=1, source_target_pairs={{0,56},{8,0},{16,8},{24,16},{32,24},{40,32},{48,40},{56,48},{1,57}... | collective-permute-start | bytes 700424 | tf_op jit(solution)/shard_map/ppermute | solution.py:626
  14.0 1.6 %collective-permute-start.2 = (bf16[912,128]{1,0:T(8,128)(2,1)S(1)}, bf16[912,128]{1,0:T(8,128)(2,1)S(1)}, u32[]{:S(2)}, u32[]{:S(2)}) collective-permute-start(bf16[912,128]{1,0:T(8,128)(2,1)S(1)} %get-tuple-element.32.after_x), channel_id=1, source_target_pairs={{0,8},{8,16},{16,24},{24,32},{32,40},{40,48},{48,56},{56,0},{1,9},... | collective-permute-start | bytes 700424 | tf_op jit(solution)/shard_map/ppermute | solution.py:626
  15.6 0.0 slice-done
  15.6 0.0 slice-done.1
  15.6 4.4 %remap.1 = (f32[640,128]{1,0:T(8,128)S(1)}, bf16[2,4,2,128,128]{4,3,2,1,0:T(8,128)(2,1)S(1)}) custom-call(bf16[4,4,32,128]{3,2,1,0:T(8,128)(2,1)S(1)} %get-tuple-element.30.flux, bf16[528,128]{1,0:T(8,128)(2,1)S(1)} %collective-permute-done.yn_r, bf16[528,128]{1,0:T(8,128)(2,1)S(1)} %collective-permute-done.1.ys_r, ...), custom_call_target="tpu_custom_call" | custom-call | bytes 18000000 | tf_op jit(solution)/shard_map/remap/pallas_call | solution.py:678
  20.0 0.1 collective-permute-done.3.xw_r
  20.1 3.1 %collective-permute-done.2.xe_r = bf16[912,128]{1,0:T(8,128)(2,1)S(1)} collective-permute-done((bf16[912,128]{1,0:T(8,128)(2,1)S(1)}, bf16[912,128]{1,0:T(8,128)(2,1)S(1)}, u32[]{:S(2)}, u32[]{:S(2)}) %collective-permute-start.2) | collective-permute-done | bytes 233504 | tf_op jit(solution)/shard_map/ppermute | solution.py:626
  23.2 0.3 rim.1
  23.5 3.1 %collective-permute-start.8 = (bf16[528,128]{1,0:T(8,128)(2,1)S(1)}, bf16[528,128]{1,0:T(8,128)(2,1)S(1)}, u32[]{:S(2)}, u32[]{:S(2)}) collective-permute-start(bf16[528,128]{1,0:T(8,128)(2,1)S(1)} %get-tuple-element.36.after), channel_id=1, source_target_pairs={{0,128},{64,192},{128,0},{192,64},{1,129},{65,193},{129,1},{193,65... | collective-permute-start | bytes 405512 | tf_op jit(solution)/shard_map/ppermute | solution.py:626
  26.6 0.6 %collective-permute-start.7 = (bf16[528,128]{1,0:T(8,128)(2,1)S(1)}, bf16[528,128]{1,0:T(8,128)(2,1)S(1)}, u32[]{:S(2)}, u32[]{:S(2)}) collective-permute-start(bf16[528,128]{1,0:T(8,128)(2,1)S(1)} %get-tuple-element.36.after), channel_id=1, source_target_pairs={{0,64},{64,128},{128,192},{192,0},{1,65},{65,129},{129,193},{193,1... | collective-permute-start | bytes 405512 | tf_op jit(solution)/shard_map/ppermute | solution.py:626
  27.2 2.6 %collective-permute-start.6 = (bf16[528,128]{1,0:T(8,128)(2,1)S(1)}, bf16[528,128]{1,0:T(8,128)(2,1)S(1)}, u32[]{:S(2)}, u32[]{:S(2)}) collective-permute-start(bf16[528,128]{1,0:T(8,128)(2,1)S(1)} %get-tuple-element.36.after), channel_id=1, source_target_pairs={{0,192},{64,0},{128,64},{192,128},{1,193},{65,1},{129,65},{193,129... | collective-permute-start | bytes 405512 | tf_op jit(solution)/shard_map/ppermute | solution.py:626
  29.9 0.0 collective-permute-done.4.after_zu.zu_r
  29.9 0.0 collective-permute-start.11
  29.9 0.0 collective-permute-done.5.after_zd.zd_r
  29.9 2.0 %collective-permute-start.12 = (bf16[384,128]{1,0:T(8,128)(2,1)S(1)}, bf16[384,128]{1,0:T(8,128)(2,1)S(1)}, u32[]{:S(2)}, u32[]{:S(2)}) collective-permute-start(bf16[384,128]{1,0:T(8,128)(2,1)S(1)} %get-tuple-element.51), channel_id=1, source_target_pairs={{0,64},{64,128},{128,192},{192,0},{1,65},{65,129},{129,193},{193,1... | collective-permute-start | bytes 294920 | tf_op jit(solution)/shard_map/ppermute | solution.py:626
  31.9 4.5 %middle.1 = (f32[2,10,5,56,128]{4,3,2,1,0:T(8,128)S(1)}, f32[2,10,5,56,128]{4,3,2,1,0:T(8,128)S(1)}, f32[2,8,5,56,128]{4,3,2,1,0:T(8,128)S(1)}, f32[2,6,5,56,128...) custom-call(f32[2,10,32,512]{3,2,1,0:T(8,128)S(1)} %copy-done, ...), custom_call_target="tpu_custom_call" | custom-call | bytes 20000000 | tf_op jit(solution)/shard_map/middle/pallas_call | solution.py:706
  36.4 0.0 collective-permute-done.8.across_r
  36.4 0.0 collective-permute-done.7.down_r
  36.4 0.0 collective-permute-done.6.up_r
  36.4 0.1 flux_sum.1
  36.6 3.9 %collective-permute-start.10 = (bf16[80,128]{1,0:T(8,128)(2,1)S(1)}, bf16[80,128]{1,0:T(8,128)(2,1)S(1)}, u32[]{:S(2)}, u32[]{:S(2)}) collective-permute-start(bf16[80,128]{1,0:T(8,128)(2,1)S(1)} %get-tuple-element.48), channel_id=1, source_target_pairs={{0,56},{8,0},{16,8},{24,16},{32,24},{40,32},{48,40},{56,48},{1,57}... | collective-permute-start | bytes 61448 | tf_op jit(solution)/shard_map/ppermute | solution.py:626
  40.5 0.0 collective-permute-start.9
  40.5 0.0 collective-permute-done.11.z2u_r
  40.5 0.0 collective-permute-done.12.z2d_r
  40.5 4.4 %outer.1 = (f32[2,2,3,32,512]{4,3,2,1,0:T(8,128)S(1)}, f32[4,32,512]{2,1,0:T(8,128)}) custom-call(f32[2,10,32,512]{3,2,1,0:T(8,128)S(1)} %copy-done, f32[2,10,5,56,128]{4,3,2,1,0:T(8,128)S(1)} %get-tuple-element.39.g0, f32[2,10,5,56,128]{4,3,2,1,0:T(8,128)S(1)} %get-tuple-element.40.vel, f32[2,8,5,56,128]{4,3,2,1,0:T(8,128)S(1)} %get-tuple-element.41.g1, ...), custom_call_target="tpu_custom_call" | custom-call | bytes 18000000 | tf_op jit(solution)/shard_map/outer/pallas_call | solution.py:739
  44.9 0.0 collective-permute-done.10.dw_r
  44.9 0.0 collective-permute-done.9.de_r
  44.9 3.0 %surface.1 = f32[2,10,32,512]{3,2,1,0:T(8,128)} custom-call(f32[2,10,32,512]{3,2,1,0:T(8,128)S(1)} %copy-done, f32[2,10,5,56,128]{4,3,2,1,0:T(8,128)S(1)} %get-tuple-element.39.g0, f32[2,10,5,56,128]{4,3,2,1,0:T(8,128)S(1)} %get-tuple-element.40.vel, f32[2,8,5,56,128]{4,3,2,1,0:T(8,128)S(1)} %get-tuple-element.41.g1, ...), custom_call_target="tpu_custom_call" | custom-call | bytes 8000000 | tf_op jit(solution)/shard_map/surface/pallas_call | solution.py:756
  (1 shorter events, 0.0 us)
Async XLA Ops:
  0.6 15.0 %slice-start = ((s8[8388608]{0:T(1024)(128)(4,1)}), s8[4194304]{0:T(1024)(128)(4,1)S(1)}, s32[]{:S(2)}) async-start(s8[8388608]{0:T(1024)(128)(4,1)} %bitcast.5), calls=%async_computation | async-start | bytes 8388608
  0.6 8.3 %copy-start = (f32[2,10,32,512]{3,2,1,0:T(8,128)S(1)}, f32[2,10,32,512]{3,2,1,0:T(8,128)}, u32[]{:S(2)}) copy-start(f32[2,10,32,512]{3,2,1,0:T(8,128)} %tr.9) | copy-start | bytes 3932164
  0.7 8.3 %copy-start.1 = (f32[2,10,32,512]{3,2,1,0:T(8,128)S(1)}, f32[2,10,32,512]{3,2,1,0:T(8,128)}, u32[]{:S(2)}) copy-start(f32[2,10,32,512]{3,2,1,0:T(8,128)} %cu_h.1) | copy-start | bytes 3932164
  0.7 14.9 %slice-start.1 = ((s8[8388608]{0:T(1024)(128)(4,1)}), s8[4194304]{0:T(1024)(128)(4,1)S(1)}, s32[]{:S(2)}) async-start(s8[8388608]{0:T(1024)(128)(4,1)} %bitcast.5), calls=%async_computation.1 | async-start | bytes 8388608
  3.1 9.1 %collective-permute-start = (bf16[528,128]{1,0:T(8,128)(2,1)S(1)}, bf16[528,128]{1,0:T(8,128)(2,1)S(1)}, u32[]{:S(2)}, u32[]{:S(2)}) collective-permute-start(bf16[528,128]{1,0:T(8,128)(2,1)S(1)} %get-tuple-element.28), channel_id=1, source_target_pairs={{0,1},{1,2},{2,3},{3,4},{4,5},{5,6},{6,7},{7,0},{8,9},{9,10},{10,1... | collective-permute-start | bytes 405512 | tf_op jit(solution)/shard_map/ppermute | solution.py:626
  3.2 9.8 %collective-permute-start.1 = (bf16[528,128]{1,0:T(8,128)(2,1)S(1)}, bf16[528,128]{1,0:T(8,128)(2,1)S(1)}, u32[]{:S(2)}, u32[]{:S(2)}) collective-permute-start(bf16[528,128]{1,0:T(8,128)(2,1)S(1)} %get-tuple-element.29), channel_id=1, source_target_pairs={{0,7},{1,0},{2,1},{3,2},{4,3},{5,4},{6,5},{7,6},{8,15},{9,8},{10,9... | collective-permute-start | bytes 405512 | tf_op jit(solution)/shard_map/ppermute | solution.py:626
  9.3 20.5 %collective-permute-start.4 = (bf16[10,32,512]{2,1,0:T(8,128)(2,1)S(1)}, bf16[10,32,512]{2,1,0:T(8,128)(2,1)S(1)}, u32[]{:S(2)}, u32[]{:S(2)}) collective-permute-start(bf16[10,32,512]{2,1,0:T(8,128)(2,1)S(1)} %get-tuple-element.37), channel_id=1, source_target_pairs={{0,192},{64,0},{128,64},{192,128},{1,193},{65,1},{129,65},{193,129... | collective-permute-start | bytes 983048 | tf_op jit(solution)/shard_map/ppermute | solution.py:626
  12.2 17.7 %collective-permute-start.5 = (bf16[10,32,512]{2,1,0:T(8,128)(2,1)S(1)}, bf16[10,32,512]{2,1,0:T(8,128)(2,1)S(1)}, u32[]{:S(2)}, u32[]{:S(2)}) collective-permute-start(bf16[10,32,512]{2,1,0:T(8,128)(2,1)S(1)} %get-tuple-element.38), channel_id=1, source_target_pairs={{0,64},{64,128},{128,192},{192,0},{1,65},{65,129},{129,193},{193,1... | collective-permute-start | bytes 983048 | tf_op jit(solution)/shard_map/ppermute | solution.py:626
  13.5 6.6 %collective-permute-start.3 = (bf16[912,128]{1,0:T(8,128)(2,1)S(1)}, bf16[912,128]{1,0:T(8,128)(2,1)S(1)}, u32[]{:S(2)}, u32[]{:S(2)}) collective-permute-start(bf16[912,128]{1,0:T(8,128)(2,1)S(1)} %get-tuple-element.33), channel_id=1, source_target_pairs={{0,56},{8,0},{16,8},{24,16},{32,24},{40,32},{48,40},{56,48},{1,57}... | collective-permute-start | bytes 700424 | tf_op jit(solution)/shard_map/ppermute | solution.py:626
  14.0 9.2 %collective-permute-start.2 = (bf16[912,128]{1,0:T(8,128)(2,1)S(1)}, bf16[912,128]{1,0:T(8,128)(2,1)S(1)}, u32[]{:S(2)}, u32[]{:S(2)}) collective-permute-start(bf16[912,128]{1,0:T(8,128)(2,1)S(1)} %get-tuple-element.32.after_x), channel_id=1, source_target_pairs={{0,8},{8,16},{16,24},{24,32},{32,40},{40,48},{48,56},{56,0},{1,9},... | collective-permute-start | bytes 700424 | tf_op jit(solution)/shard_map/ppermute | solution.py:626
  23.5 12.9 %collective-permute-start.8 = (bf16[528,128]{1,0:T(8,128)(2,1)S(1)}, bf16[528,128]{1,0:T(8,128)(2,1)S(1)}, u32[]{:S(2)}, u32[]{:S(2)}) collective-permute-start(bf16[528,128]{1,0:T(8,128)(2,1)S(1)} %get-tuple-element.36.after), channel_id=1, source_target_pairs={{0,128},{64,192},{128,0},{192,64},{1,129},{65,193},{129,1},{193,65... | collective-permute-start | bytes 405512 | tf_op jit(solution)/shard_map/ppermute | solution.py:626
  26.6 9.8 %collective-permute-start.7 = (bf16[528,128]{1,0:T(8,128)(2,1)S(1)}, bf16[528,128]{1,0:T(8,128)(2,1)S(1)}, u32[]{:S(2)}, u32[]{:S(2)}) collective-permute-start(bf16[528,128]{1,0:T(8,128)(2,1)S(1)} %get-tuple-element.36.after), channel_id=1, source_target_pairs={{0,64},{64,128},{128,192},{192,0},{1,65},{65,129},{129,193},{193,1... | collective-permute-start | bytes 405512 | tf_op jit(solution)/shard_map/ppermute | solution.py:626
  27.2 9.2 %collective-permute-start.6 = (bf16[528,128]{1,0:T(8,128)(2,1)S(1)}, bf16[528,128]{1,0:T(8,128)(2,1)S(1)}, u32[]{:S(2)}, u32[]{:S(2)}) collective-permute-start(bf16[528,128]{1,0:T(8,128)(2,1)S(1)} %get-tuple-element.36.after), channel_id=1, source_target_pairs={{0,192},{64,0},{128,64},{192,128},{1,193},{65,1},{129,65},{193,129... | collective-permute-start | bytes 405512 | tf_op jit(solution)/shard_map/ppermute | solution.py:626
  29.9 10.6 %collective-permute-start.11 = (bf16[384,128]{1,0:T(8,128)(2,1)S(1)}, bf16[384,128]{1,0:T(8,128)(2,1)S(1)}, u32[]{:S(2)}, u32[]{:S(2)}) collective-permute-start(bf16[384,128]{1,0:T(8,128)(2,1)S(1)} %get-tuple-element.50), channel_id=1, source_target_pairs={{0,192},{64,0},{128,64},{192,128},{1,193},{65,1},{129,65},{193,129... | collective-permute-start | bytes 294920 | tf_op jit(solution)/shard_map/ppermute | solution.py:626
  29.9 10.6 %collective-permute-start.12 = (bf16[384,128]{1,0:T(8,128)(2,1)S(1)}, bf16[384,128]{1,0:T(8,128)(2,1)S(1)}, u32[]{:S(2)}, u32[]{:S(2)}) collective-permute-start(bf16[384,128]{1,0:T(8,128)(2,1)S(1)} %get-tuple-element.51), channel_id=1, source_target_pairs={{0,64},{64,128},{128,192},{192,0},{1,65},{65,129},{129,193},{193,1... | collective-permute-start | bytes 294920 | tf_op jit(solution)/shard_map/ppermute | solution.py:626
  36.6 8.3 %collective-permute-start.10 = (bf16[80,128]{1,0:T(8,128)(2,1)S(1)}, bf16[80,128]{1,0:T(8,128)(2,1)S(1)}, u32[]{:S(2)}, u32[]{:S(2)}) collective-permute-start(bf16[80,128]{1,0:T(8,128)(2,1)S(1)} %get-tuple-element.48), channel_id=1, source_target_pairs={{0,56},{8,0},{16,8},{24,16},{32,24},{40,32},{48,40},{56,48},{1,57}... | collective-permute-start | bytes 61448 | tf_op jit(solution)/shard_map/ppermute | solution.py:626
  40.5 4.4 %collective-permute-start.9 = (bf16[80,128]{1,0:T(8,128)(2,1)S(1)}, bf16[80,128]{1,0:T(8,128)(2,1)S(1)}, u32[]{:S(2)}, u32[]{:S(2)}) collective-permute-start(bf16[80,128]{1,0:T(8,128)(2,1)S(1)} %get-tuple-element.47.after), channel_id=1, source_target_pairs={{0,8},{8,16},{16,24},{24,32},{32,40},{40,48},{48,56},{56,0},{1,9},... | collective-permute-start | bytes 61448 | tf_op jit(solution)/shard_map/ppermute | solution.py:626

commit v3 on v2

v3 whole, which is shorter than its diff:
```python
import jax
import jax.numpy as jnp
from jax import lax
from jax.experimental import pallas as pl
from jax.experimental.pallas import tpu as pltpu
from jax.sharding import PartitionSpec as P

f32 = jnp.float32
bf16 = jnp.bfloat16

DRAG = 0.6
WIND_GAIN = 0.5
HEAT_GAIN = 0.5
SALT_GAIN = 0.5
DIFFUSION = 0.15
ADVECTION = 0.5
VERTICAL = 0.2

NX = 32
NT = 4
NL = 10
LANES = 128

YF, YW, YC, YT, YROWS = 0, 256, 448, 464, 528
XPLANE, XP, XF, XROWS = 112, 448, 464, 496
CROWS, ZS, ZN, ZROWS = 528, 608, 640, 672
LAND = 8

VMEM_BYTES = 24 * 1024 * 1024

PLANES = (
    [("t", 0, level) for level in range(NL)]
    + [("t", 1, level) for level in range(NL)]
    + [("c", 0, 0), ("c", 0, 9), ("c", 1, 0), ("c", 1, 9)]
    + [("c", 0, level) for level in range(1, 9)]
    + [("c", 1, level) for level in range(1, 9)]
)
MASK_PLANE = len(PLANES)
PLANE_AT = {plane: index for index, plane in enumerate(PLANES)}


def x_rows(plane):
    if plane < 20:
        return 3 * plane, 3
    if plane < MASK_PLANE:
        return 60 + 2 * (plane - 20), 2
    return 100, 3


FACE_ROWS = (
    ("t", 0, 0, 0), ("t", 0, 0, 1), ("t", 0, 1, 0),
    ("t", 1, 0, 0), ("t", 1, 0, 1), ("t", 1, 1, 0),
    ("c", 0, 0, 0), ("c", 1, 0, 0),
)


def column(row):
    rows = lax.broadcasted_iota(jnp.int32, (NX, NX), 0)
    cols = lax.broadcasted_iota(jnp.int32, (NX, NX), 1)
    return jnp.sum(jnp.where(rows == cols, jnp.broadcast_to(row, (NX, NX)), 0.0), axis=1, keepdims=True)


def lane_ids(shape):
    return lax.broadcasted_iota(jnp.int32, shape, len(shape) - 1)


def start(*copies):
    for copy in copies:
        copy.start()


def wait(*copies):
    for copy in copies:
        copy.wait()


def roll(value, shift, axis):
    shift %= value.shape[axis]
    return value if shift == 0 else pltpu.roll(value, shift, axis)


def unpack_north(pack, plane, rows=slice(None)):
    return roll(pack[plane // 32][rows], -4 * (plane % 32), 1)


def unpack_south(pack, plane, rows=slice(None)):
    return roll(pack[plane // 32][rows], 4 * (plane % 32), 1)


def pack_y_kernel(
    air, src_h, live_h, land_h, w, tr, cu, yn, ys, flux, table, src, live, land, air_s, wn, ws, rows_s, edge, sems
):
    copies = [pltpu.make_async_copy(air, air_s, sems.at[0])]
    copies.append(pltpu.make_async_copy(w.at[:, NT - 1, 0, :, pl.ds(112, 16), :], wn, sems.at[1]))
    copies.append(pltpu.make_async_copy(w.at[:, 0, 0, :, pl.ds(0, 16), :], ws, sems.at[2]))
    for k, source in enumerate((tr, cu)):
        copies.append(pltpu.make_async_copy(source.at[:, :, :, pl.ds(384, 128)], edge.at[0, k], sems.at[3 + k]))
        copies.append(pltpu.make_async_copy(source.at[:, :, :, pl.ds(0, 128)], edge.at[1, k], sems.at[5 + k]))
    small = [
        pltpu.make_async_copy(source, target, sems.at[7 + k])
        for k, (source, target) in enumerate(((src_h, src), (live_h, live), (land_h, land)))
    ]
    start(copies[0], *small, *copies[1:])
    copies[0].wait()
    for t in range(NT):
        u, v, ta, qa, ts = (air_s[k, pl.ds(t, NX, stride=NT), :] for k in range(5))
        rate = DRAG * (1.0 + 0.5 * jnp.tanh(ts - ta)) * jnp.sqrt(u * u + v * v + 1.0)
        values = (rate * u, rate * v, rate * (ts - ta), rate * (jnp.exp(0.3 * ts) - qa))
        for f, value in enumerate(values):
            value = value.astype(bf16)
            flux[t, f] = value
            at = YF + ((t % 2) * 4 + f) * NX
            (ys if t < 2 else yn)[at : at + NX, :] = value
    wait(*small)
    slot = lax.broadcasted_iota(jnp.int32, (NT, 2, NX), 1)
    codes = jnp.where(slot < live[...], src[...], 9).astype(f32)
    table[...] = jnp.zeros((16, LANES), f32)
    for t in range(NT):
        table[2 * t : 2 * t + 2, 0:NX] = codes[t]
    table[LAND : LAND + NT, 0:NX] = land[...].astype(f32)
    sent = table[...].astype(bf16)
    yn[YC : YC + 16, :] = sent
    ys[YC : YC + 16, :] = sent
    wait(*copies[1:3])
    for send, tile, first in ((yn, wn, 13), (ys, ws, 0)):
        for x in range(NX):
            for s in range(2):
                block = tile[x, s].astype(f32)
                for d in range(3):
                    rows_s[pl.ds(d * 64 + s * 32 + x, 1), :] = block[first + d : first + d + 1]
        send[YW : YW + 192, :] = rows_s[...].astype(bf16)
    group = lane_ids((NX, LANES)) // 4
    packs = [[jnp.zeros((NX, LANES), f32)] * 2 for side in range(2)]
    for plane in range(MASK_PLANE + 1):
        if plane == 0:
            wait(copies[3], copies[4])
        if plane == 20:
            wait(copies[5], copies[6])
        part, at = plane // 32, plane % 32
        for side in range(2):
            if plane == MASK_PLANE:
                tile = LAND + (NT - 1 if side == 0 else 0)
                value = jnp.broadcast_to(column(table[tile : tile + 1, 0:NX]), (NX, LANES))
            else:
                kind, c, level = PLANES[plane]
                value = edge[side, 0 if kind == "t" else 1, c, level]
            turn, to = (-4 * at, 31 - at) if side == 0 else (4 * at, at)
            packs[side][part] = jnp.where(group == to, roll(value, turn, 1), packs[side][part])
    for send, halves in zip((yn, ys), packs):
        for part in range(2):
            send[YT + part * NX : YT + (part + 1) * NX, :] = halves[part].astype(bf16)


def pack_z_kernel(tr, cu, after, zu, zd, t_s, c_s, sems):
    copies = [
        pltpu.make_async_copy(tr.at[:, pl.ds(0, 3)], t_s.at[0], sems.at[0]),
        pltpu.make_async_copy(cu.at[:, pl.ds(0, 2)], c_s.at[0], sems.at[1]),
        pltpu.make_async_copy(tr.at[:, pl.ds(NL - 3, 3)], t_s.at[1], sems.at[2]),
        pltpu.make_async_copy(cu.at[:, pl.ds(NL - 2, 2)], c_s.at[1], sems.at[3]),
    ]
    for copy in copies:
        copy.start()
    for copy in copies:
        copy.wait()
    for side, send in enumerate((zu, zd)):
        for c in range(2):
            for level in range(3):
                send[c * 3 + level] = t_s[side, c, level].astype(bf16)
            for level in range(2):
                send[6 + c * 2 + level] = c_s[side, c, level].astype(bf16)


def inside(axis, low):
    at = lax.axis_index(axis)
    return jnp.where(at > 0 if low else at < lax.axis_size(axis) - 1, 1.0, 0.0).astype(f32)


def field_packs(y):
    return (y[YT : YT + NX, :].astype(f32), y[YT + NX : YT + 2 * NX, :].astype(f32))


def edge_packs(xw, xe):
    east, west = xw[XP : XP + 16, :].astype(f32), xe[XP : XP + 16, :].astype(f32)
    packs = [jnp.concatenate([east[4 * k : 4 * k + 4], west[4 * k : 4 * k + 4]], axis=0) for k in range(4)]
    return packs[:2], packs[2:]


def pack_x_kernel(flux, yn_r, ys_r, table, tr, cu, xe, xw, rows_s, edge, sems):
    copies = []
    for k, source in enumerate((tr, cu)):
        copies.append(pltpu.make_async_copy(source.at[:, :, pl.ds(0, 8), :], edge.at[0, k], sems.at[2 * k]))
        copies.append(pltpu.make_async_copy(source.at[:, :, pl.ds(24, 8), :], edge.at[1, k], sems.at[2 * k + 1]))
    start(*copies)
    packs = [*field_packs(yn_r), *field_packs(ys_r)]
    masks = [column(table[LAND + t : LAND + t + 1, 0:NX]) for t in range(NT)]
    in_south, in_north = inside("gy", True), inside("gy", False)
    for side, send in enumerate((xw, xe)):
        x = 0 if side == 0 else NX - 1
        first = 0 if side == 0 else NX - 4
        pack = jnp.concatenate([value[first : first + 4] for value in packs], axis=0)
        send[XP : XP + 16, :] = pack.astype(bf16)
        for t in range(8):
            for f in range(4):
                if 2 <= t < 6:
                    block = flux[t - 2, f].astype(f32)
                else:
                    got, half = (yn_r, t) if t < 2 else (ys_r, t - 6)
                    at = YF + (half * 4 + f) * NX
                    block = got[at : at + NX, :].astype(f32) * (in_south if t < 2 else in_north)
                rows_s[t * 4 + f : t * 4 + f + 1, :] = block[x : x + 1]
        send[XF:XROWS, :] = rows_s[0:32, :].astype(bf16)
    wait(*copies)
    for side, send in enumerate((xw, xe)):
        rows = slice(0, 8) if side == 0 else slice(24, 32)
        for c in range(4):
            for plane in range(MASK_PLANE + 1):
                if plane == MASK_PLANE:
                    value = jnp.broadcast_to(masks[c][rows], (8, LANES))
                else:
                    kind, component, level = PLANES[plane]
                    value = edge[side, 0 if kind == "t" else 1, component, level, :, c * LANES : (c + 1) * LANES]
                first, count = x_rows(plane)
                keep = slice(0, count) if side == 0 else slice(8 - count, 8)
                rows_s[c * XPLANE + first : c * XPLANE + first + count, :] = value[keep]
        send[0:XP, :] = rows_s[...].astype(bf16)


def remap_kernel(flux, yn_r, ys_r, table, w, after_x, part, wedge, rim, blk):
    zero = jnp.zeros((8, LANES), f32)
    in_south, in_north = inside("gy", True), inside("gy", False)
    for t in range(8):
        for f in range(4):
            if 2 <= t < 6:
                block = flux[t - 2, f].astype(f32)
            else:
                got, half = (yn_r, t) if t < 2 else (ys_r, t - 6)
                at = YF + (half * 4 + f) * NX
                block = got[at : at + NX, :].astype(f32) * (in_south if t < 2 else in_north)
            rim[t, f, 0:8, :] = zero
            rim[t, f, 8 : 8 + NX, :] = block
            rim[t, f, 8 + NX : 16 + NX, :] = zero

    def blocks(tile, row):
        code = jnp.broadcast_to(column(row), (NX, LANES))
        picked = [code == float(k) for k in range(9)]
        result = []
        for f in range(4):
            block = jnp.zeros((NX, LANES), f32)
            for k in range(9):
                x0 = 7 + k // 3
                block = jnp.where(picked[k], rim[tile + 2 + k % 3 - 1, f, x0 : x0 + NX, :], block)
            result.append(block)
        return result

    for t in range(NT):
        for s in range(2):
            row = 2 * t + s
            for f, block in enumerate(blocks(t, table[row : row + 1, 0:NX])):
                blk[row, f * NX : (f + 1) * NX, :] = block

    lane = lane_ids((NX, LANES))
    edges = [jnp.zeros((NX, LANES), f32) for f in range(4)]
    for got, tile, row, at in ((yn_r, -1, 6, 125), (ys_r, NT, 0, 0)):
        codes = got[YC : YC + 16, :].astype(f32)
        picked = [blocks(tile, codes[row + s : row + s + 1, 0:NX]) for s in range(2)]
        for d in range(3):
            weight = [
                got[YW + (d * 2 + s) * NX : YW + (d * 2 + s + 1) * NX, :].astype(f32) for s in range(2)
            ]
            for f in range(4):
                total = jnp.sum(weight[0] * picked[0][f] + weight[1] * picked[1][f], axis=1, keepdims=True)
                edges[f] = jnp.where(lane == at + d, total, edges[f])
    for f in range(4):
        part[4 * LANES + f * NX : 4 * LANES + (f + 1) * NX, :] = edges[f]

    for t in range(NT):

        def pair(i, _, t=t):
            x = 2 * i
            rows = [
                jnp.concatenate([blk[2 * t + s, pl.ds(x + j, 8, stride=NX), :] for j in range(2)], axis=0)
                for s in range(2)
            ]
            weights = jnp.concatenate(
                [jnp.concatenate([w[x + j, t, 0, s] for s in range(2)], axis=1) for j in range(2)], axis=0
            )
            product = lax.dot_general(
                jnp.concatenate(rows, axis=1).astype(bf16),
                weights,
                (((1,), (1,)), ((), ())),
                preferred_element_type=f32,
            )
            for j in range(2):
                block = product[8 * j : 8 * j + 4, j * LANES : (j + 1) * LANES]
                part[pl.ds(t * LANES + x + j, 4, stride=NX), :] = block
            return 0

        lax.fori_loop(0, NX // 2, pair, 0, unroll=8)
        for side, x in enumerate((0, NX - 1)):
            for s in range(2):
                wedge[side, t, s] = w[x, t, 0, s]


def rim_kernel(first_part, wedge, yn_r, ys_r, xe_r, xw_r, table, part, up, down, across, xs, rows_s):
    part[...] = first_part[...]
    near = [got[XF : XF + 32, :].astype(f32) * inside("gx", side == 0) for side, got in enumerate((xe_r, xw_r))]

    def blocks(side, tile, codes, row):
        x = 0 if side == 0 else NX - 1
        code = jnp.broadcast_to(codes[row : row + 1, x : x + 1], (4, LANES))
        block = jnp.zeros((4, LANES), f32)
        for k in range(3):
            at = (tile + 1 + k) * 4
            block = jnp.where(code == float(6 * side + k), near[side][at : at + 4], block)
        return block

    own_codes = table[...]
    gap = jnp.zeros((4, LANES), f32)
    for t in range(NT):
        rows = [
            jnp.concatenate([blocks(0, t, own_codes, 2 * t + s), gap, blocks(1, t, own_codes, 2 * t + s), gap], axis=0)
            for s in range(2)
        ]
        weights = jnp.concatenate(
            [jnp.concatenate([wedge[side, t, s] for s in range(2)], axis=1) for side in range(2)], axis=0
        )
        product = lax.dot_general(
            jnp.concatenate(rows, axis=1).astype(bf16), weights, (((1,), (1,)), ((), ())), preferred_element_type=f32
        )
        for side, x in enumerate((0, NX - 1)):
            part[pl.ds(t * LANES + x, 4, stride=NX), :] += product[8 * side : 8 * side + 4, side * LANES : (side + 1) * LANES]
    lane = lane_ids((4, LANES))
    for side, x in enumerate((0, NX - 1)):
        added = jnp.zeros((4, LANES), f32)
        for got, tile, row, at in ((yn_r, -1, 6, 125), (ys_r, NT, 0, 0)):
            codes = got[YC : YC + 16, :].astype(f32)
            picked = [blocks(side, tile, codes, row + s) for s in range(2)]
            for d in range(3):
                total = jnp.zeros((4, LANES), f32)
                for s in range(2):
                    first = YW + (d * 2 + s) * NX
                    weight = got[first : first + NX, :].astype(f32)[x : x + 1]
                    total += weight * picked[s]
                added = jnp.where(lane == at + d, jnp.sum(total, axis=1, keepdims=True), added)
        part[pl.ds(4 * LANES + x, 4, stride=NX), :] += added

    turned = part[4 * LANES : 5 * LANES, :].T
    halo = jnp.concatenate([turned[0:8], turned[LANES - 8 :]], axis=0).astype(bf16)
    own = part[0 : 4 * LANES, :].astype(bf16)
    for send in (up, down, across):
        send[0 : 4 * LANES, :] = own
        send[4 * LANES : CROWS, :] = halo
    xs[0] = xw_r[0:XP, :].astype(f32)
    xs[1] = xe_r[0:XP, :].astype(f32)
    south, north = edge_packs(xw_r, xe_r)
    low = lane_ids((8, LANES)) < 64
    for send, levels in ((up, (0, 1)), (down, (NL - 1, NL - 2))):
        for k, (kind, component, depth, column_at) in enumerate(FACE_ROWS):
            plane = PLANE_AT[(kind, component, levels[depth])]
            first, count = x_rows(plane)
            for c in range(4):
                for side in range(2):
                    at = c * XPLANE + first + (column_at if side == 0 else count - 1 - column_at)
                    to = c * 16 + side * 8 + k
                    rows_s[to : to + 1, :] = xs[side, at : at + 1, :]
            edge_col = jnp.where(low, unpack_north(north, plane), unpack_south(south, plane))
            for side in range(2):
                at = column_at if side == 0 else 7 - column_at
                to = 64 + side * 8 + k
                rows_s[to : to + 1, :] = edge_col[at : at + 1]
        send[CROWS:ZS, :] = rows_s[...].astype(bf16)
        send[ZS:ZN, :] = yn_r[YT : YT + NX, :]
        send[ZN:ZROWS, :] = ys_r[YT : YT + NX, :]


def flux_kernel(part, up_r, down_r, across_r, grid, ext, de, dw, rows_s):
    got = [ref[4 * LANES : CROWS, :].astype(f32) for ref in (up_r, down_r, across_r)]
    turned = got[0] + got[1] + got[2]
    halo = jnp.concatenate([turned[0:8], jnp.zeros((LANES - 16, LANES), f32), turned[8:16]], axis=0).T
    for c in range(5):
        for f in range(4):
            at = c * LANES + f * NX
            total = part[at : at + NX, :]
            if c < 4:
                for ref in (up_r, down_r, across_r):
                    total = total + ref[at : at + NX, :].astype(f32)
            else:
                total = total + halo[f * NX : (f + 1) * NX]
            total = total * grid[MASK, c, OWN, :]
            ext[f, :, c * LANES : (c + 1) * LANES] = total
            rows_s[0, c * 16 + f * 4 : c * 16 + f * 4 + 4, :] = total[0:4]
            rows_s[1, c * 16 + f * 4 : c * 16 + f * 4 + 4, :] = total[NX - 4 : NX]
    dw[...] = rows_s[0].astype(bf16)
    de[...] = rows_s[1].astype(bf16)


def lane_next(value, lane):
    rolled = pltpu.roll(value, LANES - 1, 2)
    return jnp.where(lane == LANES - 1, jnp.concatenate([rolled[1:], rolled[:1]], axis=0), rolled)


def lane_prev(value, lane):
    rolled = pltpu.roll(value, 1, 2)
    return jnp.where(lane == 0, jnp.concatenate([rolled[-1:], rolled[:-1]], axis=0), rolled)


OWN, WEST, EAST = slice(12, 44), slice(8, 12), slice(44, 48)
PLANE = (5, 56, LANES)


MASK, BASE, VERT, KEPT = range(4)


def advance(here, above, below, velocity, grid, rows, open_below=None):
    r = rows.start
    lane = lane_ids((5, 8, LANES))

    def at(plane, c, where=rows):
        return plane[0][c, plane[1], :, where, :]

    base, vert, kept = (grid[k, :, rows, :] for k in (BASE, VERT, KEPT))
    if above is None:
        kept = kept + vert
    if open_below is not None:
        down = vert * open_below
        kept = kept + (vert - down)
    a, b = at(velocity, 0), at(velocity, 1)
    east, west, north, south = base - a, base + a, base - b, base + b
    results = []
    for c in range(2):
        g = at(here, c)
        new = kept * g
        new += east * at(here, c, slice(r + 1, r + 9)) + west * at(here, c, slice(r - 1, r + 7))
        new += north * lane_next(g, lane) + south * lane_prev(g, lane)
        if above is None:
            new += vert * at(below, c)
        elif open_below is None:
            new += vert * (at(above, c) + at(below, c))
        else:
            new += vert * at(above, c) + down * at(below, c)
        results.append(new)
    return results


def land_or(value, grid, rows, tr, c, level, x, out):
    for col in range(4):
        cells = slice(col * LANES, (col + 1) * LANES)
        out[:, cells] = jnp.where(grid[MASK, col, rows, :] > 0.0, value[col], tr[c, level, x : x + 8, cells])


def middle_kernel(
    tr, cu, yn_r, ys_r, xe_r, xw_r, table, after, after_zu, after_zd, g0, vel, g1, g2, grid, done, xs
):
    south, north = field_packs(yn_r), field_packs(ys_r)
    low = lane_ids((NX, LANES)) < 64
    edge_south, edge_north = edge_packs(xw_r, xe_r)
    edge_low = lane_ids((8, LANES)) < 64
    xs[0] = xw_r[0:XP, :].astype(f32)
    xs[1] = xe_r[0:XP, :].astype(f32)
    in_south, in_north, in_west, in_east = inside("gy", True), inside("gy", False), inside("gx", True), inside("gx", False)

    def pieces(plane, col, own):
        first, count = x_rows(plane)
        if col < 4:
            at = col * XPLANE + first
            east, west = xs[0, at : at + count, :], xs[1, at : at + count, :]
        else:
            own = jnp.where(low, unpack_north(north, plane), unpack_south(south, plane))
            edge = jnp.where(edge_low, unpack_north(edge_north, plane), unpack_south(edge_south, plane))
            east, west = edge[0:count], edge[8 - count : 8]
        return ((OWN, own), (slice(44, 44 + count), east), (slice(12 - count, 12), west))

    for col in range(5):
        own = None
        if col < 4:
            own = jnp.broadcast_to(column(table[LAND + col : LAND + col + 1, 0:NX]), (NX, LANES))
        for (rows, value), in_x in zip(pieces(MASK_PLANE, col, own), (1.0, in_east, in_west)):
            if col == 4:
                value = value * jnp.where(low[0 : value.shape[0]], in_north, in_south)
            grid[MASK, col, rows, :] = value * in_x
    lane = lane_ids((5, 8, LANES))
    for r in range(8, 48, 8):
        rows, m = slice(r, r + 8), grid[MASK, :, r : r + 8, :]
        around = grid[MASK, :, r + 1 : r + 9, :] + grid[MASK, :, r - 1 : r + 7, :] + lane_next(m, lane) + lane_prev(m, lane)
        grid[BASE, :, rows, :] = DIFFUSION * m
        grid[VERT, :, rows, :] = VERTICAL * m
        grid[KEPT, :, rows, :] = m * (1.0 - 2.0 * VERTICAL - DIFFUSION * around)

    for col in range(5):
        for plane, (kind, c, level) in enumerate(PLANES):
            source, target = (tr, g0) if kind == "t" else (cu, vel)
            own = source[c, level, :, col * LANES : (col + 1) * LANES] if col < 4 else None
            for rows, value in pieces(plane, col, own):
                scale = grid[MASK, col, rows, :]
                target[c, level, col, rows, :] = value * (scale if kind == "t" else ADVECTION * scale)

    def sweep(src, src_at, dst, dst_at, levels):
        def one_level(l, _):
            for r in range(8, 48, 8):
                rows = slice(r, r + 8)
                at = l - src_at
                step = advance((src, at), (src, at - 1), (src, at + 1), (vel, l - 3), grid, rows)
                for c, value in enumerate(step):
                    dst[c, l - dst_at, :, rows, :] = value
            return 0

        lax.fori_loop(levels[0], levels[1], one_level, 0, unroll=2)

    sweep(g0, 3, g1, 4, (4, 12))
    sweep(g1, 4, g2, 5, (5, 11))

    def last(l, _):
        for r in range(12, 44, 8):
            rows = slice(r, r + 8)
            at = l - 5
            step = advance((g2, at), (g2, at - 1), (g2, at + 1), (vel, l - 3), grid, rows)
            for c, value in enumerate(step):
                land_or(value, grid, rows, tr, c, l - 3, r - 12, done.at[c, l - 6, r - 12 : r - 4])
        return 0

    lax.fori_loop(6, 10, last, 0, unroll=2)


def face_steps(planes, velocities, levels, out, grid, tr, starts, last_starts, out_x=lambda x: x, open_below=None):
    for k in range(3):
        for l in levels[k]:
            here, above, below = (planes[k].get(i) for i in (l, l - 1, l + 1))
            floor = open_below if l == 12 else None
            for r in starts if k < 2 else last_starts:
                rows = slice(r, r + 8)
                step = advance(here, above, below, velocities[l], grid, rows, floor)
                for c, value in enumerate(step):
                    if k < 2:
                        ref, index = planes[k + 1][l]
                        ref[c, index, :, rows, :] = value
                    else:
                        x = r - 12
                        land_or(value, grid, rows, tr, c, l - 3, x, out.at[c, l - levels[2][0], out_x(x) : out_x(x) + 8])


def planes_of(*runs):
    return {first + k: (ref, index + k) for first, count, ref, index in runs for k in range(count)}


def forced(velocities, tracers):
    return (
        (velocities, 0, ADVECTION * WIND_GAIN),
        (velocities, 1, ADVECTION * WIND_GAIN),
        (tracers, 0, HEAT_GAIN),
        (tracers, 1, -SALT_GAIN),
    )


WHOLE, INNER = range(8, 48, 8), range(12, 44, 8)


def outer_kernel(
    tr, g0, vel, g1, g2, grid, zu_r, zd_r, up_r, down_r, ext, middle, after, out, ocean_flux, s0, sv, s1, s2,
    b0, bv, b1, b2, top, bottom, sems,
):
    sec = lax.axis_index("sec")
    writes = [
        pltpu.make_async_copy(ext.at[:, :, pl.ds(0, 512)], ocean_flux, sems.at[0]),
        pltpu.make_async_copy(middle.at[:, pl.ds(1, 3)], out.at[:, pl.ds(4, 3)], sems.at[1]),
        pltpu.make_async_copy(bottom, out.at[:, pl.ds(7, 3)], sems.at[2]),
    ]
    start(*writes[:2])
    low = lane_ids((NX, LANES)) < 64

    def halo_planes(got, z, face, tracers, velocities):
        z_south = (got[ZS:ZN, :].astype(f32),)
        z_north = (got[ZN:ZROWS, :].astype(f32),)
        near = [got[CROWS + c * 16 : CROWS + (c + 1) * 16, :].astype(f32) for c in range(5)]

        def put(target, body, plane, at, scale):
            for col in range(4):
                value = body[:, col * LANES : (col + 1) * LANES].astype(f32)
                target[col, OWN, :] = value * (scale * grid[MASK, col, OWN, :])
            if plane is None:
                return
            col4 = jnp.where(low, unpack_north(z_north, plane), unpack_south(z_south, plane))
            target[4, OWN, :] = col4 * (scale * grid[MASK, 4, OWN, :])
            for col in range(5):
                for k, row in enumerate(at):
                    for to, value in ((44 + k, near[col][row : row + 1]), (11 - k, near[col][8 + row : 9 + row])):
                        target[col, to : to + 1, :] = value * (scale * grid[MASK, col, to : to + 1, :])

        for c in range(2):
            for k in range(3):
                depth = k if face == 1 else 2 - k
                level = k if face == 1 else 7 + k
                plane = PLANE_AT[("t", c, level)] if depth < 2 else None
                at = (3 * c, 3 * c + 1) if depth == 0 else (3 * c + 2,)
                put(tracers.at[c, k], z[c * 3 + k], plane, at, 1.0)
            for k in range(2):
                depth = k if face == 1 else 1 - k
                plane = PLANE_AT[("c", c, 0 if face == 1 else 9)] if depth == 0 else None
                put(velocities.at[c, k], z[6 + c * 2 + k], plane, (6 + c,), ADVECTION)

    halo_planes(up_r, zu_r, 1, b0, bv)
    face_steps(
        (
            planes_of((11, 2, g0, 8), (13, 3, b0, 0)),
            planes_of((10, 2, g1, 6), (12, 3, b1, 0)),
            planes_of((9, 2, g2, 4), (11, 3, b2, 0)),
        ),
        planes_of((10, 3, vel, 7), (13, 2, bv, 0)),
        (range(12, 15), range(11, 14), range(10, 13)),
        bottom, grid, tr, WHOLE, INNER,
        open_below=jnp.where(sec < lax.axis_size("sec") - 1, 1.0, 0.0).astype(f32),
    )
    writes[2].start()

    @pl.when(sec != 0)
    def _():
        level3 = pltpu.make_async_copy(middle.at[:, pl.ds(0, 1)], out.at[:, pl.ds(3, 1)], sems.at[3])
        level3.start()
        halo_planes(down_r, zd_r, 0, s0, sv)
        face_steps(
            (
                planes_of((0, 3, s0, 0), (3, 2, g0, 0)),
                planes_of((1, 3, s1, 0), (4, 2, g1, 0)),
                planes_of((2, 3, s2, 0), (5, 2, g2, 0)),
            ),
            planes_of((1, 2, sv, 0), (3, 3, vel, 0)),
            (range(1, 4), range(2, 5), range(3, 6)),
            top, grid, tr, WHOLE, INNER,
        )
        write = pltpu.make_async_copy(top.at[:, pl.ds(0, 3)], out.at[:, pl.ds(0, 3)], sems.at[4])
        write.start()
        wait(level3, write)

    @pl.when(sec == 0)
    def _():
        for f, (ref, c, gain) in enumerate(forced(sv, s0)):
            source = vel if f < 2 else g0
            for col in range(5):
                for r in range(8, 48, 8):
                    ref[c, 0, col, r : r + 8, :] = source[c, 0, col, r : r + 8, :]
                ref[c, 0, col, OWN, :] += gain * ext[f, :, col * LANES : (col + 1) * LANES] * grid[MASK, col, OWN, :]
        face_steps(
            surface_planes(s0, s1, s2, g0, g1, g2),
            planes_of((3, 1, sv, 0), (4, 3, vel, 1)),
            SURFACE_LEVELS,
            top, grid, tr, WHOLE, INNER,
        )
        write = pltpu.make_async_copy(top, out.at[:, pl.ds(0, 4)], sems.at[3])
        write.start()
        write.wait()

    wait(*writes)


SURFACE_LEVELS = (range(3, 5), range(3, 6), range(3, 7))


def surface_planes(s0, s1, s2, g0, g1, g2):
    return (
        planes_of((3, 1, s0, 0), (4, 2, g0, 1)),
        planes_of((3, 2, s1, 0), (5, 2, g1, 1)),
        planes_of((3, 3, s2, 0), (6, 2, g2, 1)),
    )


def surface_kernel(
    unfinished, tr, s0, sv, s1, s2, g0, vel, g1, g2, grid, de_r, dw_r, out, e0, ev, e1, e2, edge, sems
):
    @pl.when(lax.axis_index("sec") == 0)
    def _():
        halo = (de_r[...].astype(f32), dw_r[...].astype(f32))
        for c in range(2):
            for target, source, planes, groups in (
                (e0, s0, 1, (8, 16, 32, 40)),
                (ev, sv, 1, (8, 16, 32, 40)),
                (e1, s1, 2, (16, 32)),
                (e2, s2, 3, (16, 32)),
            ):
                for k in range(planes):
                    for r in groups:
                        target[c, k, :, r : r + 8, :] = source[c, k, :, r : r + 8, :]
        for side, rows in enumerate((WEST, EAST)):
            for f, (ref, c, gain) in enumerate(forced(ev, e0)):
                for col in range(5):
                    r = col * 16 + f * 4
                    ref[c, 0, col, rows, :] += gain * halo[side][r : r + 4] * grid[MASK, col, rows, :]
        face_steps(
            surface_planes(e0, e1, e2, g0, g1, g2),
            planes_of((3, 1, ev, 0), (4, 3, vel, 1)),
            SURFACE_LEVELS,
            edge, grid, tr, (8, 40), (12, 36), lambda x: 0 if x == 0 else 8,
        )
        writes = [
            pltpu.make_async_copy(
                edge.at[:, :, pl.ds(8 * side, 8)], out.at[:, pl.ds(0, 4), pl.ds(24 * side, 8)], sems.at[side]
            )
            for side in range(2)
        ]
        start(*writes)
        wait(*writes)


ANY = pl.BlockSpec(memory_space=pl.ANY)
HBM = pl.BlockSpec(memory_space=pltpu.HBM)
VMEM = pl.BlockSpec(memory_space=pltpu.VMEM)


def hbm(value):
    return pltpu.with_memory_space_constraint(value, pltpu.HBM)


def call(kernel, in_specs, outs, scratch, name, bytes_accessed, out_specs=None, aliases=None):
    return pl.pallas_call(
        kernel,
        out_shape=[jax.ShapeDtypeStruct(shape, dtype) for shape, dtype in outs],
        in_specs=in_specs,
        out_specs=out_specs or [VMEM] * len(outs),
        scratch_shapes=scratch,
        input_output_aliases=aliases or {},
        compiler_params=pltpu.CompilerParams(vmem_limit_bytes=VMEM_BYTES),
        cost_estimate=pl.CostEstimate(flops=0, bytes_accessed=bytes_accessed, transcendentals=0),
        name=name,
    )


def shifted(value, axis, step):
    count = lax.axis_size(axis)
    return lax.ppermute(value, axis, [(i, (i + step) % count) for i in range(count)])


def on_device(air_surface, remap_weights, sources, live_count, land_sea, tracers, currents):
    src = hbm(jnp.transpose(sources[:, :, 0, :], (1, 2, 0)))
    live = hbm(jnp.transpose(live_count, (1, 2, 0)))
    land = hbm(jnp.transpose(land_sea, (1, 0)))
    dma = pltpu.SemaphoreType.DMA

    yn, ys, flux, table = call(
        pack_y_kernel,
        [HBM] * 7,
        [((YROWS, LANES), bf16), ((YROWS, LANES), bf16), ((NT, 4, NX, LANES), bf16), ((16, LANES), f32)],
        [
            pltpu.VMEM((NT, 2, NX), jnp.int32),
            pltpu.VMEM((NT, 1, NX), jnp.int32),
            pltpu.VMEM((NT, NX), jnp.int32),
            pltpu.VMEM((5, NX * NT, LANES), f32),
            pltpu.VMEM((NX, 2, 16, LANES), bf16),
            pltpu.VMEM((NX, 2, 16, LANES), bf16),
            pltpu.VMEM((192, LANES), f32),
            pltpu.VMEM((2, 2, 2, NL, NX, LANES), f32),
            dma((10,)),
        ],
        "pack_y",
        6_000_000,
    )(hbm(air_surface.reshape(5, NX * NT, LANES)), src, live, land, hbm(remap_weights), hbm(tracers), hbm(currents))
    yn_r = shifted(yn, "gy", 1)
    ys_r = shifted(ys, "gy", -1)

    zu, zd = call(
        pack_z_kernel,
        [ANY, ANY, ANY],
        [((10, NX, 512), bf16)] * 2,
        [pltpu.VMEM((2, 2, 3, NX, 512), f32), pltpu.VMEM((2, 2, 2, NX, 512), f32), dma((4,))],
        "pack_z",
        3_000_000,
    )(tracers, currents, table)
    zu_r = shifted(zu, "sec", -1)
    zd_r = shifted(zd, "sec", 1)

    xe, xw = call(
        pack_x_kernel,
        [VMEM, VMEM, VMEM, VMEM, ANY, ANY],
        [((XROWS, LANES), bf16)] * 2,
        [pltpu.VMEM((XP, LANES), f32), pltpu.VMEM((2, 2, 2, NL, 8, 512), f32), dma((4,))],
        "pack_x",
        3_000_000,
    )(flux, yn_r, ys_r, table, tracers, currents)
    xe_r = shifted(xe, "gx", 1)
    xw_r = shifted(xw, "gx", -1)

    first_part, wedge = call(
        remap_kernel,
        [VMEM] * 5 + [ANY],
        [((5 * LANES, LANES), f32), ((2, NT, 2, LANES, LANES), bf16)],
        [
            pltpu.VMEM((8, 4, 48, LANES), f32),
            pltpu.VMEM((2 * NT, 2 * LANES, LANES), f32),
        ],
        "remap",
        18_000_000,
    )(flux, yn_r, ys_r, table, remap_weights, xe)
    part, up, down, across = call(
        rim_kernel,
        [VMEM] * 7,
        [((5 * LANES, LANES), f32), ((ZROWS, LANES), bf16), ((ZROWS, LANES), bf16), ((CROWS, LANES), bf16)],
        [pltpu.VMEM((2, XP, LANES), f32), pltpu.VMEM((80, LANES), f32)],
        "rim",
        4_000_000,
    )(first_part, wedge, yn_r, ys_r, xe_r, xw_r, table)
    up_r = shifted(up, "sec", -1)
    down_r = shifted(down, "sec", 1)
    across_r = shifted(across, "sec", 2)

    plane = (5, 56, LANES)
    g0, vel, g1, g2, grid, middle = call(
        middle_kernel,
        [VMEM] * 7 + [ANY] * 3,
        [
            ((2, NL) + plane, f32),
            ((2, NL) + plane, f32),
            ((2, NL - 2) + plane, f32),
            ((2, NL - 4) + plane, f32),
            ((4,) + plane, f32),
            ((2, NL - 6, NX, 512), f32),
        ],
        [
            pltpu.VMEM((2, XP, LANES), f32),
        ],
        "middle",
        20_000_000,
    )(tracers, currents, yn_r, ys_r, xe_r, xw_r, table, across, zu_r, zd_r)

    ext, de, dw = call(
        flux_kernel,
        [VMEM] * 5,
        [((4, NX, 5 * LANES), f32), ((80, LANES), bf16), ((80, LANES), bf16)],
        [pltpu.VMEM((2, 80, LANES), f32)],
        "flux_sum",
        3_000_000,
    )(part, up_r, down_r, across_r, grid)
    de_r = shifted(de, "gx", 1)
    dw_r = shifted(dw, "gx", -1)

    unfinished, ocean_flux, s0, sv, s1, s2 = call(
        outer_kernel,
        [VMEM] * 12 + [ANY],
        [((2, NL, NX, 512), f32), ((4, NX, 512), f32)] + [((2, count) + plane, f32) for count in (3, 2, 3, 3)],
        [pltpu.VMEM((2, count) + plane, f32) for count in (3, 2, 3, 3)]
        + [pltpu.VMEM((2, 4, NX, 512), f32), pltpu.VMEM((2, 3, NX, 512), f32), dma((5,))],
        "outer",
        18_000_000,
        [HBM, HBM] + [VMEM] * 4,
    )(tracers, g0, vel, g1, g2, grid, zu_r, zd_r, up_r, down_r, ext, middle, de)

    (tracers_out,) = call(
        surface_kernel,
        [HBM] + [VMEM] * 12,
        [((2, NL, NX, 512), f32)],
        [pltpu.VMEM((2, count) + plane, f32) for count in (1, 1, 2, 3)]
        + [pltpu.VMEM((2, 4, 16, 512), f32), dma((2,))],
        "surface",
        8_000_000,
        [HBM],
        {0: 0},
    )(unfinished, tracers, s0, sv, s1, s2, g0, vel, g1, g2, grid, de_r, dw_r)
    return (tracers_out, ocean_flux)


def solution(mesh):
    return jax.shard_map(
        on_device,
        mesh=mesh,
        in_specs=(
            P(None, "gx", "gy", "sec", None),
            P("gx", "gy", "sec", None, None, None),
            P("gx", "gy", "sec", None),
            P("gx", "gy", "sec"),
            P("gx", "gy"),
            P(None, "sec", "gx", "gy"),
            P(None, "sec", "gx", "gy"),
        ),
        out_specs=(P(None, "sec", "gx", "gy"), P(None, "gx", "gy")),
        check_vma=False,
    )
```

time: 48.1 us -> 43.5 us (0.904)
  the two profiles are of different devices: /device:TPU:8 before, /device:TPU:32 now
where the time goes in v3:
time: 43.5 us; the launch traced here: 43.4 us
  starting transfers between devices  20 us (46%)
  Pallas kernels  15.8 us (36%)
  waiting for transfers between devices  6.55 us (15%)
  between operations  0.92 us (2%)
    ppermute x11, starting transfers between devices, shifted(): lax.ppermute(value, axis, [(i, (i + step) % count) for i in range(count)])  20 us
    ppermute x11, waiting for transfers between devices, shifted(): lax.ppermute(value, axis, [(i, (i + step) % count) for i in range(count)])  6.55 us
    pallas_call x1, Pallas kernels, on_device(): call(middle_kernel, [VMEM] * 7 + [ANY] * 3, [((2, NL) + plane, f32), ((2,...  3.96 us
    pallas_call x1, Pallas kernels, on_device(): call(remap_kernel, [VMEM] * 5 + [ANY], [((5 * LANES, LANES), f32), ((2, N...  3.78 us
    pallas_call x1, Pallas kernels, on_device(): call(outer_kernel, [VMEM] * 12 + [ANY], [((2, NL, NX, 512), f32), ((4, NX...  3.55 us
    pallas_call x1, Pallas kernels, on_device(): call(pack_y_kernel, [HBM] * 7, [((YROWS, LANES), bf16), ((YROWS, LANES),...  2.09 us
    pallas_call x1, Pallas kernels, on_device(): call(surface_kernel, [HBM] + [VMEM] * 12, [((2, NL, NX, 512), f32)], [plt...  1.31 us
  transfers between devices with their start and end apart: 11, of which 4 were waited for; matrix products, arithmetic and copies ran while one was open for 0% of the time, Pallas kernels for 28%

profile of v3, /device:TPU:32, one launch (start us, length us, event | category | flops | bytes accessed | tf_op | source)
XLA Modules:
  0.0 43.4 jit_solution(13938216011907795694)
XLA Ops:
  0.6 0.0 slice-start
  0.6 0.0 copy-start
  0.7 0.0 copy-start.1
  0.7 0.0 slice-start.1
  0.7 2.1 %pack_y.1 = (bf16[528,128]{1,0:T(8,128)(2,1)S(1)}, bf16[528,128]{1,0:T(8,128)(2,1)S(1)}, bf16[4,4,32,128]{3,2,1,0:T(8,128)(2,1)S(1)}, f32[16,128]{1,0:T(8,128)S(1)}) custom-call(f32[5,128,128]{2,1,0:T(8,128)} %bitcast.8, s32[4,2,32]{2,1,0:T(2,128)} %bitcast.9, s32[4,1,32]{2,1,0:T(1,128)} %bitcast.10, s32[4,32]{1,0:T(4,128)} %bitcast.11, ...), custom_call_target="tpu_custom_call" | custom-call | bytes 6000000 | tf_op jit(solution)/shard_map/pack_y/pallas_call | solution.py:736
  2.8 0.1 collective-permute-start
  2.9 4.9 %collective-permute-start.1 = (bf16[528,128]{1,0:T(8,128)(2,1)S(1)}, bf16[528,128]{1,0:T(8,128)(2,1)S(1)}, u32[]{:S(2)}, u32[]{:S(2)}) collective-permute-start(bf16[528,128]{1,0:T(8,128)(2,1)S(1)} %get-tuple-element.32), channel_id=1, source_target_pairs={{0,7},{1,0},{2,1},{3,2},{4,3},{5,4},{6,5},{7,6},{8,15},{9,8},{10,9... | collective-permute-start | bytes 405512 | tf_op jit(solution)/shard_map/ppermute | solution.py:727
  7.8 0.0 copy-done
  7.8 0.0 copy-done.1
  7.8 0.3 pack_z.1
  8.1 2.8 %collective-permute-start.4 = (bf16[10,32,512]{2,1,0:T(8,128)(2,1)S(1)}, bf16[10,32,512]{2,1,0:T(8,128)(2,1)S(1)}, u32[]{:S(2)}, u32[]{:S(2)}) collective-permute-start(bf16[10,32,512]{2,1,0:T(8,128)(2,1)S(1)} %get-tuple-element.40), channel_id=1, source_target_pairs={{0,192},{64,0},{128,64},{192,128},{1,193},{65,1},{129,65},{193,129... | collective-permute-start | bytes 983048 | tf_op jit(solution)/shard_map/ppermute | solution.py:727
  11.0 0.0 collective-permute-start.5
  11.0 0.9 %collective-permute-done.yn_r = bf16[528,128]{1,0:T(8,128)(2,1)S(1)} collective-permute-done((bf16[528,128]{1,0:T(8,128)(2,1)S(1)}, bf16[528,128]{1,0:T(8,128)(2,1)S(1)}, u32[]{:S(2)}, u32[]{:S(2)}) %collective-permute-start) | collective-permute-done | bytes 135200 | tf_op jit(solution)/shard_map/ppermute | solution.py:727
  11.8 0.0 collective-permute-done.1.ys_r
  11.8 0.3 pack_x.1
  12.2 1.7 %collective-permute-start.2 = (bf16[496,128]{1,0:T(8,128)(2,1)S(1)}, bf16[496,128]{1,0:T(8,128)(2,1)S(1)}, u32[]{:S(2)}, u32[]{:S(2)}) collective-permute-start(bf16[496,128]{1,0:T(8,128)(2,1)S(1)} %get-tuple-element.35.after_x), channel_id=1, source_target_pairs={{0,8},{8,16},{16,24},{24,32},{32,40},{40,48},{48,56},{56,0},{1,9},... | collective-permute-start | bytes 380936 | tf_op jit(solution)/shard_map/ppermute | solution.py:727
  13.8 2.6 %collective-permute-start.3 = (bf16[496,128]{1,0:T(8,128)(2,1)S(1)}, bf16[496,128]{1,0:T(8,128)(2,1)S(1)}, u32[]{:S(2)}, u32[]{:S(2)}) collective-permute-start(bf16[496,128]{1,0:T(8,128)(2,1)S(1)} %get-tuple-element.36), channel_id=1, source_target_pairs={{0,56},{8,0},{16,8},{24,16},{32,24},{40,32},{48,40},{56,48},{1,57}... | collective-permute-start | bytes 380936 | tf_op jit(solution)/shard_map/ppermute | solution.py:727
  16.4 0.0 slice-done
  16.4 0.0 slice-done.1
  16.4 3.8 %remap.1 = (f32[640,128]{1,0:T(8,128)S(1)}, bf16[2,4,2,128,128]{4,3,2,1,0:T(8,128)(2,1)S(1)}) custom-call(bf16[4,4,32,128]{3,2,1,0:T(8,128)(2,1)S(1)} %get-tuple-element.33.flux, bf16[528,128]{1,0:T(8,128)(2,1)S(1)} %collective-permute-done.yn_r, bf16[528,128]{1,0:T(8,128)(2,1)S(1)} %collective-permute-done.1.ys_r, ...), custom_call_target="tpu_custom_call" | custom-call | bytes 18000000 | tf_op jit(solution)/shard_map/remap/pallas_call | solution.py:779
  20.2 0.0 collective-permute-done.2.xe_r
  20.2 0.0 collective-permute-done.3.xw_r
  20.2 0.4 rim.1
  20.6 2.8 %collective-permute-start.6 = (bf16[672,128]{1,0:T(8,128)(2,1)S(1)}, bf16[672,128]{1,0:T(8,128)(2,1)S(1)}, u32[]{:S(2)}, u32[]{:S(2)}) collective-permute-start(bf16[672,128]{1,0:T(8,128)(2,1)S(1)} %get-tuple-element.47), channel_id=1, source_target_pairs={{0,192},{64,0},{128,64},{192,128},{1,193},{65,1},{129,65},{193,129... | collective-permute-start | bytes 516104 | tf_op jit(solution)/shard_map/ppermute | solution.py:727
  23.4 0.0 collective-permute-start.7
  23.4 2.3 %collective-permute-start.8 = (bf16[528,128]{1,0:T(8,128)(2,1)S(1)}, bf16[528,128]{1,0:T(8,128)(2,1)S(1)}, u32[]{:S(2)}, u32[]{:S(2)}) collective-permute-start(bf16[528,128]{1,0:T(8,128)(2,1)S(1)} %get-tuple-element.39.after), channel_id=1, source_target_pairs={{0,128},{64,192},{128,0},{192,64},{1,129},{65,193},{129,1},{193,65... | collective-permute-start | bytes 405512 | tf_op jit(solution)/shard_map/ppermute | solution.py:727
  25.7 0.0 collective-permute-done.4.after_zu.zu_r
  25.7 0.0 collective-permute-done.5.after_zd.zd_r
  25.7 4.0 %middle.1 = (f32[2,10,5,56,128]{4,3,2,1,0:T(8,128)S(1)}, f32[2,10,5,56,128]{4,3,2,1,0:T(8,128)S(1)}, f32[2,8,5,56,128]{4,3,2,1,0:T(8,128)S(1)}, f32[2,6,5,56,128...) custom-call(f32[2,10,32,512]{3,2,1,0:T(8,128)S(1)} %copy-done, ...), custom_call_target="tpu_custom_call" | custom-call | bytes 20000000 | tf_op jit(solution)/shard_map/middle/pallas_call | solution.py:803
  29.7 2.5 %collective-permute-done.8.across_r = bf16[528,128]{1,0:T(8,128)(2,1)S(1)} collective-permute-done((bf16[528,128]{1,0:T(8,128)(2,1)S(1)}, bf16[528,128]{1,0:T(8,128)(2,1)S(1)}, u32[]{:S(2)}, u32[]{:S(2)}) %collective-permute-start.8) | collective-permute-done | bytes 135200 | tf_op jit(solution)/shard_map/ppermute | solution.py:727
  32.2 0.0 collective-permute-done.6.up_r
  32.2 0.8 %collective-permute-done.7.down_r = bf16[672,128]{1,0:T(8,128)(2,1)S(1)} collective-permute-done((bf16[672,128]{1,0:T(8,128)(2,1)S(1)}, bf16[672,128]{1,0:T(8,128)(2,1)S(1)}, u32[]{:S(2)}, u32[]{:S(2)}) %collective-permute-start.7) | collective-permute-done | bytes 172064 | tf_op jit(solution)/shard_map/ppermute | solution.py:727
  33.0 0.1 flux_sum.1
  33.2 2.9 %collective-permute-start.10 = (bf16[80,128]{1,0:T(8,128)(2,1)S(1)}, bf16[80,128]{1,0:T(8,128)(2,1)S(1)}, u32[]{:S(2)}, u32[]{:S(2)}) collective-permute-start(bf16[80,128]{1,0:T(8,128)(2,1)S(1)} %get-tuple-element.58), channel_id=1, source_target_pairs={{0,56},{8,0},{16,8},{24,16},{32,24},{40,32},{48,40},{56,48},{1,57}... | collective-permute-start | bytes 61448 | tf_op jit(solution)/shard_map/ppermute | solution.py:727
  36.0 0.0 collective-permute-start.9
  36.0 3.6 %outer.1 = (f32[2,10,32,512]{3,2,1,0:T(8,128)}, f32[4,32,512]{2,1,0:T(8,128)}, f32[2,3,5,56,128]{4,3,2,1,0:T(8,128)S(1)}, f32[2,2,5,56,128]{4,3,2,1,0:T(8,128)S(...) custom-call(f32[2,10,32,512]{3,2,1,0:T(8,128)S(1)} %copy-done, ...), custom_call_target="tpu_custom_call" | custom-call | bytes 18000000 | tf_op jit(solution)/shard_map/outer/pallas_call | solution.py:832
  39.6 0.0 collective-permute-done.10.dw_r
  39.6 2.3 %collective-permute-done.9.de_r = bf16[80,128]{1,0:T(8,128)(2,1)S(1)} collective-permute-done((bf16[80,128]{1,0:T(8,128)(2,1)S(1)}, bf16[80,128]{1,0:T(8,128)(2,1)S(1)}, u32[]{:S(2)}, u32[]{:S(2)}) %collective-permute-start.9) | collective-permute-done | bytes 20512 | tf_op jit(solution)/shard_map/ppermute | solution.py:727
  41.9 1.3 %surface.1 = f32[2,10,32,512]{3,2,1,0:T(8,128)} custom-call(f32[2,10,32,512]{3,2,1,0:T(8,128)} %get-tuple-element.53.unfinished, f32[2,10,32,512]{3,2,1,0:T(8,128)S(1)} %copy-done, f32[2,3,5,56,128]{4,3,2,1,0:T(8,128)S(1)} %get-tuple-element.54.s0, f32[2,2,5,56,128]{4,3,2,1,0:T(8,128)S(1)} %get-tuple-element.55.sv, ...), custom_call_target="tpu_custom_call", output_to_operand_aliasing={{}: (0, {})} | custom-call | bytes 8000000 | tf_op jit(solution)/shard_map/surface/pallas_call | solution.py:843
  (1 shorter events, 0.0 us)
Async XLA Ops:
  0.6 15.8 %slice-start = ((s8[8388608]{0:T(1024)(128)(4,1)}), s8[4194304]{0:T(1024)(128)(4,1)S(1)}, s32[]{:S(2)}) async-start(s8[8388608]{0:T(1024)(128)(4,1)} %bitcast.6), calls=%async_computation | async-start | bytes 8388608
  0.6 7.1 %copy-start = (f32[2,10,32,512]{3,2,1,0:T(8,128)S(1)}, f32[2,10,32,512]{3,2,1,0:T(8,128)}, u32[]{:S(2)}) copy-start(f32[2,10,32,512]{3,2,1,0:T(8,128)} %tr.11) | copy-start | bytes 3932164
  0.7 7.1 %copy-start.1 = (f32[2,10,32,512]{3,2,1,0:T(8,128)S(1)}, f32[2,10,32,512]{3,2,1,0:T(8,128)}, u32[]{:S(2)}) copy-start(f32[2,10,32,512]{3,2,1,0:T(8,128)} %cu.7) | copy-start | bytes 3932164
  0.7 15.7 %slice-start.1 = ((s8[8388608]{0:T(1024)(128)(4,1)}), s8[4194304]{0:T(1024)(128)(4,1)S(1)}, s32[]{:S(2)}) async-start(s8[8388608]{0:T(1024)(128)(4,1)} %bitcast.6), calls=%async_computation.1 | async-start | bytes 8388608
  2.8 9.1 %collective-permute-start = (bf16[528,128]{1,0:T(8,128)(2,1)S(1)}, bf16[528,128]{1,0:T(8,128)(2,1)S(1)}, u32[]{:S(2)}, u32[]{:S(2)}) collective-permute-start(bf16[528,128]{1,0:T(8,128)(2,1)S(1)} %get-tuple-element.31), channel_id=1, source_target_pairs={{0,1},{1,2},{2,3},{3,4},{4,5},{5,6},{6,7},{7,0},{8,9},{9,10},{10,1... | collective-permute-start | bytes 405512 | tf_op jit(solution)/shard_map/ppermute | solution.py:727
  2.9 9.0 %collective-permute-start.1 = (bf16[528,128]{1,0:T(8,128)(2,1)S(1)}, bf16[528,128]{1,0:T(8,128)(2,1)S(1)}, u32[]{:S(2)}, u32[]{:S(2)}) collective-permute-start(bf16[528,128]{1,0:T(8,128)(2,1)S(1)} %get-tuple-element.32), channel_id=1, source_target_pairs={{0,7},{1,0},{2,1},{3,2},{4,3},{5,4},{6,5},{7,6},{8,15},{9,8},{10,9... | collective-permute-start | bytes 405512 | tf_op jit(solution)/shard_map/ppermute | solution.py:727
  8.1 17.6 %collective-permute-start.4 = (bf16[10,32,512]{2,1,0:T(8,128)(2,1)S(1)}, bf16[10,32,512]{2,1,0:T(8,128)(2,1)S(1)}, u32[]{:S(2)}, u32[]{:S(2)}) collective-permute-start(bf16[10,32,512]{2,1,0:T(8,128)(2,1)S(1)} %get-tuple-element.40), channel_id=1, source_target_pairs={{0,192},{64,0},{128,64},{192,128},{1,193},{65,1},{129,65},{193,129... | collective-permute-start | bytes 983048 | tf_op jit(solution)/shard_map/ppermute | solution.py:727
  11.0 14.7 %collective-permute-start.5 = (bf16[10,32,512]{2,1,0:T(8,128)(2,1)S(1)}, bf16[10,32,512]{2,1,0:T(8,128)(2,1)S(1)}, u32[]{:S(2)}, u32[]{:S(2)}) collective-permute-start(bf16[10,32,512]{2,1,0:T(8,128)(2,1)S(1)} %get-tuple-element.41), channel_id=1, source_target_pairs={{0,64},{64,128},{128,192},{192,0},{1,65},{65,129},{129,193},{193,1... | collective-permute-start | bytes 983048 | tf_op jit(solution)/shard_map/ppermute | solution.py:727
  12.2 8.0 %collective-permute-start.2 = (bf16[496,128]{1,0:T(8,128)(2,1)S(1)}, bf16[496,128]{1,0:T(8,128)(2,1)S(1)}, u32[]{:S(2)}, u32[]{:S(2)}) collective-permute-start(bf16[496,128]{1,0:T(8,128)(2,1)S(1)} %get-tuple-element.35.after_x), channel_id=1, source_target_pairs={{0,8},{8,16},{16,24},{24,32},{32,40},{40,48},{48,56},{56,0},{1,9},... | collective-permute-start | bytes 380936 | tf_op jit(solution)/shard_map/ppermute | solution.py:727
  13.8 6.4 %collective-permute-start.3 = (bf16[496,128]{1,0:T(8,128)(2,1)S(1)}, bf16[496,128]{1,0:T(8,128)(2,1)S(1)}, u32[]{:S(2)}, u32[]{:S(2)}) collective-permute-start(bf16[496,128]{1,0:T(8,128)(2,1)S(1)} %get-tuple-element.36), channel_id=1, source_target_pairs={{0,56},{8,0},{16,8},{24,16},{32,24},{40,32},{48,40},{56,48},{1,57}... | collective-permute-start | bytes 380936 | tf_op jit(solution)/shard_map/ppermute | solution.py:727
  20.6 11.6 %collective-permute-start.6 = (bf16[672,128]{1,0:T(8,128)(2,1)S(1)}, bf16[672,128]{1,0:T(8,128)(2,1)S(1)}, u32[]{:S(2)}, u32[]{:S(2)}) collective-permute-start(bf16[672,128]{1,0:T(8,128)(2,1)S(1)} %get-tuple-element.47), channel_id=1, source_target_pairs={{0,192},{64,0},{128,64},{192,128},{1,193},{65,1},{129,65},{193,129... | collective-permute-start | bytes 516104 | tf_op jit(solution)/shard_map/ppermute | solution.py:727
  23.4 9.6 %collective-permute-start.7 = (bf16[672,128]{1,0:T(8,128)(2,1)S(1)}, bf16[672,128]{1,0:T(8,128)(2,1)S(1)}, u32[]{:S(2)}, u32[]{:S(2)}) collective-permute-start(bf16[672,128]{1,0:T(8,128)(2,1)S(1)} %get-tuple-element.48), channel_id=1, source_target_pairs={{0,64},{64,128},{128,192},{192,0},{1,65},{65,129},{129,193},{193,1... | collective-permute-start | bytes 516104 | tf_op jit(solution)/shard_map/ppermute | solution.py:727
  23.4 8.8 %collective-permute-start.8 = (bf16[528,128]{1,0:T(8,128)(2,1)S(1)}, bf16[528,128]{1,0:T(8,128)(2,1)S(1)}, u32[]{:S(2)}, u32[]{:S(2)}) collective-permute-start(bf16[528,128]{1,0:T(8,128)(2,1)S(1)} %get-tuple-element.39.after), channel_id=1, source_target_pairs={{0,128},{64,192},{128,0},{192,64},{1,129},{65,193},{129,1},{193,65... | collective-permute-start | bytes 405512 | tf_op jit(solution)/shard_map/ppermute | solution.py:727
  33.2 6.4 %collective-permute-start.10 = (bf16[80,128]{1,0:T(8,128)(2,1)S(1)}, bf16[80,128]{1,0:T(8,128)(2,1)S(1)}, u32[]{:S(2)}, u32[]{:S(2)}) collective-permute-start(bf16[80,128]{1,0:T(8,128)(2,1)S(1)} %get-tuple-element.58), channel_id=1, source_target_pairs={{0,56},{8,0},{16,8},{24,16},{32,24},{40,32},{48,40},{56,48},{1,57}... | collective-permute-start | bytes 61448 | tf_op jit(solution)/shard_map/ppermute | solution.py:727
  36.0 5.9 %collective-permute-start.9 = (bf16[80,128]{1,0:T(8,128)(2,1)S(1)}, bf16[80,128]{1,0:T(8,128)(2,1)S(1)}, u32[]{:S(2)}, u32[]{:S(2)}) collective-permute-start(bf16[80,128]{1,0:T(8,128)(2,1)S(1)} %get-tuple-element.52.after), channel_id=1, source_target_pairs={{0,8},{8,16},{16,24},{24,32},{32,40},{40,48},{48,56},{56,0},{1,9},... | collective-permute-start | bytes 61448 | tf_op jit(solution)/shard_map/ppermute | solution.py:727

commit v4 on v3

--- a/solution.py
+++ b/solution.py
@@ -21,9 +21,9 @@
 NL = 10
 LANES = 128
 
-YF, YW, YC, YT, YROWS = 0, 256, 448, 464, 528
+YF, YW, YC, YT, YROWS = 0, 256, 448, 464, 496
 XPLANE, XP, XF, XROWS = 112, 448, 464, 496
-CROWS, ZS, ZN, ZROWS = 528, 608, 640, 672
+CROWS, ZP, ZROWS = 528, 608, 640
 LAND = 8
 
 VMEM_BYTES = 24 * 1024 * 1024
@@ -52,6 +52,7 @@
     ("t", 1, 0, 0), ("t", 1, 0, 1), ("t", 1, 1, 0),
     ("c", 0, 0, 0), ("c", 1, 0, 0),
 )
+APART = 6
 
 
 def column(row):
@@ -74,21 +75,37 @@
         copy.wait()
 
 
+def even(axis):
+    return lax.axis_index(axis) % 2 == 0
+
+
+def sort_pair(axis, a, b, plus, minus):
+    @pl.when(even(axis))
+    def _():
+        plus[...] = a[...]
+        minus[...] = b[...]
+
+    @pl.when(jnp.logical_not(even(axis)))
+    def _():
+        plus[...] = b[...]
+        minus[...] = a[...]
+
+
 def roll(value, shift, axis):
     shift %= value.shape[axis]
     return value if shift == 0 else pltpu.roll(value, shift, axis)
 
 
 def unpack_north(pack, plane, rows=slice(None)):
-    return roll(pack[plane // 32][rows], -4 * (plane % 32), 1)
+    return roll(pack[rows], -3 * plane, 1)
 
 
 def unpack_south(pack, plane, rows=slice(None)):
-    return roll(pack[plane // 32][rows], 4 * (plane % 32), 1)
+    return roll(pack[rows], 125 - 3 * plane, 1)
 
 
 def pack_y_kernel(
-    air, src_h, live_h, land_h, w, tr, cu, yn, ys, flux, table, src, live, land, air_s, wn, ws, rows_s, edge, sems
+    air, src_h, live_h, land_h, w, tr, cu, ya, yb, flux, table, yn, ys, src, live, land, air_s, wn, ws, rows_s, edge, sems
 ):
     copies = [pltpu.make_async_copy(air, air_s, sems.at[0])]
     copies.append(pltpu.make_async_copy(w.at[:, NT - 1, 0, :, pl.ds(112, 16), :], wn, sems.at[1]))
@@ -129,14 +146,13 @@
                 for d in range(3):
                     rows_s[pl.ds(d * 64 + s * 32 + x, 1), :] = block[first + d : first + d + 1]
         send[YW : YW + 192, :] = rows_s[...].astype(bf16)
-    group = lane_ids((NX, LANES)) // 4
-    packs = [[jnp.zeros((NX, LANES), f32)] * 2 for side in range(2)]
+    group = lane_ids((NX, LANES)) // 3
+    packs = [jnp.zeros((NX, LANES), f32)] * 2
     for plane in range(MASK_PLANE + 1):
         if plane == 0:
             wait(copies[3], copies[4])
         if plane == 20:
             wait(copies[5], copies[6])
-        part, at = plane // 32, plane % 32
         for side in range(2):
             if plane == MASK_PLANE:
                 tile = LAND + (NT - 1 if side == 0 else 0)
@@ -144,11 +160,11 @@
             else:
                 kind, c, level = PLANES[plane]
                 value = edge[side, 0 if kind == "t" else 1, c, level]
-            turn, to = (-4 * at, 31 - at) if side == 0 else (4 * at, at)
-            packs[side][part] = jnp.where(group == to, roll(value, turn, 1), packs[side][part])
-    for send, halves in zip((yn, ys), packs):
-        for part in range(2):
-            send[YT + part * NX : YT + (part + 1) * NX, :] = halves[part].astype(bf16)
+            turn = 3 * plane - (125 if side == 0 else 0)
+            packs[side] = jnp.where(group == plane, roll(value, turn, 1), packs[side])
+    for send, pack in zip((yn, ys), packs):
+        send[YT : YT + NX, :] = pack.astype(bf16)
+    sort_pair("gy", yn, ys, ya, yb)
 
 
 def pack_z_kernel(tr, cu, after, zu, zd, t_s, c_s, sems):
@@ -175,29 +191,29 @@
     return jnp.where(at > 0 if low else at < lax.axis_size(axis) - 1, 1.0, 0.0).astype(f32)
 
 
-def field_packs(y):
-    return (y[YT : YT + NX, :].astype(f32), y[YT + NX : YT + 2 * NX, :].astype(f32))
+def field_pack(y):
+    return y[YT : YT + NX, :].astype(f32)
 
 
 def edge_packs(xw, xe):
     east, west = xw[XP : XP + 16, :].astype(f32), xe[XP : XP + 16, :].astype(f32)
-    packs = [jnp.concatenate([east[4 * k : 4 * k + 4], west[4 * k : 4 * k + 4]], axis=0) for k in range(4)]
-    return packs[:2], packs[2:]
-
-
-def pack_x_kernel(flux, yn_r, ys_r, table, tr, cu, xe, xw, rows_s, edge, sems):
+    return [jnp.concatenate([east[4 * k : 4 * k + 4], west[4 * k : 4 * k + 4]], axis=0) for k in range(2)]
+
+
+def pack_x_kernel(flux, ya_r, yb_r, table, tr, cu, xa, xb, yn_r, ys_r, xe, xw, rows_s, edge, sems):
     copies = []
     for k, source in enumerate((tr, cu)):
         copies.append(pltpu.make_async_copy(source.at[:, :, pl.ds(0, 8), :], edge.at[0, k], sems.at[2 * k]))
         copies.append(pltpu.make_async_copy(source.at[:, :, pl.ds(24, 8), :], edge.at[1, k], sems.at[2 * k + 1]))
     start(*copies)
-    packs = [*field_packs(yn_r), *field_packs(ys_r)]
+    sort_pair("gy", ya_r, yb_r, ys_r, yn_r)
+    packs = [field_pack(yn_r), field_pack(ys_r)]
     masks = [column(table[LAND + t : LAND + t + 1, 0:NX]) for t in range(NT)]
     in_south, in_north = inside("gy", True), inside("gy", False)
     for side, send in enumerate((xw, xe)):
         x = 0 if side == 0 else NX - 1
         first = 0 if side == 0 else NX - 4
-        pack = jnp.concatenate([value[first : first + 4] for value in packs], axis=0)
+        pack = jnp.concatenate([value[first : first + 4] for value in packs * 2], axis=0)
         send[XP : XP + 16, :] = pack.astype(bf16)
         for t in range(8):
             for f in range(4):
@@ -223,6 +239,7 @@
                 keep = slice(0, count) if side == 0 else slice(8 - count, 8)
                 rows_s[c * XPLANE + first : c * XPLANE + first + count, :] = value[keep]
         send[0:XP, :] = rows_s[...].astype(bf16)
+    sort_pair("gx", xe, xw, xa, xb)
 
 
 def remap_kernel(flux, yn_r, ys_r, table, w, after_x, part, wedge, rim, blk):
@@ -301,7 +318,10 @@
                 wedge[side, t, s] = w[x, t, 0, s]
 
 
-def rim_kernel(first_part, wedge, yn_r, ys_r, xe_r, xw_r, table, part, up, down, across, xs, rows_s):
+def rim_kernel(
+    first_part, wedge, yn_r, ys_r, xa_r, xb_r, table, part, ua, ub, across, xe_r, xw_r, up, down, xs, rows_s
+):
+    sort_pair("gx", xa_r, xb_r, xw_r, xe_r)
     part[...] = first_part[...]
     near = [got[XF : XF + 32, :].astype(f32) * inside("gx", side == 0) for side, got in enumerate((xe_r, xw_r))]
 
@@ -368,13 +388,17 @@
                 at = column_at if side == 0 else 7 - column_at
                 to = 64 + side * 8 + k
                 rows_s[to : to + 1, :] = edge_col[at : at + 1]
-        send[CROWS:ZS, :] = rows_s[...].astype(bf16)
-        send[ZS:ZN, :] = yn_r[YT : YT + NX, :]
-        send[ZN:ZROWS, :] = ys_r[YT : YT + NX, :]
-
-
-def flux_kernel(part, up_r, down_r, across_r, grid, ext, de, dw, rows_s):
-    got = [ref[4 * LANES : CROWS, :].astype(f32) for ref in (up_r, down_r, across_r)]
+        send[CROWS:ZP, :] = rows_s[...].astype(bf16)
+        pack, group = field_pack(ys_r), lane_ids((NX, LANES)) // 3
+        moved = roll(field_pack(yn_r), 3 * APART, 1)
+        for plane in sorted({PLANE_AT[(kind, component, levels[depth])] for kind, component, depth, _ in FACE_ROWS}):
+            pack = jnp.where(group == plane + APART, moved, pack)
+        send[ZP:ZROWS, :] = pack.astype(bf16)
+    sort_pair("sec", down, up, ua, ub)
+
+
+def flux_kernel(part, ua_r, ub_r, across_r, grid, ext, da, db, rows_s):
+    got = [ref[4 * LANES : CROWS, :].astype(f32) for ref in (ua_r, ub_r, across_r)]
     turned = got[0] + got[1] + got[2]
     halo = jnp.concatenate([turned[0:8], jnp.zeros((LANES - 16, LANES), f32), turned[8:16]], axis=0).T
     for c in range(5):
@@ -382,7 +406,7 @@
             at = c * LANES + f * NX
             total = part[at : at + NX, :]
             if c < 4:
-                for ref in (up_r, down_r, across_r):
+                for ref in (ua_r, ub_r, across_r):
                     total = total + ref[at : at + NX, :].astype(f32)
             else:
                 total = total + halo[f * NX : (f + 1) * NX]
@@ -390,8 +414,9 @@
             ext[f, :, c * LANES : (c + 1) * LANES] = total
             rows_s[0, c * 16 + f * 4 : c * 16 + f * 4 + 4, :] = total[0:4]
             rows_s[1, c * 16 + f * 4 : c * 16 + f * 4 + 4, :] = total[NX - 4 : NX]
-    dw[...] = rows_s[0].astype(bf16)
-    de[...] = rows_s[1].astype(bf16)
+    first = jnp.where(even("gx"), 1, 0)
+    da[...] = rows_s[first].astype(bf16)
+    db[...] = rows_s[1 - first].astype(bf16)
 
 
 def lane_next(value, lane):
@@ -451,7 +476,7 @@
 def middle_kernel(
     tr, cu, yn_r, ys_r, xe_r, xw_r, table, after, after_zu, after_zd, g0, vel, g1, g2, grid, done, xs
 ):
-    south, north = field_packs(yn_r), field_packs(ys_r)
+    south, north = field_pack(yn_r), field_pack(ys_r)
     low = lane_ids((NX, LANES)) < 64
     edge_south, edge_north = edge_packs(xw_r, xe_r)
     edge_low = lane_ids((8, LANES)) < 64
@@ -555,8 +580,8 @@
 
 
 def outer_kernel(
-    tr, g0, vel, g1, g2, grid, zu_r, zd_r, up_r, down_r, ext, middle, after, out, ocean_flux, s0, sv, s1, s2,
-    b0, bv, b1, b2, top, bottom, sems,
+    tr, g0, vel, g1, g2, grid, zu_r, zd_r, ua_r, ub_r, ext, middle, after, out, ocean_flux, s0, sv, s1, s2,
+    up_r, down_r, b0, bv, b1, b2, top, bottom, sems,
 ):
     sec = lax.axis_index("sec")
     writes = [
@@ -565,12 +590,12 @@
         pltpu.make_async_copy(bottom, out.at[:, pl.ds(7, 3)], sems.at[2]),
     ]
     start(*writes[:2])
+    sort_pair("sec", ua_r.at[pl.ds(CROWS, ZROWS - CROWS)], ub_r.at[pl.ds(CROWS, ZROWS - CROWS)], up_r, down_r)
     low = lane_ids((NX, LANES)) < 64
 
     def halo_planes(got, z, face, tracers, velocities):
-        z_south = (got[ZS:ZN, :].astype(f32),)
-        z_north = (got[ZN:ZROWS, :].astype(f32),)
-        near = [got[CROWS + c * 16 : CROWS + (c + 1) * 16, :].astype(f32) for c in range(5)]
+        pack = got[ZP - CROWS : ZROWS - CROWS, :].astype(f32)
+        near = [got[c * 16 : (c + 1) * 16, :].astype(f32) for c in range(5)]
 
         def put(target, body, plane, at, scale):
             for col in range(4):
@@ -578,7 +603,7 @@
                 target[col, OWN, :] = value * (scale * grid[MASK, col, OWN, :])
             if plane is None:
                 return
-            col4 = jnp.where(low, unpack_north(z_north, plane), unpack_south(z_south, plane))
+            col4 = jnp.where(low, unpack_north(pack, plane), unpack_south(pack, plane + APART))
             target[4, OWN, :] = col4 * (scale * grid[MASK, 4, OWN, :])
             for col in range(5):
                 for k, row in enumerate(at):
@@ -663,11 +688,12 @@
 
 
 def surface_kernel(
-    unfinished, tr, s0, sv, s1, s2, g0, vel, g1, g2, grid, de_r, dw_r, out, e0, ev, e1, e2, edge, sems
+    unfinished, tr, s0, sv, s1, s2, g0, vel, g1, g2, grid, da_r, db_r, out, e0, ev, e1, e2, edge, sems
 ):
     @pl.when(lax.axis_index("sec") == 0)
     def _():
-        halo = (de_r[...].astype(f32), dw_r[...].astype(f32))
+        got_a, got_b = da_r[...].astype(f32), db_r[...].astype(f32)
+        halo = (jnp.where(even("gx"), got_b, got_a), jnp.where(even("gx"), got_a, got_b))
         for c in range(2):
             for target, source, planes, groups in (
                 (e0, s0, 1, (8, 16, 32, 40)),
@@ -727,17 +753,26 @@
     return lax.ppermute(value, axis, [(i, (i + step) % count) for i in range(count)])
 
 
+def swapped(a, b, axis):
+    count = lax.axis_size(axis)
+    one = [(i, i ^ 1) for i in range(count)]
+    other = [(i, (i + (1 if i % 2 else -1)) % count) for i in range(count)]
+    return lax.ppermute(a, axis, one), lax.ppermute(b, axis, other)
+
+
 def on_device(air_surface, remap_weights, sources, live_count, land_sea, tracers, currents):
     src = hbm(jnp.transpose(sources[:, :, 0, :], (1, 2, 0)))
     live = hbm(jnp.transpose(live_count, (1, 2, 0)))
     land = hbm(jnp.transpose(land_sea, (1, 0)))
     dma = pltpu.SemaphoreType.DMA
 
-    yn, ys, flux, table = call(
+    ya, yb, flux, table = call(
         pack_y_kernel,
         [HBM] * 7,
         [((YROWS, LANES), bf16), ((YROWS, LANES), bf16), ((NT, 4, NX, LANES), bf16), ((16, LANES), f32)],
         [
+            pltpu.VMEM((YROWS, LANES), bf16),
+            pltpu.VMEM((YROWS, LANES), bf16),
             pltpu.VMEM((NT, 2, NX), jnp.int32),
             pltpu.VMEM((NT, 1, NX), jnp.int32),
             pltpu.VMEM((NT, NX), jnp.int32),
@@ -751,8 +786,7 @@
         "pack_y",
         6_000_000,
     )(hbm(air_surface.reshape(5, NX * NT, LANES)), src, live, land, hbm(remap_weights), hbm(tracers), hbm(currents))
-    yn_r = shifted(yn, "gy", 1)
-    ys_r = shifted(ys, "gy", -1)
+    ya_r, yb_r = swapped(ya, yb, "gy")
 
     zu, zd = call(
         pack_z_kernel,
@@ -765,16 +799,16 @@
     zu_r = shifted(zu, "sec", -1)
     zd_r = shifted(zd, "sec", 1)
 
-    xe, xw = call(
+    xa, xb, yn_r, ys_r = call(
         pack_x_kernel,
         [VMEM, VMEM, VMEM, VMEM, ANY, ANY],
-        [((XROWS, LANES), bf16)] * 2,
-        [pltpu.VMEM((XP, LANES), f32), pltpu.VMEM((2, 2, 2, NL, 8, 512), f32), dma((4,))],
+        [((XROWS, LANES), bf16)] * 2 + [((YROWS, LANES), bf16)] * 2,
+        [pltpu.VMEM((XROWS, LANES), bf16)] * 2
+        + [pltpu.VMEM((XP, LANES), f32), pltpu.VMEM((2, 2, 2, NL, 8, 512), f32), dma((4,))],
         "pack_x",
         3_000_000,
-    )(flux, yn_r, ys_r, table, tracers, currents)
-    xe_r = shifted(xe, "gx", 1)
-    xw_r = shifted(xw, "gx", -1)
+    )(flux, ya_r, yb_r, table, tracers, currents)
+    xa_r, xb_r = swapped(xa, xb, "gx")
 
     first_part, wedge = call(
         remap_kernel,
@@ -786,18 +820,18 @@
         ],
         "remap",
         18_000_000,
-    )(flux, yn_r, ys_r, table, remap_weights, xe)
-    part, up, down, across = call(
+    )(flux, yn_r, ys_r, table, remap_weights, xa)
+    part, ua, ub, across, xe_r, xw_r = call(
         rim_kernel,
         [VMEM] * 7,
-        [((5 * LANES, LANES), f32), ((ZROWS, LANES), bf16), ((ZROWS, LANES), bf16), ((CROWS, LANES), bf16)],
-        [pltpu.VMEM((2, XP, LANES), f32), pltpu.VMEM((80, LANES), f32)],
+        [((5 * LANES, LANES), f32)]
+        + [((rows, LANES), bf16) for rows in (ZROWS, ZROWS, CROWS, XROWS, XROWS)],
+        [pltpu.VMEM((ZROWS, LANES), bf16)] * 2 + [pltpu.VMEM((2, XP, LANES), f32), pltpu.VMEM((80, LANES), f32)],
         "rim",
         4_000_000,
-    )(first_part, wedge, yn_r, ys_r, xe_r, xw_r, table)
-    up_r = shifted(up, "sec", -1)
-    down_r = shifted(down, "sec", 1)
+    )(first_part, wedge, yn_r, ys_r, xa_r, xb_r, table)
     across_r = shifted(across, "sec", 2)
+    ua_r, ub_r = swapped(ua, ub, "sec")
 
     plane = (5, 56, LANES)
     g0, vel, g1, g2, grid, middle = call(
@@ -818,27 +852,27 @@
         20_000_000,
     )(tracers, currents, yn_r, ys_r, xe_r, xw_r, table, across, zu_r, zd_r)
 
-    ext, de, dw = call(
+    ext, da, db = call(
         flux_kernel,
         [VMEM] * 5,
         [((4, NX, 5 * LANES), f32), ((80, LANES), bf16), ((80, LANES), bf16)],
         [pltpu.VMEM((2, 80, LANES), f32)],
         "flux_sum",
         3_000_000,
-    )(part, up_r, down_r, across_r, grid)
-    de_r = shifted(de, "gx", 1)
-    dw_r = shifted(dw, "gx", -1)
+    )(part, ua_r, ub_r, across_r, grid)
+    da_r, db_r = swapped(da, db, "gx")
 
     unfinished, ocean_flux, s0, sv, s1, s2 = call(
         outer_kernel,
         [VMEM] * 12 + [ANY],
         [((2, NL, NX, 512), f32), ((4, NX, 512), f32)] + [((2, count) + plane, f32) for count in (3, 2, 3, 3)],
-        [pltpu.VMEM((2, count) + plane, f32) for count in (3, 2, 3, 3)]
+        [pltpu.VMEM((ZROWS - CROWS, LANES), bf16)] * 2
+        + [pltpu.VMEM((2, count) + plane, f32) for count in (3, 2, 3, 3)]
         + [pltpu.VMEM((2, 4, NX, 512), f32), pltpu.VMEM((2, 3, NX, 512), f32), dma((5,))],
         "outer",
         18_000_000,
         [HBM, HBM] + [VMEM] * 4,
-    )(tracers, g0, vel, g1, g2, grid, zu_r, zd_r, up_r, down_r, ext, middle, de)
+    )(tracers, g0, vel, g1, g2, grid, zu_r, zd_r, ua_r, ub_r, ext, middle, da)
 
     (tracers_out,) = call(
         surface_kernel,
@@ -850,7 +884,7 @@
         8_000_000,
         [HBM],
         {0: 0},
-    )(unfinished, tracers, s0, sv, s1, s2, g0, vel, g1, g2, grid, de_r, dw_r)
+    )(unfinished, tracers, s0, sv, s1, s2, g0, vel, g1, g2, grid, da_r, db_r)
     return (tracers_out, ocean_flux)
 
 

time: 43.5 us -> 41.4 us (0.952)
  the two profiles are of different devices: /device:TPU:32 before, /device:TPU:8 now
where the time goes in v4:
time: 41.4 us; the launch traced here: 41.3 us
  starting transfers between devices  21.8 us (53%)
  Pallas kernels  16 us (39%)
  waiting for transfers between devices  2.63 us (6%)
  between operations  0.93 us (2%)
    ppermute x8, starting transfers between devices, swapped(): return (lax.ppermute(a, axis, one), lax.ppermute(b, axis, other))  18.3 us
    pallas_call x1, Pallas kernels, on_device(): call(middle_kernel, [VMEM] * 7 + [ANY] * 3, [((2, NL) + plane, f32), ((2,...  3.91 us
    pallas_call x1, Pallas kernels, on_device(): call(remap_kernel, [VMEM] * 5 + [ANY], [((5 * LANES, LANES), f32), ((2, N...  3.78 us
    pallas_call x1, Pallas kernels, on_device(): call(outer_kernel, [VMEM] * 12 + [ANY], [((2, NL, NX, 512), f32), ((4, NX...  3.57 us
    ppermute x3, starting transfers between devices, shifted(): lax.ppermute(value, axis, [(i, (i + step) % count) for i in range(count)])  3.47 us
    pallas_call x1, Pallas kernels, on_device(): call(pack_y_kernel, [HBM] * 7, [((YROWS, LANES), bf16), ((YROWS, LANES),...  2.11 us
    ppermute x3, waiting for transfers between devices, shifted(): lax.ppermute(value, axis, [(i, (i + step) % count) for i in range(count)])  1.97 us
    pallas_call x1, Pallas kernels, on_device(): call(surface_kernel, [HBM] + [VMEM] * 12, [((2, NL, NX, 512), f32)], [plt...  1.33 us
  transfers between devices with their start and end apart: 11, of which 2 were waited for; matrix products, arithmetic and copies ran while one was open for 0% of the time, Pallas kernels for 30%

profile of v4, /device:TPU:8, one launch (start us, length us, event | category | flops | bytes accessed | tf_op | source)
XLA Modules:
  0.0 41.3 jit_solution(10990928263055561148)
XLA Ops:
  0.6 0.0 slice-start
  0.6 0.0 copy-start
  0.7 0.0 copy-start.1
  0.7 0.0 slice-start.1
  0.7 2.1 %pack_y.1 = (bf16[496,128]{1,0:T(8,128)(2,1)S(1)}, bf16[496,128]{1,0:T(8,128)(2,1)S(1)}, bf16[4,4,32,128]{3,2,1,0:T(8,128)(2,1)S(1)}, f32[16,128]{1,0:T(8,128)S(1)}) custom-call(f32[5,128,128]{2,1,0:T(8,128)} %bitcast.8, s32[4,2,32]{2,1,0:T(2,128)} %bitcast.9, s32[4,1,32]{2,1,0:T(1,128)} %bitcast.10, s32[4,32]{1,0:T(4,128)} %bitcast.11, ...), custom_call_target="tpu_custom_call" | custom-call | bytes 6000000 | tf_op jit(solution)/shard_map/pack_y/pallas_call | solution.py:769
  2.8 0.1 collective-permute-start
  2.9 6.4 %collective-permute-start.1 = (bf16[496,128]{1,0:T(8,128)(2,1)S(1)}, bf16[496,128]{1,0:T(8,128)(2,1)S(1)}, u32[]{:S(2)}, u32[]{:S(2)}) collective-permute-start(bf16[496,128]{1,0:T(8,128)(2,1)S(1)} %get-tuple-element.37), channel_id=1, source_target_pairs={{0,7},{1,2},{2,1},{3,4},{4,3},{5,6},{6,5},{7,0},{8,15},{9,10},{10,... | collective-permute-start | bytes 380936 | tf_op jit(solution)/shard_map/ppermute | solution.py:760
  9.3 0.0 copy-done
  9.3 0.0 copy-done.1
  9.3 0.3 pack_z.1
  9.6 2.8 %collective-permute-start.4 = (bf16[10,32,512]{2,1,0:T(8,128)(2,1)S(1)}, bf16[10,32,512]{2,1,0:T(8,128)(2,1)S(1)}, u32[]{:S(2)}, u32[]{:S(2)}) collective-permute-start(bf16[10,32,512]{2,1,0:T(8,128)(2,1)S(1)} %get-tuple-element.48), channel_id=1, source_target_pairs={{0,192},{64,0},{128,64},{192,128},{1,193},{65,1},{129,65},{193,129... | collective-permute-start | bytes 983048 | tf_op jit(solution)/shard_map/ppermute | solution.py:753
  12.5 0.0 collective-permute-start.5
  12.5 0.0 collective-permute-done.ya_r
  12.5 0.6 %collective-permute-done.1.yb_r = bf16[496,128]{1,0:T(8,128)(2,1)S(1)} collective-permute-done((bf16[496,128]{1,0:T(8,128)(2,1)S(1)}, bf16[496,128]{1,0:T(8,128)(2,1)S(1)}, u32[]{:S(2)}, u32[]{:S(2)}) %collective-permute-start.1) | collective-permute-done | bytes 127008 | tf_op jit(solution)/shard_map/ppermute | solution.py:760
  13.1 0.4 pack_x.1
  13.5 0.5 %collective-permute-start.2 = (bf16[496,128]{1,0:T(8,128)(2,1)S(1)}, bf16[496,128]{1,0:T(8,128)(2,1)S(1)}, u32[]{:S(2)}, u32[]{:S(2)}) collective-permute-start(bf16[496,128]{1,0:T(8,128)(2,1)S(1)} %get-tuple-element.41.after_x), channel_id=1, source_target_pairs={{0,8},{8,0},{16,24},{24,16},{32,40},{40,32},{48,56},{56,48},{1,9},... | collective-permute-start | bytes 380936 | tf_op jit(solution)/shard_map/ppermute | solution.py:760
  14.0 2.4 %collective-permute-start.3 = (bf16[496,128]{1,0:T(8,128)(2,1)S(1)}, bf16[496,128]{1,0:T(8,128)(2,1)S(1)}, u32[]{:S(2)}, u32[]{:S(2)}) collective-permute-start(bf16[496,128]{1,0:T(8,128)(2,1)S(1)} %get-tuple-element.44), channel_id=1, source_target_pairs={{0,56},{8,16},{16,8},{24,32},{32,24},{40,48},{48,40},{56,0},{1,57}... | collective-permute-start | bytes 380936 | tf_op jit(solution)/shard_map/ppermute | solution.py:760
  16.5 0.0 slice-done
  16.5 0.0 slice-done.1
  16.5 3.8 %remap.1 = (f32[640,128]{1,0:T(8,128)S(1)}, bf16[2,4,2,128,128]{4,3,2,1,0:T(8,128)(2,1)S(1)}) custom-call(bf16[4,4,32,128]{3,2,1,0:T(8,128)(2,1)S(1)} %get-tuple-element.35.flux, bf16[496,128]{1,0:T(8,128)(2,1)S(1)} %get-tuple-element.39.yn_r, bf16[496,128]{1,0:T(8,128)(2,1)S(1)} %get-tuple-element.40.ys_r, f32[16,128]{1,0:T(8,128)S(1)} %get-tuple-element.38.table.after, ...), custom_call_target="tpu_custom_call" | custom-call | bytes 18000000 | tf_op jit(solution)/shard_map/remap/pallas_call | solution.py:813
  20.2 0.0 collective-permute-done.2.xa_r
  20.3 0.0 collective-permute-done.3.xb_r
  20.3 0.4 %rim.1 = (f32[640,128]{1,0:T(8,128)S(1)}, bf16[640,128]{1,0:T(8,128)(2,1)S(1)}, bf16[640,128]{1,0:T(8,128)(2,1)S(1)}, bf16[528,128]{1,0:T(8,128)(2,1)S(1)}, bf16...) custom-call(f32[640,128]{1,0:T(8,128)S(1)} %get-tuple-element.42.first_part, ...), custom_call_target="tpu_custom_call" | custom-call | bytes 4000000 | tf_op jit(solution)/shard_map/rim/pallas_call | solution.py:824
  20.7 1.6 %collective-permute-start.6 = (bf16[640,128]{1,0:T(8,128)(2,1)S(1)}, bf16[640,128]{1,0:T(8,128)(2,1)S(1)}, u32[]{:S(2)}, u32[]{:S(2)}) collective-permute-start(bf16[640,128]{1,0:T(8,128)(2,1)S(1)} %get-tuple-element.55), channel_id=1, source_target_pairs={{0,64},{64,0},{128,192},{192,128},{1,65},{65,1},{129,193},{193,129... | collective-permute-start | bytes 491528 | tf_op jit(solution)/shard_map/ppermute | solution.py:760
  22.3 2.1 %collective-permute-start.7 = (bf16[640,128]{1,0:T(8,128)(2,1)S(1)}, bf16[640,128]{1,0:T(8,128)(2,1)S(1)}, u32[]{:S(2)}, u32[]{:S(2)}) collective-permute-start(bf16[640,128]{1,0:T(8,128)(2,1)S(1)} %get-tuple-element.56), channel_id=1, source_target_pairs={{0,192},{64,128},{128,64},{192,0},{1,193},{65,129},{129,65},{193,1... | collective-permute-start | bytes 491528 | tf_op jit(solution)/shard_map/ppermute | solution.py:760
  24.4 0.6 %collective-permute-start.8 = (bf16[528,128]{1,0:T(8,128)(2,1)S(1)}, bf16[528,128]{1,0:T(8,128)(2,1)S(1)}, u32[]{:S(2)}, u32[]{:S(2)}) collective-permute-start(bf16[528,128]{1,0:T(8,128)(2,1)S(1)} %get-tuple-element.47.after), channel_id=1, source_target_pairs={{0,128},{64,192},{128,0},{192,64},{1,129},{65,193},{129,1},{193,65... | collective-permute-start | bytes 405512 | tf_op jit(solution)/shard_map/ppermute | solution.py:753
  25.0 0.0 collective-permute-done.4.after_zu.zu_r
  25.0 0.0 collective-permute-done.5.after_zd.zd_r
  25.0 3.9 %middle.1 = (f32[2,10,5,56,128]{4,3,2,1,0:T(8,128)S(1)}, f32[2,10,5,56,128]{4,3,2,1,0:T(8,128)S(1)}, f32[2,8,5,56,128]{4,3,2,1,0:T(8,128)S(1)}, f32[2,6,5,56,128...) custom-call(f32[2,10,32,512]{3,2,1,0:T(8,128)S(1)} %copy-done, ...), custom_call_target="tpu_custom_call" | custom-call | bytes 20000000 | tf_op jit(solution)/shard_map/middle/pallas_call | solution.py:837
  28.9 2.0 %collective-permute-done.8.across_r = bf16[528,128]{1,0:T(8,128)(2,1)S(1)} collective-permute-done((bf16[528,128]{1,0:T(8,128)(2,1)S(1)}, bf16[528,128]{1,0:T(8,128)(2,1)S(1)}, u32[]{:S(2)}, u32[]{:S(2)}) %collective-permute-start.8) | collective-permute-done | bytes 135200 | tf_op jit(solution)/shard_map/ppermute | solution.py:753
  30.9 0.0 collective-permute-done.6.ua_r
  30.9 0.0 collective-permute-done.7.ub_r
  30.9 0.1 flux_sum.1
  31.0 1.2 %collective-permute-start.10 = (bf16[80,128]{1,0:T(8,128)(2,1)S(1)}, bf16[80,128]{1,0:T(8,128)(2,1)S(1)}, u32[]{:S(2)}, u32[]{:S(2)}) collective-permute-start(bf16[80,128]{1,0:T(8,128)(2,1)S(1)} %get-tuple-element.66), channel_id=1, source_target_pairs={{0,56},{8,16},{16,8},{24,32},{32,24},{40,48},{48,40},{56,0},{1,57}... | collective-permute-start | bytes 61448 | tf_op jit(solution)/shard_map/ppermute | solution.py:760
  32.2 4.0 %collective-permute-start.9 = (bf16[80,128]{1,0:T(8,128)(2,1)S(1)}, bf16[80,128]{1,0:T(8,128)(2,1)S(1)}, u32[]{:S(2)}, u32[]{:S(2)}) collective-permute-start(bf16[80,128]{1,0:T(8,128)(2,1)S(1)} %get-tuple-element.60.after), channel_id=1, source_target_pairs={{0,8},{8,0},{16,24},{24,16},{32,40},{40,32},{48,56},{56,48},{1,9},... | collective-permute-start | bytes 61448 | tf_op jit(solution)/shard_map/ppermute | solution.py:760
  36.3 3.6 %outer.1 = (f32[2,10,32,512]{3,2,1,0:T(8,128)}, f32[4,32,512]{2,1,0:T(8,128)}, f32[2,3,5,56,128]{4,3,2,1,0:T(8,128)S(1)}, f32[2,2,5,56,128]{4,3,2,1,0:T(8,128)S(...) custom-call(f32[2,10,32,512]{3,2,1,0:T(8,128)S(1)} %copy-done, ...), custom_call_target="tpu_custom_call" | custom-call | bytes 18000000 | tf_op jit(solution)/shard_map/outer/pallas_call | solution.py:865
  39.8 0.0 collective-permute-done.10.db_r
  39.8 0.0 collective-permute-done.9.da_r
  39.9 1.3 %surface.1 = f32[2,10,32,512]{3,2,1,0:T(8,128)} custom-call(f32[2,10,32,512]{3,2,1,0:T(8,128)} %get-tuple-element.61.unfinished, f32[2,10,32,512]{3,2,1,0:T(8,128)S(1)} %copy-done, f32[2,3,5,56,128]{4,3,2,1,0:T(8,128)S(1)} %get-tuple-element.62.s0, f32[2,2,5,56,128]{4,3,2,1,0:T(8,128)S(1)} %get-tuple-element.63.sv, ...), custom_call_target="tpu_custom_call", output_to_operand_aliasing={{}: (0, {})} | custom-call | bytes 8000000 | tf_op jit(solution)/shard_map/surface/pallas_call | solution.py:877
  (1 shorter events, 0.0 us)
Async XLA Ops:
  0.6 15.8 %slice-start = ((s8[8388608]{0:T(1024)(128)(4,1)}), s8[4194304]{0:T(1024)(128)(4,1)S(1)}, s32[]{:S(2)}) async-start(s8[8388608]{0:T(1024)(128)(4,1)} %bitcast.6), calls=%async_computation | async-start | bytes 8388608
  0.6 8.7 %copy-start = (f32[2,10,32,512]{3,2,1,0:T(8,128)S(1)}, f32[2,10,32,512]{3,2,1,0:T(8,128)}, u32[]{:S(2)}) copy-start(f32[2,10,32,512]{3,2,1,0:T(8,128)} %tr.11) | copy-start | bytes 3932164
  0.7 8.6 %copy-start.1 = (f32[2,10,32,512]{3,2,1,0:T(8,128)S(1)}, f32[2,10,32,512]{3,2,1,0:T(8,128)}, u32[]{:S(2)}) copy-start(f32[2,10,32,512]{3,2,1,0:T(8,128)} %cu.7) | copy-start | bytes 3932164
  0.7 15.8 %slice-start.1 = ((s8[8388608]{0:T(1024)(128)(4,1)}), s8[4194304]{0:T(1024)(128)(4,1)S(1)}, s32[]{:S(2)}) async-start(s8[8388608]{0:T(1024)(128)(4,1)} %bitcast.6), calls=%async_computation.1 | async-start | bytes 8388608
  2.8 9.7 %collective-permute-start = (bf16[496,128]{1,0:T(8,128)(2,1)S(1)}, bf16[496,128]{1,0:T(8,128)(2,1)S(1)}, u32[]{:S(2)}, u32[]{:S(2)}) collective-permute-start(bf16[496,128]{1,0:T(8,128)(2,1)S(1)} %get-tuple-element.36), channel_id=1, source_target_pairs={{0,1},{1,0},{2,3},{3,2},{4,5},{5,4},{6,7},{7,6},{8,9},{9,8},{10,11... | collective-permute-start | bytes 380936 | tf_op jit(solution)/shard_map/ppermute | solution.py:760
  2.9 10.2 %collective-permute-start.1 = (bf16[496,128]{1,0:T(8,128)(2,1)S(1)}, bf16[496,128]{1,0:T(8,128)(2,1)S(1)}, u32[]{:S(2)}, u32[]{:S(2)}) collective-permute-start(bf16[496,128]{1,0:T(8,128)(2,1)S(1)} %get-tuple-element.37), channel_id=1, source_target_pairs={{0,7},{1,2},{2,1},{3,4},{4,3},{5,6},{6,5},{7,0},{8,15},{9,10},{10,... | collective-permute-start | bytes 380936 | tf_op jit(solution)/shard_map/ppermute | solution.py:760
  9.6 15.4 %collective-permute-start.4 = (bf16[10,32,512]{2,1,0:T(8,128)(2,1)S(1)}, bf16[10,32,512]{2,1,0:T(8,128)(2,1)S(1)}, u32[]{:S(2)}, u32[]{:S(2)}) collective-permute-start(bf16[10,32,512]{2,1,0:T(8,128)(2,1)S(1)} %get-tuple-element.48), channel_id=1, source_target_pairs={{0,192},{64,0},{128,64},{192,128},{1,193},{65,1},{129,65},{193,129... | collective-permute-start | bytes 983048 | tf_op jit(solution)/shard_map/ppermute | solution.py:753
  12.5 12.5 %collective-permute-start.5 = (bf16[10,32,512]{2,1,0:T(8,128)(2,1)S(1)}, bf16[10,32,512]{2,1,0:T(8,128)(2,1)S(1)}, u32[]{:S(2)}, u32[]{:S(2)}) collective-permute-start(bf16[10,32,512]{2,1,0:T(8,128)(2,1)S(1)} %get-tuple-element.49), channel_id=1, source_target_pairs={{0,64},{64,128},{128,192},{192,0},{1,65},{65,129},{129,193},{193,1... | collective-permute-start | bytes 983048 | tf_op jit(solution)/shard_map/ppermute | solution.py:753
  13.5 6.7 %collective-permute-start.2 = (bf16[496,128]{1,0:T(8,128)(2,1)S(1)}, bf16[496,128]{1,0:T(8,128)(2,1)S(1)}, u32[]{:S(2)}, u32[]{:S(2)}) collective-permute-start(bf16[496,128]{1,0:T(8,128)(2,1)S(1)} %get-tuple-element.41.after_x), channel_id=1, source_target_pairs={{0,8},{8,0},{16,24},{24,16},{32,40},{40,32},{48,56},{56,48},{1,9},... | collective-permute-start | bytes 380936 | tf_op jit(solution)/shard_map/ppermute | solution.py:760
  14.0 6.2 %collective-permute-start.3 = (bf16[496,128]{1,0:T(8,128)(2,1)S(1)}, bf16[496,128]{1,0:T(8,128)(2,1)S(1)}, u32[]{:S(2)}, u32[]{:S(2)}) collective-permute-start(bf16[496,128]{1,0:T(8,128)(2,1)S(1)} %get-tuple-element.44), channel_id=1, source_target_pairs={{0,56},{8,16},{16,8},{24,32},{32,24},{40,48},{48,40},{56,0},{1,57}... | collective-permute-start | bytes 380936 | tf_op jit(solution)/shard_map/ppermute | solution.py:760
  20.7 10.2 %collective-permute-start.6 = (bf16[640,128]{1,0:T(8,128)(2,1)S(1)}, bf16[640,128]{1,0:T(8,128)(2,1)S(1)}, u32[]{:S(2)}, u32[]{:S(2)}) collective-permute-start(bf16[640,128]{1,0:T(8,128)(2,1)S(1)} %get-tuple-element.55), channel_id=1, source_target_pairs={{0,64},{64,0},{128,192},{192,128},{1,65},{65,1},{129,193},{193,129... | collective-permute-start | bytes 491528 | tf_op jit(solution)/shard_map/ppermute | solution.py:760
  22.3 8.6 %collective-permute-start.7 = (bf16[640,128]{1,0:T(8,128)(2,1)S(1)}, bf16[640,128]{1,0:T(8,128)(2,1)S(1)}, u32[]{:S(2)}, u32[]{:S(2)}) collective-permute-start(bf16[640,128]{1,0:T(8,128)(2,1)S(1)} %get-tuple-element.56), channel_id=1, source_target_pairs={{0,192},{64,128},{128,64},{192,0},{1,193},{65,129},{129,65},{193,1... | collective-permute-start | bytes 491528 | tf_op jit(solution)/shard_map/ppermute | solution.py:760
  24.4 6.5 %collective-permute-start.8 = (bf16[528,128]{1,0:T(8,128)(2,1)S(1)}, bf16[528,128]{1,0:T(8,128)(2,1)S(1)}, u32[]{:S(2)}, u32[]{:S(2)}) collective-permute-start(bf16[528,128]{1,0:T(8,128)(2,1)S(1)} %get-tuple-element.47.after), channel_id=1, source_target_pairs={{0,128},{64,192},{128,0},{192,64},{1,129},{65,193},{129,1},{193,65... | collective-permute-start | bytes 405512 | tf_op jit(solution)/shard_map/ppermute | solution.py:753
  31.0 8.8 %collective-permute-start.10 = (bf16[80,128]{1,0:T(8,128)(2,1)S(1)}, bf16[80,128]{1,0:T(8,128)(2,1)S(1)}, u32[]{:S(2)}, u32[]{:S(2)}) collective-permute-start(bf16[80,128]{1,0:T(8,128)(2,1)S(1)} %get-tuple-element.66), channel_id=1, source_target_pairs={{0,56},{8,16},{16,8},{24,32},{32,24},{40,48},{48,40},{56,0},{1,57}... | collective-permute-start | bytes 61448 | tf_op jit(solution)/shard_map/ppermute | solution.py:760
  32.2 7.6 %collective-permute-start.9 = (bf16[80,128]{1,0:T(8,128)(2,1)S(1)}, bf16[80,128]{1,0:T(8,128)(2,1)S(1)}, u32[]{:S(2)}, u32[]{:S(2)}) collective-permute-start(bf16[80,128]{1,0:T(8,128)(2,1)S(1)} %get-tuple-element.60.after), channel_id=1, source_target_pairs={{0,8},{8,0},{16,24},{24,16},{32,40},{40,32},{48,56},{56,48},{1,9},... | collective-permute-start | bytes 61448 | tf_op jit(solution)/shard_map/ppermute | solution.py:760

commit v5 on v4

--- a/solution.py
+++ b/solution.py
@@ -200,7 +200,7 @@
     return [jnp.concatenate([east[4 * k : 4 * k + 4], west[4 * k : 4 * k + 4]], axis=0) for k in range(2)]
 
 
-def pack_x_kernel(flux, ya_r, yb_r, table, tr, cu, xa, xb, yn_r, ys_r, xe, xw, rows_s, edge, sems):
+def pack_x_kernel(flux, yb_r, ya_r, table, tr, cu, xa, xb, yn_r, ys_r, xe, xw, rows_s, edge, sems):
     copies = []
     for k, source in enumerate((tr, cu)):
         copies.append(pltpu.make_async_copy(source.at[:, :, pl.ds(0, 8), :], edge.at[0, k], sems.at[2 * k]))
@@ -319,7 +319,7 @@
 
 
 def rim_kernel(
-    first_part, wedge, yn_r, ys_r, xa_r, xb_r, table, part, ua, ub, across, xe_r, xw_r, up, down, xs, rows_s
+    first_part, wedge, yn_r, ys_r, xb_r, xa_r, table, part, ua, ub, across, xe_r, xw_r, up, down, xs, rows_s
 ):
     sort_pair("gx", xa_r, xb_r, xw_r, xe_r)
     part[...] = first_part[...]
@@ -688,7 +688,7 @@
 
 
 def surface_kernel(
-    unfinished, tr, s0, sv, s1, s2, g0, vel, g1, g2, grid, da_r, db_r, out, e0, ev, e1, e2, edge, sems
+    unfinished, tr, s0, sv, s1, s2, g0, vel, g1, g2, grid, db_r, da_r, out, e0, ev, e1, e2, edge, sems
 ):
     @pl.when(lax.axis_index("sec") == 0)
     def _():
@@ -757,7 +757,8 @@
     count = lax.axis_size(axis)
     one = [(i, i ^ 1) for i in range(count)]
     other = [(i, (i + (1 if i % 2 else -1)) % count) for i in range(count)]
-    return lax.ppermute(a, axis, one), lax.ppermute(b, axis, other)
+    b = lax.ppermute(b, axis, other)
+    return lax.ppermute(a, axis, one), b
 
 
 def on_device(air_surface, remap_weights, sources, live_count, land_sea, tracers, currents):
@@ -807,7 +808,7 @@
         + [pltpu.VMEM((XP, LANES), f32), pltpu.VMEM((2, 2, 2, NL, 8, 512), f32), dma((4,))],
         "pack_x",
         3_000_000,
-    )(flux, ya_r, yb_r, table, tracers, currents)
+    )(flux, yb_r, ya_r, table, tracers, currents)
     xa_r, xb_r = swapped(xa, xb, "gx")
 
     first_part, wedge = call(
@@ -829,7 +830,7 @@
         [pltpu.VMEM((ZROWS, LANES), bf16)] * 2 + [pltpu.VMEM((2, XP, LANES), f32), pltpu.VMEM((80, LANES), f32)],
         "rim",
         4_000_000,
-    )(first_part, wedge, yn_r, ys_r, xa_r, xb_r, table)
+    )(first_part, wedge, yn_r, ys_r, xb_r, xa_r, table)
     across_r = shifted(across, "sec", 2)
     ua_r, ub_r = swapped(ua, ub, "sec")
 
@@ -884,7 +885,7 @@
         8_000_000,
         [HBM],
         {0: 0},
-    )(unfinished, tracers, s0, sv, s1, s2, g0, vel, g1, g2, grid, da_r, db_r)
+    )(unfinished, tracers, s0, sv, s1, s2, g0, vel, g1, g2, grid, db_r, da_r)
     return (tracers_out, ocean_flux)
 
 

time: 41.4 us -> 39.9 us (0.964)
  starting transfers between devices: 21.8 us -> 19.3 us
  waiting for transfers between devices: 2.63 us -> 3.25 us
    ppermute x8, starting transfers between devices: 18.3 us -> 15.9 us  [the longest x4 11.7 us: swapped(): b = lax.ppermute(b, axis, other)]
    ppermute x3, waiting for transfers between devices: 1.97 us -> 2.4 us  [shifted(): lax.ppermute(value, axis, [(i, (i + step) % count) for i in range(count)])]
  transfers between devices with their start and end apart: 11 -> 11, of which waited for: 2 -> 3; matrix products, arithmetic and copies ran while one was open for 0% -> 0% of each run, Pallas kernels for 30% -> 31%
where the time goes in v5:
time: 39.9 us; the launch traced here: 39.5 us
  starting transfers between devices  19.3 us (48%)
  Pallas kernels  16 us (40%)
  waiting for transfers between devices  3.25 us (8%)
  between operations  0.92 us (2%)
    ppermute x4, starting transfers between devices, swapped(): b = lax.ppermute(b, axis, other)  11.7 us
    ppermute x4, starting transfers between devices, swapped(): return (lax.ppermute(a, axis, one), b)  4.11 us
    pallas_call x1, Pallas kernels, on_device(): call(middle_kernel, [VMEM] * 7 + [ANY] * 3, [((2, NL) + plane, f32), ((2,...  3.9 us
    pallas_call x1, Pallas kernels, on_device(): call(remap_kernel, [VMEM] * 5 + [ANY], [((5 * LANES, LANES), f32), ((2, N...  3.78 us
    pallas_call x1, Pallas kernels, on_device(): call(outer_kernel, [VMEM] * 12 + [ANY], [((2, NL, NX, 512), f32), ((4, NX...  3.57 us
    ppermute x3, starting transfers between devices, shifted(): lax.ppermute(value, axis, [(i, (i + step) % count) for i in range(count)])  3.47 us
    ppermute x3, waiting for transfers between devices, shifted(): lax.ppermute(value, axis, [(i, (i + step) % count) for i in range(count)])  2.4 us
    pallas_call x1, Pallas kernels, on_device(): call(pack_y_kernel, [HBM] * 7, [((YROWS, LANES), bf16), ((YROWS, LANES),...  2.11 us
  transfers between devices with their start and end apart: 11, of which 3 were waited for; matrix products, arithmetic and copies ran while one was open for 0% of the time, Pallas kernels for 31%

profile of v5, /device:TPU:8, one launch (start us, length us, event | category | flops | bytes accessed | tf_op | source)
XLA Modules:
  0.0 39.5 jit_solution(10869573667160346112)
XLA Ops:
  0.6 0.0 slice-start
  0.6 0.0 copy-start
  0.7 0.0 copy-start.1
  0.7 0.0 slice-start.1
  0.7 2.1 %pack_y.1 = (bf16[496,128]{1,0:T(8,128)(2,1)S(1)}, bf16[496,128]{1,0:T(8,128)(2,1)S(1)}, bf16[4,4,32,128]{3,2,1,0:T(8,128)(2,1)S(1)}, f32[16,128]{1,0:T(8,128)S(1)}) custom-call(f32[5,128,128]{2,1,0:T(8,128)} %bitcast.8, s32[4,2,32]{2,1,0:T(2,128)} %bitcast.9, s32[4,1,32]{2,1,0:T(1,128)} %bitcast.10, s32[4,32]{1,0:T(4,128)} %bitcast.11, ...), custom_call_target="tpu_custom_call" | custom-call | bytes 6000000 | tf_op jit(solution)/shard_map/pack_y/pallas_call | solution.py:770
  2.8 5.8 %collective-permute-start = (bf16[496,128]{1,0:T(8,128)(2,1)S(1)}, bf16[496,128]{1,0:T(8,128)(2,1)S(1)}, u32[]{:S(2)}, u32[]{:S(2)}) collective-permute-start(bf16[496,128]{1,0:T(8,128)(2,1)S(1)} %get-tuple-element.36), channel_id=1, source_target_pairs={{0,7},{1,2},{2,1},{3,4},{4,3},{5,6},{6,5},{7,0},{8,15},{9,10},{10,... | collective-permute-start | bytes 380936 | tf_op jit(solution)/shard_map/ppermute | solution.py:760
  8.6 0.0 collective-permute-start.1
  8.6 0.0 copy-done
  8.6 0.0 copy-done.1
  8.6 0.3 pack_z.1
  9.0 2.8 %collective-permute-start.4 = (bf16[10,32,512]{2,1,0:T(8,128)(2,1)S(1)}, bf16[10,32,512]{2,1,0:T(8,128)(2,1)S(1)}, u32[]{:S(2)}, u32[]{:S(2)}) collective-permute-start(bf16[10,32,512]{2,1,0:T(8,128)(2,1)S(1)} %get-tuple-element.48), channel_id=1, source_target_pairs={{0,192},{64,0},{128,64},{192,128},{1,193},{65,1},{129,65},{193,129... | collective-permute-start | bytes 983048 | tf_op jit(solution)/shard_map/ppermute | solution.py:753
  11.8 0.0 collective-permute-start.5
  11.8 0.6 %collective-permute-done.yb_r = bf16[496,128]{1,0:T(8,128)(2,1)S(1)} collective-permute-done((bf16[496,128]{1,0:T(8,128)(2,1)S(1)}, bf16[496,128]{1,0:T(8,128)(2,1)S(1)}, u32[]{:S(2)}, u32[]{:S(2)}) %collective-permute-start) | collective-permute-done | bytes 127008 | tf_op jit(solution)/shard_map/ppermute | solution.py:760
  12.5 0.0 collective-permute-done.1.ya_r
  12.5 0.4 pack_x.1
  12.8 0.5 %collective-permute-start.3 = (bf16[496,128]{1,0:T(8,128)(2,1)S(1)}, bf16[496,128]{1,0:T(8,128)(2,1)S(1)}, u32[]{:S(2)}, u32[]{:S(2)}) collective-permute-start(bf16[496,128]{1,0:T(8,128)(2,1)S(1)} %get-tuple-element.41.after_x), channel_id=1, source_target_pairs={{0,8},{8,0},{16,24},{24,16},{32,40},{40,32},{48,56},{56,48},{1,9},... | collective-permute-start | bytes 380936 | tf_op jit(solution)/shard_map/ppermute | solution.py:761
  13.4 2.4 %collective-permute-start.2 = (bf16[496,128]{1,0:T(8,128)(2,1)S(1)}, bf16[496,128]{1,0:T(8,128)(2,1)S(1)}, u32[]{:S(2)}, u32[]{:S(2)}) collective-permute-start(bf16[496,128]{1,0:T(8,128)(2,1)S(1)} %get-tuple-element.44), channel_id=1, source_target_pairs={{0,56},{8,16},{16,8},{24,32},{32,24},{40,48},{48,40},{56,0},{1,57}... | collective-permute-start | bytes 380936 | tf_op jit(solution)/shard_map/ppermute | solution.py:760
  15.8 0.0 slice-done
  15.8 0.0 slice-done.1
  15.8 3.8 %remap.1 = (f32[640,128]{1,0:T(8,128)S(1)}, bf16[2,4,2,128,128]{4,3,2,1,0:T(8,128)(2,1)S(1)}) custom-call(bf16[4,4,32,128]{3,2,1,0:T(8,128)(2,1)S(1)} %get-tuple-element.35.flux, bf16[496,128]{1,0:T(8,128)(2,1)S(1)} %get-tuple-element.39.yn_r, bf16[496,128]{1,0:T(8,128)(2,1)S(1)} %get-tuple-element.40.ys_r, f32[16,128]{1,0:T(8,128)S(1)} %get-tuple-element.38.table.after, ...), custom_call_target="tpu_custom_call" | custom-call | bytes 18000000 | tf_op jit(solution)/shard_map/remap/pallas_call | solution.py:814
  19.6 0.0 collective-permute-done.3.xa_r
  19.6 0.0 collective-permute-done.2.xb_r
  19.6 0.4 %rim.1 = (f32[640,128]{1,0:T(8,128)S(1)}, bf16[640,128]{1,0:T(8,128)(2,1)S(1)}, bf16[640,128]{1,0:T(8,128)(2,1)S(1)}, bf16[528,128]{1,0:T(8,128)(2,1)S(1)}, bf16...) custom-call(f32[640,128]{1,0:T(8,128)S(1)} %get-tuple-element.42.first_part, ...), custom_call_target="tpu_custom_call" | custom-call | bytes 4000000 | tf_op jit(solution)/shard_map/rim/pallas_call | solution.py:825
  20.1 1.6 %collective-permute-start.6 = (bf16[640,128]{1,0:T(8,128)(2,1)S(1)}, bf16[640,128]{1,0:T(8,128)(2,1)S(1)}, u32[]{:S(2)}, u32[]{:S(2)}) collective-permute-start(bf16[640,128]{1,0:T(8,128)(2,1)S(1)} %get-tuple-element.55), channel_id=1, source_target_pairs={{0,64},{64,0},{128,192},{192,128},{1,65},{65,1},{129,193},{193,129... | collective-permute-start | bytes 491528 | tf_op jit(solution)/shard_map/ppermute | solution.py:761
  21.6 2.1 %collective-permute-start.7 = (bf16[640,128]{1,0:T(8,128)(2,1)S(1)}, bf16[640,128]{1,0:T(8,128)(2,1)S(1)}, u32[]{:S(2)}, u32[]{:S(2)}) collective-permute-start(bf16[640,128]{1,0:T(8,128)(2,1)S(1)} %get-tuple-element.56), channel_id=1, source_target_pairs={{0,192},{64,128},{128,64},{192,0},{1,193},{65,129},{129,65},{193,1... | collective-permute-start | bytes 491528 | tf_op jit(solution)/shard_map/ppermute | solution.py:760
  23.7 0.6 %collective-permute-start.8 = (bf16[528,128]{1,0:T(8,128)(2,1)S(1)}, bf16[528,128]{1,0:T(8,128)(2,1)S(1)}, u32[]{:S(2)}, u32[]{:S(2)}) collective-permute-start(bf16[528,128]{1,0:T(8,128)(2,1)S(1)} %get-tuple-element.47.after), channel_id=1, source_target_pairs={{0,128},{64,192},{128,0},{192,64},{1,129},{65,193},{129,1},{193,65... | collective-permute-start | bytes 405512 | tf_op jit(solution)/shard_map/ppermute | solution.py:753
  24.4 0.0 collective-permute-done.4.after_zu.zu_r
  24.4 0.0 collective-permute-done.5.after_zd.zd_r
  24.4 3.9 %middle.1 = (f32[2,10,5,56,128]{4,3,2,1,0:T(8,128)S(1)}, f32[2,10,5,56,128]{4,3,2,1,0:T(8,128)S(1)}, f32[2,8,5,56,128]{4,3,2,1,0:T(8,128)S(1)}, f32[2,6,5,56,128...) custom-call(f32[2,10,32,512]{3,2,1,0:T(8,128)S(1)} %copy-done, ...), custom_call_target="tpu_custom_call" | custom-call | bytes 20000000 | tf_op jit(solution)/shard_map/middle/pallas_call | solution.py:838
  28.3 2.4 %collective-permute-done.8.across_r = bf16[528,128]{1,0:T(8,128)(2,1)S(1)} collective-permute-done((bf16[528,128]{1,0:T(8,128)(2,1)S(1)}, bf16[528,128]{1,0:T(8,128)(2,1)S(1)}, u32[]{:S(2)}, u32[]{:S(2)}) %collective-permute-start.8) | collective-permute-done | bytes 135200 | tf_op jit(solution)/shard_map/ppermute | solution.py:753
  30.7 0.0 collective-permute-done.6.ua_r
  30.7 0.2 collective-permute-done.7.ub_r
  30.9 0.1 flux_sum.1
  31.0 2.0 %collective-permute-start.10 = (bf16[80,128]{1,0:T(8,128)(2,1)S(1)}, bf16[80,128]{1,0:T(8,128)(2,1)S(1)}, u32[]{:S(2)}, u32[]{:S(2)}) collective-permute-start(bf16[80,128]{1,0:T(8,128)(2,1)S(1)} %get-tuple-element.60.after), channel_id=1, source_target_pairs={{0,8},{8,0},{16,24},{24,16},{32,40},{40,32},{48,56},{56,48},{1,9},... | collective-permute-start | bytes 61448 | tf_op jit(solution)/shard_map/ppermute | solution.py:761
  33.0 1.4 %collective-permute-start.9 = (bf16[80,128]{1,0:T(8,128)(2,1)S(1)}, bf16[80,128]{1,0:T(8,128)(2,1)S(1)}, u32[]{:S(2)}, u32[]{:S(2)}) collective-permute-start(bf16[80,128]{1,0:T(8,128)(2,1)S(1)} %get-tuple-element.66), channel_id=1, source_target_pairs={{0,56},{8,16},{16,8},{24,32},{32,24},{40,48},{48,40},{56,0},{1,57}... | collective-permute-start | bytes 61448 | tf_op jit(solution)/shard_map/ppermute | solution.py:760
  34.4 3.6 %outer.1 = (f32[2,10,32,512]{3,2,1,0:T(8,128)}, f32[4,32,512]{2,1,0:T(8,128)}, f32[2,3,5,56,128]{4,3,2,1,0:T(8,128)S(1)}, f32[2,2,5,56,128]{4,3,2,1,0:T(8,128)S(...) custom-call(f32[2,10,32,512]{3,2,1,0:T(8,128)S(1)} %copy-done, ...), custom_call_target="tpu_custom_call" | custom-call | bytes 18000000 | tf_op jit(solution)/shard_map/outer/pallas_call | solution.py:866
  38.0 0.0 collective-permute-done.10.da_r
  38.0 0.0 collective-permute-done.9.db_r
  38.0 1.3 %surface.1 = f32[2,10,32,512]{3,2,1,0:T(8,128)} custom-call(f32[2,10,32,512]{3,2,1,0:T(8,128)} %get-tuple-element.61.unfinished, f32[2,10,32,512]{3,2,1,0:T(8,128)S(1)} %copy-done, f32[2,3,5,56,128]{4,3,2,1,0:T(8,128)S(1)} %get-tuple-element.62.s0, f32[2,2,5,56,128]{4,3,2,1,0:T(8,128)S(1)} %get-tuple-element.63.sv, ...), custom_call_target="tpu_custom_call", output_to_operand_aliasing={{}: (0, {})} | custom-call | bytes 8000000 | tf_op jit(solution)/shard_map/surface/pallas_call | solution.py:878
  (1 shorter events, 0.0 us)
Async XLA Ops:
  0.6 15.2 %slice-start = ((s8[8388608]{0:T(1024)(128)(4,1)}), s8[4194304]{0:T(1024)(128)(4,1)S(1)}, s32[]{:S(2)}) async-start(s8[8388608]{0:T(1024)(128)(4,1)} %bitcast.6), calls=%async_computation | async-start | bytes 8388608
  0.6 8.0 %copy-start = (f32[2,10,32,512]{3,2,1,0:T(8,128)S(1)}, f32[2,10,32,512]{3,2,1,0:T(8,128)}, u32[]{:S(2)}) copy-start(f32[2,10,32,512]{3,2,1,0:T(8,128)} %tr.11) | copy-start | bytes 3932164
  0.7 8.0 %copy-start.1 = (f32[2,10,32,512]{3,2,1,0:T(8,128)S(1)}, f32[2,10,32,512]{3,2,1,0:T(8,128)}, u32[]{:S(2)}) copy-start(f32[2,10,32,512]{3,2,1,0:T(8,128)} %cu.7) | copy-start | bytes 3932164
  0.7 15.1 %slice-start.1 = ((s8[8388608]{0:T(1024)(128)(4,1)}), s8[4194304]{0:T(1024)(128)(4,1)S(1)}, s32[]{:S(2)}) async-start(s8[8388608]{0:T(1024)(128)(4,1)} %bitcast.6), calls=%async_computation.1 | async-start | bytes 8388608
  2.8 9.7 %collective-permute-start = (bf16[496,128]{1,0:T(8,128)(2,1)S(1)}, bf16[496,128]{1,0:T(8,128)(2,1)S(1)}, u32[]{:S(2)}, u32[]{:S(2)}) collective-permute-start(bf16[496,128]{1,0:T(8,128)(2,1)S(1)} %get-tuple-element.36), channel_id=1, source_target_pairs={{0,7},{1,2},{2,1},{3,4},{4,3},{5,6},{6,5},{7,0},{8,15},{9,10},{10,... | collective-permute-start | bytes 380936 | tf_op jit(solution)/shard_map/ppermute | solution.py:760
  8.6 3.8 %collective-permute-start.1 = (bf16[496,128]{1,0:T(8,128)(2,1)S(1)}, bf16[496,128]{1,0:T(8,128)(2,1)S(1)}, u32[]{:S(2)}, u32[]{:S(2)}) collective-permute-start(bf16[496,128]{1,0:T(8,128)(2,1)S(1)} %get-tuple-element.37), channel_id=1, source_target_pairs={{0,1},{1,0},{2,3},{3,2},{4,5},{5,4},{6,7},{7,6},{8,9},{9,8},{10,11... | collective-permute-start | bytes 380936 | tf_op jit(solution)/shard_map/ppermute | solution.py:761
  9.0 15.4 %collective-permute-start.4 = (bf16[10,32,512]{2,1,0:T(8,128)(2,1)S(1)}, bf16[10,32,512]{2,1,0:T(8,128)(2,1)S(1)}, u32[]{:S(2)}, u32[]{:S(2)}) collective-permute-start(bf16[10,32,512]{2,1,0:T(8,128)(2,1)S(1)} %get-tuple-element.48), channel_id=1, source_target_pairs={{0,192},{64,0},{128,64},{192,128},{1,193},{65,1},{129,65},{193,129... | collective-permute-start | bytes 983048 | tf_op jit(solution)/shard_map/ppermute | solution.py:753
  11.8 12.5 %collective-permute-start.5 = (bf16[10,32,512]{2,1,0:T(8,128)(2,1)S(1)}, bf16[10,32,512]{2,1,0:T(8,128)(2,1)S(1)}, u32[]{:S(2)}, u32[]{:S(2)}) collective-permute-start(bf16[10,32,512]{2,1,0:T(8,128)(2,1)S(1)} %get-tuple-element.49), channel_id=1, source_target_pairs={{0,64},{64,128},{128,192},{192,0},{1,65},{65,129},{129,193},{193,1... | collective-permute-start | bytes 983048 | tf_op jit(solution)/shard_map/ppermute | solution.py:753
  12.8 6.7 %collective-permute-start.3 = (bf16[496,128]{1,0:T(8,128)(2,1)S(1)}, bf16[496,128]{1,0:T(8,128)(2,1)S(1)}, u32[]{:S(2)}, u32[]{:S(2)}) collective-permute-start(bf16[496,128]{1,0:T(8,128)(2,1)S(1)} %get-tuple-element.41.after_x), channel_id=1, source_target_pairs={{0,8},{8,0},{16,24},{24,16},{32,40},{40,32},{48,56},{56,48},{1,9},... | collective-permute-start | bytes 380936 | tf_op jit(solution)/shard_map/ppermute | solution.py:761
  13.4 6.2 %collective-permute-start.2 = (bf16[496,128]{1,0:T(8,128)(2,1)S(1)}, bf16[496,128]{1,0:T(8,128)(2,1)S(1)}, u32[]{:S(2)}, u32[]{:S(2)}) collective-permute-start(bf16[496,128]{1,0:T(8,128)(2,1)S(1)} %get-tuple-element.44), channel_id=1, source_target_pairs={{0,56},{8,16},{16,8},{24,32},{32,24},{40,48},{48,40},{56,0},{1,57}... | collective-permute-start | bytes 380936 | tf_op jit(solution)/shard_map/ppermute | solution.py:760
  20.1 10.6 %collective-permute-start.6 = (bf16[640,128]{1,0:T(8,128)(2,1)S(1)}, bf16[640,128]{1,0:T(8,128)(2,1)S(1)}, u32[]{:S(2)}, u32[]{:S(2)}) collective-permute-start(bf16[640,128]{1,0:T(8,128)(2,1)S(1)} %get-tuple-element.55), channel_id=1, source_target_pairs={{0,64},{64,0},{128,192},{192,128},{1,65},{65,1},{129,193},{193,129... | collective-permute-start | bytes 491528 | tf_op jit(solution)/shard_map/ppermute | solution.py:761
  21.6 9.3 %collective-permute-start.7 = (bf16[640,128]{1,0:T(8,128)(2,1)S(1)}, bf16[640,128]{1,0:T(8,128)(2,1)S(1)}, u32[]{:S(2)}, u32[]{:S(2)}) collective-permute-start(bf16[640,128]{1,0:T(8,128)(2,1)S(1)} %get-tuple-element.56), channel_id=1, source_target_pairs={{0,192},{64,128},{128,64},{192,0},{1,193},{65,129},{129,65},{193,1... | collective-permute-start | bytes 491528 | tf_op jit(solution)/shard_map/ppermute | solution.py:760
  23.7 6.9 %collective-permute-start.8 = (bf16[528,128]{1,0:T(8,128)(2,1)S(1)}, bf16[528,128]{1,0:T(8,128)(2,1)S(1)}, u32[]{:S(2)}, u32[]{:S(2)}) collective-permute-start(bf16[528,128]{1,0:T(8,128)(2,1)S(1)} %get-tuple-element.47.after), channel_id=1, source_target_pairs={{0,128},{64,192},{128,0},{192,64},{1,129},{65,193},{129,1},{193,65... | collective-permute-start | bytes 405512 | tf_op jit(solution)/shard_map/ppermute | solution.py:753
  31.0 7.0 %collective-permute-start.10 = (bf16[80,128]{1,0:T(8,128)(2,1)S(1)}, bf16[80,128]{1,0:T(8,128)(2,1)S(1)}, u32[]{:S(2)}, u32[]{:S(2)}) collective-permute-start(bf16[80,128]{1,0:T(8,128)(2,1)S(1)} %get-tuple-element.60.after), channel_id=1, source_target_pairs={{0,8},{8,0},{16,24},{24,16},{32,40},{40,32},{48,56},{56,48},{1,9},... | collective-permute-start | bytes 61448 | tf_op jit(solution)/shard_map/ppermute | solution.py:761
  33.0 5.0 %collective-permute-start.9 = (bf16[80,128]{1,0:T(8,128)(2,1)S(1)}, bf16[80,128]{1,0:T(8,128)(2,1)S(1)}, u32[]{:S(2)}, u32[]{:S(2)}) collective-permute-start(bf16[80,128]{1,0:T(8,128)(2,1)S(1)} %get-tuple-element.66), channel_id=1, source_target_pairs={{0,56},{8,16},{16,8},{24,32},{32,24},{40,48},{48,40},{56,0},{1,57}... | collective-permute-start | bytes 61448 | tf_op jit(solution)/shard_map/ppermute | solution.py:760
